TPU v7x, 32 devices: a whole 2x2x4 slice. The times are simulated.
32 devices in a mesh: seq: 16 (over z, x, core), chan: 2 (over y).
Axes of the slice: x: 2, y: 2, z: 4, core: 2. Of those that a mesh axis runs over, the one named last changes fastest.
Arguments:
- tokens: int32 [2048], P('seq'), may hold values from 0 to 3
- stem_weight: bfloat16 [5, 4, 768], replicated, may hold values from -2.5 to 2.5
- conv_weight: bfloat16 [5, 768, 768], P(None, None, 'chan'), may hold values from -0.09375 to 0.09375
- cotangent: bfloat16 [2048, 768], P('seq', 'chan'), may hold values from -6 to 6
Outputs:
- blended: bfloat16 [2048, 768], P('seq', 'chan')
- grad_conv: float32 [5, 768, 768], P(None, 'seq', 'chan')
- grad_stem: float32 [5, 4, 768], P(None, None, 'chan')
All inputs are finite; a program needn't handle non-finite values.
Results may differ from a plain program's by a relative error of at most 0.012.
Values may be sent and summed in bfloat16 or wider, within the bound.
No kernel may reach another device: no remote copies, remote signals or barrier semaphores. Data moves between devices by JAX's collectives and lax.ppermute only.
A program may use at most 128 MiB of HBM per device.

v0:
```python
import math

import jax
import jax.numpy as jnp
from jax import lax
from jax.sharding import PartitionSpec as P


def from_partner(value, axis, distance):
    mask = 2**distance
    pairs = [(source, source ^ mask) for source in range(lax.axis_size(axis))]
    return lax.ppermute(value, axis, pairs)


def padded(block, sides, width):
    for axis, dim in sides:
        count = lax.axis_size(axis)
        forward = [(i, i + 1) for i in range(count - 1)]
        backward = [(target, source) for source, target in forward]
        low = lax.ppermute(
            lax.slice_in_dim(block, block.shape[dim] - width, None, axis=dim), axis, forward
        )
        high = lax.ppermute(lax.slice_in_dim(block, 0, width, axis=dim), axis, backward)
        block = jnp.concatenate([low, block, high], axis=dim)
    return block


def gelu_parts(values_in):
    coeff = math.sqrt(2.0 / math.pi)
    tanh_val = jnp.tanh(coeff * (values_in + 0.044715 * values_in**3))
    result = 0.5 * values_in * (1.0 + tanh_val)
    slopes = 0.5 * (1.0 + tanh_val) + 0.5 * values_in * (1.0 - tanh_val**2) * coeff * (
        1.0 + 3.0 * 0.044715 * values_in**2
    )
    return (result, slopes)


def on_device(tokens, stem_weight, conv_weight, cotangent):
    positions = tokens.shape[0]
    full_width = conv_weight.shape[1]
    half_width = conv_weight.shape[2]
    taps = conv_weight.shape[0]
    shards = lax.axis_size("seq")
    chan_start = lax.axis_index("chan") * half_width
    dir_grad = cotangent * 0.5
    moved_bases = tokens.astype(jnp.bfloat16)
    moved_cot = cotangent
    for bit_pos in range(shards.bit_length() - 1):
        moved_bases, moved_cot = from_partner((moved_bases, moved_cot), "seq", bit_pos)
    rc_ids = 4 - jnp.flip(moved_bases, 0).astype(jnp.int32)
    rc_grad = jnp.flip(moved_cot, 0) * 0.5
    stem_pair = jnp.stack([stem_weight, stem_weight])
    conv_pair = jnp.stack([conv_weight, conv_weight])
    letter_ids = jnp.stack([tokens + 1, rc_ids])
    wide_ids = padded(letter_ids, (("seq", 1),), 4)
    one_hot = (wide_ids[:, :, None] == jnp.arange(1, 5, dtype=jnp.int32)[None, None, :]).astype(
        jnp.bfloat16
    )
    span = positions + 4
    stem_sum = jnp.zeros((2, span, full_width), jnp.float32)
    for k in range(taps):
        stem_sum = stem_sum + jnp.einsum(
            "spv,svc->spc",
            one_hot[:, k : k + span],
            stem_pair[:, k],
            preferred_element_type=jnp.float32,
        )
    stem_act = stem_sum.astype(jnp.bfloat16)
    place = lax.axis_index("seq") * positions - 2 + jnp.arange(span, dtype=jnp.int32)
    inside = (place >= 0) & (place < positions * shards)
    gelu_val, gelu_slope = gelu_parts(stem_act.astype(jnp.float32))
    act = jnp.where(inside[None, :, None], gelu_val, 0.0).astype(jnp.bfloat16)
    conv_sum = jnp.zeros((2, positions, half_width), jnp.float32)
    for k in range(taps):
        conv_sum = conv_sum + jnp.einsum(
            "spc,scd->spd",
            act[:, k : k + positions],
            conv_pair[:, k],
            preferred_element_type=jnp.float32,
        )
    own_stem = lax.dynamic_slice_in_dim(
        stem_act[:, 2 : positions + 2], chan_start, half_width, 2
    ).astype(jnp.float32)
    layer_out = own_stem + conv_sum
    moved_out = layer_out[1]
    for bit_pos in range(shards.bit_length() - 1):
        moved_out = from_partner(moved_out, "seq", bit_pos)
    rc_out = jnp.flip(moved_out, 0)
    blended = (0.5 * (layer_out[0] + rc_out)).astype(jnp.bfloat16)
    out_grad = jnp.stack([dir_grad, rc_grad])
    wide_grad = padded(out_grad, (("seq", 1),), 2)
    kernel_list = []
    for k in range(taps):
        kernel_list.append(
            jnp.einsum(
                "spc,spd->scd",
                act[:, k : k + positions],
                out_grad,
                preferred_element_type=jnp.float32,
            )
        )
    kernel_grad = jnp.stack(kernel_list, axis=1)
    slope_rows = gelu_slope[:, 2 : positions + 2]
    own_hot = [one_hot[:, k + 2 : k + 2 + positions].astype(jnp.float32) for k in range(taps)]
    data_part = jnp.zeros((2, positions, full_width), jnp.float32)
    for k in range(taps):
        data_part = data_part + jnp.einsum(
            "spd,scd->spc",
            wide_grad[:, 4 - k : 4 - k + positions],
            conv_pair[:, k],
            preferred_element_type=jnp.float32,
        )
    data_full = lax.psum(data_part, "chan")
    stem_in = data_full * slope_rows
    stem_list = []
    for k in range(taps):
        stem_list.append(
            jnp.einsum("spv,spc->svc", own_hot[k], stem_in, precision=lax.Precision.HIGHEST)
        )
    stem_grad = lax.dynamic_slice_in_dim(jnp.stack(stem_list, axis=1), chan_start, half_width, 3)
    grad_conv = jnp.sum(
        lax.psum_scatter(kernel_grad, "seq", scatter_dimension=2, tiled=True), axis=0
    )
    grad_stem = lax.psum(stem_grad[0] + stem_grad[1], "seq")
    return (blended, grad_conv, grad_stem)


def solution(mesh):
    return jax.shard_map(
        on_device,
        mesh=mesh,
        in_specs=(P("seq"), P(), P(None, None, "chan"), P("seq", "chan")),
        out_specs=(P("seq", "chan"), P(None, "seq", "chan"), P(None, None, "chan")),
        check_vma=False,
    )
```

profile of v0, /device:TPU:0, one launch (start us, length us, event | category | flops | bytes accessed | tf_op | source)
XLA Modules:
  0.0 213.9 jit_solution(6710911784890804444)
XLA Ops:
  8.0 0.7 add_bitcast_fusion
  9.3 0.9 multiply_bitcast_fusion.1
  10.2 3.9 %fusion.11 = (bf16[2,768,384]{2,1,0:T(8,128)(2,1)}, bf16[2,768,384]{2,1,0:T(8,128)(2,1)}, bf16[2,768,384]{2,1,0:T(8,128)(2,1)}) fusion(bf16[1,5,768,384]{3,2,0,1:T(8,128)(2,1)} %bitcast.94), kind=kLoop, calls=%fused_computation.38 | loop fusion | flops 1769472 | bytes 6488064 | tf_op jit(solution)/shard_map/squeeze | solution.py:78
  14.2 3.0 %collective-permute-start.1 = (bf16[128]{0:T(256)(128)(2,1)S(1)}, bf16[128]{0:T(256)(128)(2,1)S(1)}, u32[]{:S(2)}, u32[]{:S(2)}) collective-permute-start(bf16[128]{0:T(256)(128)(2,1)S(1)} %collective-permute-done), channel_id=1, source_target_pairs={{0,4},{2,6},{4,0},{6,2},{8,12},{10,14},{12,8},{14,10},{16,20},{18,... | collective-permute-start | bytes 776 | tf_op jit(solution)/shard_map/ppermute | solution.py:12
  17.2 1.5 collective-permute-done.1
  18.7 2.1 collective-permute-start.2
  20.8 1.5 collective-permute-done.2
  22.3 3.0 %collective-permute-start.3 = (bf16[128]{0:T(256)(128)(2,1)S(1)}, bf16[128]{0:T(256)(128)(2,1)S(1)}, u32[]{:S(2)}, u32[]{:S(2)}) collective-permute-start(bf16[128]{0:T(256)(128)(2,1)S(1)} %collective-permute-done.2), channel_id=1, source_target_pairs={{0,16},{2,18},{4,20},{6,22},{8,24},{10,26},{12,28},{14,30},{16,0},... | collective-permute-start | bytes 776 | tf_op jit(solution)/shard_map/ppermute | solution.py:12
  25.3 1.5 collective-permute-done.3
  27.1 1.3 collective-permute-start.4
  28.3 1.3 collective-permute-start.5
  29.6 3.8 %collective-permute-done.5 = s32[2,4]{1,0:T(2,128)S(1)} collective-permute-done((s32[2,4]{1,0:T(2,128)S(1)}, s32[2,4]{1,0:T(2,128)S(1)}, u32[]{:S(2)}, u32[]{:S(2)}) %collective-permute-start.5) | collective-permute-done | bytes 64 | tf_op jit(solution)/shard_map/ppermute | solution.py:23
  34.3 2.4 %collective-permute-start.11 = (bf16[128,384]{1,0:T(8,128)(2,1)S(1)}, bf16[128,384]{1,0:T(8,128)(2,1)S(1)}, u32[]{:S(2)}, u32[]{:S(2)}) collective-permute-start(bf16[128,384]{1,0:T(8,128)(2,1)S(1)} %collective-permute-done.10), channel_id=1, source_target_pairs={{0,4},{2,6},{4,0},{6,2},{8,12},{10,14},{12,8},{14,10},{16,20},{18,... | collective-permute-start | bytes 294920 | tf_op jit(solution)/shard_map/ppermute | solution.py:12
  37.1 2.2 %collective-permute-done.11 = bf16[128,384]{1,0:T(8,128)(2,1)S(1)} collective-permute-done((bf16[128,384]{1,0:T(8,128)(2,1)S(1)}, bf16[128,384]{1,0:T(8,128)(2,1)S(1)}, u32[]{:S(2)}, u32[]{:S(2)}) %collective-permute-start.11) | collective-permute-done | bytes 98336 | tf_op jit(solution)/shard_map/ppermute | solution.py:12
  39.3 3.8 %collective-permute-start.12 = (bf16[128,384]{1,0:T(8,128)(2,1)S(1)}, bf16[128,384]{1,0:T(8,128)(2,1)S(1)}, u32[]{:S(2)}, u32[]{:S(2)}) collective-permute-start(bf16[128,384]{1,0:T(8,128)(2,1)S(1)} %collective-permute-done.11), channel_id=1, source_target_pairs={{0,8},{2,10},{4,12},{6,14},{8,0},{10,2},{12,4},{14,6},{16,24},{18,... | collective-permute-start | bytes 294920 | tf_op jit(solution)/shard_map/ppermute | solution.py:12
  43.4 2.7 %collective-permute-done.12 = bf16[128,384]{1,0:T(8,128)(2,1)S(1)} collective-permute-done((bf16[128,384]{1,0:T(8,128)(2,1)S(1)}, bf16[128,384]{1,0:T(8,128)(2,1)S(1)}, u32[]{:S(2)}, u32[]{:S(2)}) %collective-permute-start.12) | collective-permute-done | bytes 98336 | tf_op jit(solution)/shard_map/ppermute | solution.py:12
  46.1 2.8 %collective-permute-start.13 = (bf16[128,384]{1,0:T(8,128)(2,1)S(1)}, bf16[128,384]{1,0:T(8,128)(2,1)S(1)}, u32[]{:S(2)}, u32[]{:S(2)}) collective-permute-start(bf16[128,384]{1,0:T(8,128)(2,1)S(1)} %collective-permute-done.12), channel_id=1, source_target_pairs={{0,16},{2,18},{4,20},{6,22},{8,24},{10,26},{12,28},{14,30},{16,0},... | collective-permute-start | bytes 294920 | tf_op jit(solution)/shard_map/ppermute | solution.py:12
  48.9 2.4 %fusion.20 = (f32[2,132,768]{2,1,0:T(8,128)}, f32[2,132,768]{2,1,0:T(8,128)}, bf16[2,132,768]{2,1,0:T(8,128)(2,1)S(1)}, f32[2,132,768]{2,1,0:T(8,128)}, f32[2,132,768]{2,1,0:T(8,128)}, /*index=5*/bf16[2,132,768]{2,1,0:T(8,128)(2,1)}) fusion(pred[132]{0:T(512)(128)(4,1)S(1)} %compare_and_fusion, f32[2,132,768]{2,1,0:T(8,128)S(1)} %convolution_add_fusion.1, ...), kind=kOutput, calls=%fused_computation.53 | convolution fusion | flops 4282368 | bytes 4897988 | tf_op jit(solution)/shard_map/spv,svc->spc/dot_general | solution.py:62
  51.3 2.1 collective-permute-done.13
  53.6 1.3 collective-permute-start.14
  54.9 3.0 %collective-permute-start.15 = (bf16[2,2,384]{2,1,0:T(2,128)(2,1)S(1)}, bf16[2,2,384]{2,1,0:T(2,128)(2,1)S(1)}, u32[]{:S(2)}, u32[]{:S(2)}) collective-permute-start(bf16[2,2,384]{2,1,0:T(2,128)(2,1)S(1)} %get-tuple-element.14), channel_id=1, source_target_pairs={{0,2},{2,4},{4,6},{6,8},{8,10},{10,12},{12,14},{14,16},{16,18},{18... | collective-permute-start | bytes 9224 | tf_op jit(solution)/shard_map/ppermute | solution.py:20
  58.0 2.0 bitcast_dynamic-update-slice_fusion.4
  59.9 1.9 bitcast_dynamic-update-slice_fusion.3
  62.6 0.5 fusion.38
  63.1 0.7 copy-done.3
  63.9 0.5 fusion.41
  64.5 0.5 fusion.1
  65.0 1.4 fusion
  66.5 2.9 %bitcast_dynamic-update-slice_fusion.2 = f32[2,5,768,384]{3,2,0,1:T(8,128)} fusion(f32[2,5,768,384]{3,2,0,1:T(8,128)} %bitcast_dynamic-update-slice_fusion.3, bf16[2,132,768]{2,1,0:T(8,128)(2,1)S(1)} %get-tuple-element.8, bf16[1,128,384]{2,1,0:T(8,128)(2,1)} %copy-done.6, bf16[1,128,384]{2,1,0:T(8,128)(2,1)S(1)} %multiply_bitcast_fusion.1), kind=kOutput, calls=%fused_computation.10 | convolution fusion | flops 151093248 | bytes 2949120 | tf_op jit(solution)/shard_map/spc,spd->scd/dot_general | solution.py:95
  69.4 2.0 bitcast_dynamic-update-slice_fusion.1
  71.4 1.9 bitcast_dynamic-update-slice_fusion
  73.4 1.1 slice.183
  74.5 1.7 fusion.36
  76.6 0.9 copy-done.2
  78.7 0.7 copy-done.9
  79.4 0.8 collective-permute-start.6
  80.2 1.1 collective-permute-done.6
  81.2 1.8 collective-permute-start.7
  83.1 5.4 %collective-permute-done.7 = f32[128,384]{1,0:T(8,128)S(1)} collective-permute-done((f32[128,384]{1,0:T(8,128)S(1)}, f32[128,384]{1,0:T(8,128)S(1)}, u32[]{:S(2)}, u32[]{:S(2)}) %collective-permute-start.7) | collective-permute-done | bytes 196640 | tf_op jit(solution)/shard_map/ppermute | solution.py:12
  88.5 0.6 collective-permute-start.8
  89.1 5.8 %collective-permute-done.8 = f32[128,384]{1,0:T(8,128)S(1)} collective-permute-done((f32[128,384]{1,0:T(8,128)S(1)}, f32[128,384]{1,0:T(8,128)S(1)}, u32[]{:S(2)}, u32[]{:S(2)}) %collective-permute-start.8) | collective-permute-done | bytes 196640 | tf_op jit(solution)/shard_map/ppermute | solution.py:12
  94.9 2.1 collective-permute-start.9
  97.1 8.3 %collective-permute-done.9 = f32[128,384]{1,0:T(8,128)S(1)} collective-permute-done((f32[128,384]{1,0:T(8,128)S(1)}, f32[128,384]{1,0:T(8,128)S(1)}, u32[]{:S(2)}, u32[]{:S(2)}) %collective-permute-start.9) | collective-permute-done | bytes 196640 | tf_op jit(solution)/shard_map/ppermute | solution.py:12
  105.4 1.6 fusion.46
  107.0 3.0 %fusion.22 = f32[2,128,768]{2,1,0:T(8,128)S(1)} fusion(f32[2,128,768]{2,1,0:T(8,128)} %all-reduce.2.cloned.1.call-done, f32[2,132,768]{2,1,0:T(8,128)} %get-tuple-element.7, f32[2,132,768]{2,1,0:T(8,128)} %get-tuple-element.9, f32[2,132,768]{2,1,0:T(8,128)} %get-tuple-element.10, f32[2,132,768]{2,1,0:T(8,128)S(1)} %copy-done.8), kind=kLoop, calls=%fused_computation.57 | loop fusion | flops 1966080 | bytes 4718592 | tf_op jit(solution)/shard_map/mul | solution.py:114
  111.9 62.8 %psum.15 = f32[5,4,384]{2,1,0:T(4,128)} all-reduce(f32[5,4,384]{2,1,0:T(4,128)S(1)} %fusion.47), channel_id=1, replica_groups=mesh['seq'=16,'chan'=2] {'seq'}, use_global_device_ids=true, to_apply=%region_3.4 | all-reduce | flops 7680 | bytes 61440 | tf_op jit(solution)/shard_map/psum | solution.py:124
  174.7 29.8 %reduce-scatter.2.cloned.1.call-done = f32[2,5,48,384]{3,2,0,1:T(8,128)} async-done(((f32[2,5,768,384]{3,2,0,1:T(8,128)}), f32[2,5,48,384]{3,2,0,1:T(8,128)}) %reduce-scatter.2.cloned.1.call-update) | async-done | bytes 737296 | tf_op jit(solution)/shard_map/reduce_scatter | solution.py:122
  204.6 1.9 reduce_sum.9
  (60 shorter events, 7.0 us)
Async XLA Ops:
  8.0 99.0 %all-reduce.2.cloned.1.call-start = ((), (), s32[]{:S(2)}) async-start(), calls=%async_computation.2 | async-start | bytes 1572864 | tf_op jit(solution)/shard_map/psum | solution.py:113
  8.8 5.4 %collective-permute-start = (bf16[128]{0:T(256)(128)(2,1)S(1)}, bf16[128]{0:T(256)(128)(2,1)S(1)}, u32[]{:S(2)}, u32[]{:S(2)}) collective-permute-start(bf16[128]{0:T(256)(128)(2,1)S(1)} %get-tuple-element.18), channel_id=1, source_target_pairs={{0,2},{2,0},{4,6},{6,4},{8,10},{10,8},{12,14},{14,12},{16,18},{18,... | collective-permute-start | bytes 776 | tf_op jit(solution)/shard_map/ppermute | solution.py:12
  9.2 25.1 %collective-permute-start.10 = (bf16[128,384]{1,0:T(8,128)(2,1)}, bf16[128,384]{1,0:T(8,128)(2,1)S(1)}, u32[]{:S(2)}, u32[]{:S(2)}) collective-permute-start(bf16[128,384]{1,0:T(8,128)(2,1)} %param.7), channel_id=1, source_target_pairs={{0,2},{2,0},{4,6},{6,4},{8,10},{10,8},{12,14},{14,12},{16,18},{18,... | collective-permute-start | bytes 294920 | tf_op jit(solution)/shard_map/ppermute | solution.py:12
  10.2 23.4 %copy-start.10 = (bf16[5,4,768]{2,1,0:T(4,128)(2,1)S(1)}, bf16[5,4,768]{2,1,0:T(4,128)(2,1)}, u32[]{:S(2)}) copy-start(bf16[5,4,768]{2,1,0:T(4,128)(2,1)} %param.5) | copy-start | bytes 92164
  14.2 4.5 %collective-permute-start.1 = (bf16[128]{0:T(256)(128)(2,1)S(1)}, bf16[128]{0:T(256)(128)(2,1)S(1)}, u32[]{:S(2)}, u32[]{:S(2)}) collective-permute-start(bf16[128]{0:T(256)(128)(2,1)S(1)} %collective-permute-done), channel_id=1, source_target_pairs={{0,4},{2,6},{4,0},{6,2},{8,12},{10,14},{12,8},{14,10},{16,20},{18,... | collective-permute-start | bytes 776 | tf_op jit(solution)/shard_map/ppermute | solution.py:12
  18.7 3.6 %collective-permute-start.2 = (bf16[128]{0:T(256)(128)(2,1)S(1)}, bf16[128]{0:T(256)(128)(2,1)S(1)}, u32[]{:S(2)}, u32[]{:S(2)}) collective-permute-start(bf16[128]{0:T(256)(128)(2,1)S(1)} %collective-permute-done.1), channel_id=1, source_target_pairs={{0,8},{2,10},{4,12},{6,14},{8,0},{10,2},{12,4},{14,6},{16,24},{18,... | collective-permute-start | bytes 776 | tf_op jit(solution)/shard_map/ppermute | solution.py:12
  22.3 4.6 %collective-permute-start.3 = (bf16[128]{0:T(256)(128)(2,1)S(1)}, bf16[128]{0:T(256)(128)(2,1)S(1)}, u32[]{:S(2)}, u32[]{:S(2)}) collective-permute-start(bf16[128]{0:T(256)(128)(2,1)S(1)} %collective-permute-done.2), channel_id=1, source_target_pairs={{0,16},{2,18},{4,20},{6,22},{8,24},{10,26},{12,28},{14,30},{16,0},... | collective-permute-start | bytes 776 | tf_op jit(solution)/shard_map/ppermute | solution.py:12
  27.1 2.6 %collective-permute-start.4 = (s32[2,4]{1,0:T(2,128)S(1)}, s32[2,4]{1,0:T(2,128)S(1)}, u32[]{:S(2)}, u32[]{:S(2)}) collective-permute-start(s32[2,4]{1,0:T(2,128)S(1)} %get-tuple-element.15), channel_id=1, source_target_pairs={{0,2},{2,4},{4,6},{6,8},{8,10},{10,12},{12,14},{14,16},{16,18},{18... | collective-permute-start | bytes 104 | tf_op jit(solution)/shard_map/ppermute | solution.py:20
  28.3 5.1 %collective-permute-start.5 = (s32[2,4]{1,0:T(2,128)S(1)}, s32[2,4]{1,0:T(2,128)S(1)}, u32[]{:S(2)}, u32[]{:S(2)}) collective-permute-start(s32[2,4]{1,0:T(2,128)S(1)} %get-tuple-element.16), channel_id=1, source_target_pairs={{2,0},{4,2},{6,4},{8,6},{10,8},{12,10},{14,12},{16,14},{18,16},{20... | collective-permute-start | bytes 104 | tf_op jit(solution)/shard_map/ppermute | solution.py:23
  34.3 5.0 %collective-permute-start.11 = (bf16[128,384]{1,0:T(8,128)(2,1)S(1)}, bf16[128,384]{1,0:T(8,128)(2,1)S(1)}, u32[]{:S(2)}, u32[]{:S(2)}) collective-permute-start(bf16[128,384]{1,0:T(8,128)(2,1)S(1)} %collective-permute-done.10), channel_id=1, source_target_pairs={{0,4},{2,6},{4,0},{6,2},{8,12},{10,14},{12,8},{14,10},{16,20},{18,... | collective-permute-start | bytes 294920 | tf_op jit(solution)/shard_map/ppermute | solution.py:12
  39.3 6.8 %collective-permute-start.12 = (bf16[128,384]{1,0:T(8,128)(2,1)S(1)}, bf16[128,384]{1,0:T(8,128)(2,1)S(1)}, u32[]{:S(2)}, u32[]{:S(2)}) collective-permute-start(bf16[128,384]{1,0:T(8,128)(2,1)S(1)} %collective-permute-done.11), channel_id=1, source_target_pairs={{0,8},{2,10},{4,12},{6,14},{8,0},{10,2},{12,4},{14,6},{16,24},{18,... | collective-permute-start | bytes 294920 | tf_op jit(solution)/shard_map/ppermute | solution.py:12
  46.1 7.3 %collective-permute-start.13 = (bf16[128,384]{1,0:T(8,128)(2,1)S(1)}, bf16[128,384]{1,0:T(8,128)(2,1)S(1)}, u32[]{:S(2)}, u32[]{:S(2)}) collective-permute-start(bf16[128,384]{1,0:T(8,128)(2,1)S(1)} %collective-permute-done.12), channel_id=1, source_target_pairs={{0,16},{2,18},{4,20},{6,22},{8,24},{10,26},{12,28},{14,30},{16,0},... | collective-permute-start | bytes 294920 | tf_op jit(solution)/shard_map/ppermute | solution.py:12
  53.6 8.8 %copy-start.6 = (bf16[1,128,384]{2,1,0:T(8,128)(2,1)}, bf16[1,128,384]{2,1,0:T(8,128)(2,1)S(1)}, u32[]{:S(2)}) copy-start(bf16[1,128,384]{2,1,0:T(8,128)(2,1)S(1)} %multiply_bitcast_fusion) | copy-start | bytes 294916
  53.6 8.8 %collective-permute-start.14 = (bf16[2,2,384]{2,1,0:T(2,128)(2,1)S(1)}, bf16[2,2,384]{2,1,0:T(2,128)(2,1)S(1)}, u32[]{:S(2)}, u32[]{:S(2)}) collective-permute-start(bf16[2,2,384]{2,1,0:T(2,128)(2,1)S(1)} %get-tuple-element.13), channel_id=1, source_target_pairs={{2,0},{4,2},{6,4},{8,6},{10,8},{12,10},{14,12},{16,14},{18,16},{20... | collective-permute-start | bytes 9224 | tf_op jit(solution)/shard_map/ppermute | solution.py:23
  54.9 7.5 %collective-permute-start.15 = (bf16[2,2,384]{2,1,0:T(2,128)(2,1)S(1)}, bf16[2,2,384]{2,1,0:T(2,128)(2,1)S(1)}, u32[]{:S(2)}, u32[]{:S(2)}) collective-permute-start(bf16[2,2,384]{2,1,0:T(2,128)(2,1)S(1)} %get-tuple-element.14), channel_id=1, source_target_pairs={{0,2},{2,4},{4,6},{6,8},{8,10},{10,12},{12,14},{14,16},{16,18},{18... | collective-permute-start | bytes 9224 | tf_op jit(solution)/shard_map/ppermute | solution.py:20
  58.0 3.9 %copy-start.1 = (bf16[2,768,384]{2,1,0:T(8,128)(2,1)S(1)}, bf16[2,768,384]{2,1,0:T(8,128)(2,1)}, u32[]{:S(2)}) copy-start(bf16[2,768,384]{2,1,0:T(8,128)(2,1)} %get-tuple-element.3) | copy-start | bytes 3538948
  59.9 2.7 %copy-start = (bf16[5,768,384]{2,1,0:T(8,128)(2,1)S(1)}, bf16[5,768,384]{2,1,0:T(8,128)(2,1)}, u32[]{:S(2)}) copy-start(bf16[5,768,384]{2,1,0:T(8,128)(2,1)} %param.6) | copy-start | bytes 8847364
  62.6 1.3 copy-start.3
  63.1 1.4 copy-start.5
  66.5 138.1 %reduce-scatter.2.cloned.1.call-start = ((), (), s32[]{:S(2)}) async-start(), calls=%async_computation.1 | async-start | bytes 12533760 | tf_op jit(solution)/shard_map/reduce_scatter | solution.py:122
  66.5 2.9 %copy-start.7 = (bf16[1,128,384]{2,1,0:T(8,128)(2,1)S(1)}, bf16[1,128,384]{2,1,0:T(8,128)(2,1)}, u32[]{:S(2)}) copy-start(bf16[1,128,384]{2,1,0:T(8,128)(2,1)} %copy-done.6) | copy-start | bytes 294916
  74.5 1.7 copy-start.4
  76.3 1.3 copy-start.2
  78.7 0.8 copy-start.9
  79.4 27.6 %copy-start.8 = (f32[2,132,768]{2,1,0:T(8,128)S(1)}, f32[2,132,768]{2,1,0:T(8,128)}, u32[]{:S(2)}) copy-start(f32[2,132,768]{2,1,0:T(8,128)} %get-tuple-element.6) | copy-start | bytes 2433028
  79.4 1.8 collective-permute-start.6
  81.2 7.2 %collective-permute-start.7 = (f32[128,384]{1,0:T(8,128)S(1)}, f32[128,384]{1,0:T(8,128)S(1)}, u32[]{:S(2)}, u32[]{:S(2)}) collective-permute-start(f32[128,384]{1,0:T(8,128)S(1)} %collective-permute-done.6), channel_id=1, source_target_pairs={{0,4},{2,6},{4,0},{6,2},{8,12},{10,14},{12,8},{14,10},{16,20},{18,... | collective-permute-start | bytes 589832 | tf_op jit(solution)/shard_map/ppermute | solution.py:12
  88.5 6.4 %collective-permute-start.8 = (f32[128,384]{1,0:T(8,128)S(1)}, f32[128,384]{1,0:T(8,128)S(1)}, u32[]{:S(2)}, u32[]{:S(2)}) collective-permute-start(f32[128,384]{1,0:T(8,128)S(1)} %collective-permute-done.7), channel_id=1, source_target_pairs={{0,8},{2,10},{4,12},{6,14},{8,0},{10,2},{12,4},{14,6},{16,24},{18,... | collective-permute-start | bytes 589832 | tf_op jit(solution)/shard_map/ppermute | solution.py:12
  94.9 10.4 %collective-permute-start.9 = (f32[128,384]{1,0:T(8,128)S(1)}, f32[128,384]{1,0:T(8,128)S(1)}, u32[]{:S(2)}, u32[]{:S(2)}) collective-permute-start(f32[128,384]{1,0:T(8,128)S(1)} %collective-permute-done.8), channel_id=1, source_target_pairs={{0,16},{2,18},{4,20},{6,22},{8,24},{10,26},{12,28},{14,30},{16,0},... | collective-permute-start | bytes 589832 | tf_op jit(solution)/shard_map/ppermute | solution.py:12
Sparse Core Ops, SparseCore 0:
  66.6 34.5 all-reduce.1
Sparse Core Ops, SparseCore 1:
  73.5 131.0 reduce-scatter.1
where the time goes:
time: 215 us; the launch traced here: 214 us
  waiting for transfers between devices  65.8 us (31%)
  blocking collectives  62.8 us (29%)
  starting transfers between devices  29.8 us (14%)
  matrix products  23.3 us (11%)
  between operations  15.8 us (7%)
  other arithmetic  12.4 us (6%)
  local copies, waits for them, and re-layouts  4.12 us (2%)
    psum x1, blocking collectives, on_device(): grad_stem = lax.psum(stem_grad[0] + stem_grad[1], 'seq')  62.8 us
    ppermute x12, waiting for transfers between devices, from_partner(): return lax.ppermute(value, axis, pairs)  32.1 us
    reduce_scatter x1, waiting for transfers between devices, on_device(): lax.psum_scatter(kernel_grad, 'seq', scatter_dimension=2, tiled=True)  29.8 us
    ppermute x12, starting transfers between devices, from_partner(): return lax.ppermute(value, axis, pairs)  22.8 us
    dot_general x5, matrix products, on_device(): jnp.einsum('spc,spd->scd', act[:, k:k + positions], out_grad, preferred_e...  10.7 us
    ppermute x2, starting transfers between devices, padded(): lax.ppermute(lax.slice_in_dim(block, block.shape[dim] - width, None, axis...  4.31 us
  transfers between devices with their start and end apart: 18, of which 12 were waited for; matrix products, arithmetic and copies ran while one was open for 15% of the time, Pallas kernels for 0%

commit v1 on v0

v1 whole, which is shorter than its diff:
```python
import functools
import math

import jax
import jax.numpy as jnp
from jax import lax
from jax.experimental import pallas as pl
from jax.experimental.pallas import tpu as pltpu
from jax.sharding import PartitionSpec as P

VMEM = pl.BlockSpec(memory_space=pltpu.VMEM)
SMEM = pl.BlockSpec(memory_space=pltpu.SMEM)
LANES = 128


def swap(value, mask):
    count = lax.axis_size("seq")
    return lax.ppermute(value, "seq", [(i, i ^ mask) for i in range(count)])


def swap_chan(value):
    count = lax.axis_size("chan")
    return lax.ppermute(value, "chan", [(i, i ^ 1) for i in range(count)])


def swap_next_chip(value):
    count = lax.axis_size("seq")
    pairs = [(i, i + 1) for i in range(1, count - 1, 2)]
    return lax.ppermute(value, "seq", pairs + [(b, a) for a, b in pairs])


def round_up(value, step):
    return (value + step - 1) // step * step


def gelu_value(stem):
    tanh_val = jnp.tanh(math.sqrt(2.0 / math.pi) * (stem + 0.044715 * stem * stem * stem))
    return 0.5 * stem * (1.0 + tanh_val), tanh_val


def gelu_slope(stem, tanh_val):
    coeff = math.sqrt(2.0 / math.pi)
    return 0.5 * (1.0 + tanh_val) + 0.5 * stem * (1.0 - tanh_val * tanh_val) * coeff * (
        1.0 + 3.0 * 0.044715 * stem * stem
    )


def indicators(codes, taps, middle, reverse):
    width = codes.shape[1]
    rows = 32
    wide = jnp.broadcast_to(codes, (rows, width))
    row = lax.broadcasted_iota(jnp.int32, (rows, width), 0)
    if reverse:
        row = 4 * taps - 1 - row
    seen = jnp.zeros((rows, width), jnp.int32)
    for k in range(taps):
        moved = pltpu.roll(wide, (middle - k) % width, 1) if k != middle else wide
        seen = jnp.where((row >= 4 * k) & (row < 4 * k + 4), moved, seen)
    letter = jnp.where(row >= 0, row & 3, 8) + 1
    return (seen == letter).astype(jnp.float32).astype(jnp.bfloat16)


def dot(left, right, dims=((1,), (0,))):
    return lax.dot_general(left, right, (dims, ((), ())), preferred_element_type=jnp.float32)


def local_kernel(taps, chan_ref, codes_ref, stem_w_ref, conv_w_ref, cot_ref, blended_ref, keep_ref, send_ref, act_f, act_r, stem_own, dact_f, dact_r, grad):
    span = cot_ref.shape[0]
    half = cot_ref.shape[1]
    rows = act_f.shape[0]
    chan = chan_ref[0]
    codes = codes_ref[...]
    hot_f = indicators(codes, taps, 0, False)[:, :rows]
    hot_r = indicators(codes, taps, 0, True)[:, :rows]
    centre = lax.broadcasted_iota(jnp.int32, (32, LANES), 0)
    centre = ((centre >= 8) & (centre < 12)).astype(jnp.float32).astype(jnp.bfloat16)
    inside = dot(hot_f, centre, ((0,), (0,)))[:, :1]
    stem_w = stem_w_ref[...]
    slopes = []
    for hot, act in ((hot_f, act_f), (hot_r, act_r)):
        stem = dot(hot, stem_w, ((0,), (0,))).astype(jnp.bfloat16).astype(jnp.float32)
        value, tanh_val = gelu_value(stem)
        act[...] = (value * inside).astype(jnp.bfloat16).astype(jnp.float32)
        slopes.append(gelu_slope(stem, tanh_val) * inside)
        if hot is hot_f:
            stem_own[...] = stem
        else:
            stem_own[...] += stem
    cot = cot_ref[...]
    dact_f[...] = jnp.zeros_like(dact_f)
    dact_r[...] = jnp.zeros_like(dact_r)
    total = stem_own[pl.ds(2, span), pl.ds(pl.multiple_of(chan * half, LANES), half)]
    for k in range(taps):
        weight = conv_w_ref[k]
        both = (act_f[k : k + span] + act_r[taps - 1 - k : taps - 1 - k + span]).astype(jnp.bfloat16)
        total += dot(both, weight)
        part = dot(cot, weight, ((1,), (1,)))
        dact_f[k : k + span] += part
        dact_r[taps - 1 - k : taps - 1 - k + span] += part
    blended_ref[...] = (0.5 * total).astype(jnp.bfloat16)
    result = jnp.zeros(grad.shape, jnp.float32)
    for hot, dact, slope in ((hot_f, dact_f, slopes[0]), (hot_r, dact_r, slopes[1])):
        dstem = 0.5 * dact[...] * slope
        high = dstem.astype(jnp.bfloat16)
        low = (dstem - high.astype(jnp.float32)).astype(jnp.bfloat16)
        result += dot(hot, high) + dot(hot, low)
    grad[...] = result
    keep_ref[...] = grad[: keep_ref.shape[0], pl.ds(pl.multiple_of(chan * half, LANES), half)]
    send_ref[...] = grad[: keep_ref.shape[0], pl.ds(pl.multiple_of((1 - chan) * half, LANES), half)]


def local_part(chan, codes, stem_w, conv_w, cot):
    taps, full, half = conv_w.shape
    span = cot.shape[0]
    rows = round_up(span + taps - 1, 16)
    out_rows = round_up(4 * taps, 8)
    return pl.pallas_call(
        functools.partial(local_kernel, taps),
        out_shape=(
            jax.ShapeDtypeStruct((span, half), jnp.bfloat16),
            jax.ShapeDtypeStruct((out_rows, half), jnp.float32),
            jax.ShapeDtypeStruct((out_rows, half), jnp.float32),
        ),
        in_specs=[SMEM, VMEM, VMEM, VMEM, VMEM],
        out_specs=(VMEM, VMEM, VMEM),
        scratch_shapes=[pltpu.VMEM((rows, full), jnp.float32) for _ in range(5)] + [pltpu.VMEM((32, full), jnp.float32)],
        compiler_params=pltpu.CompilerParams(vmem_limit_bytes=48 * 2**20),
        cost_estimate=pl.CostEstimate(flops=6 * span * taps * full * half, bytes_accessed=2 * taps * full * half, transcendentals=2 * span * full),
        name="local_part",
    )(chan, codes, stem_w, conv_w, cot)


def acts_kernel(taps, place, seq_ref, codes_ref, stem_w_ref, out_ref, line):
    count, span = codes_ref.shape
    chans = stem_w_ref.shape[0]
    seq = seq_ref[0]
    line[...] = jnp.zeros_like(line)
    for b in range(count):
        line[:, LANES + b * span : LANES + (b + 1) * span] = codes_ref[pl.ds(place(seq ^ b), 1), :]
    codes = line[...]
    stem_w = stem_w_ref[...]
    acts = []
    for reverse in (False, True):
        hot = indicators(codes, taps, taps // 2, reverse)
        stem = dot(stem_w, hot).astype(jnp.bfloat16).astype(jnp.float32)
        value, _ = gelu_value(stem)
        acts.append(jnp.where(codes > 0, value, 0.0).astype(jnp.bfloat16).astype(jnp.float32))
    width = codes.shape[1]
    for k in range(taps):
        move = (taps // 2 - k) % width
        back = (k - taps // 2) % width
        ahead = pltpu.roll(acts[0], move, 1) if move else acts[0]
        behind = pltpu.roll(acts[1], back, 1) if back else acts[1]
        out_ref[k * chans : (k + 1) * chans, :] = (ahead + behind)[:, LANES : LANES + count * span].astype(jnp.bfloat16)


def acts_part(seq, codes, stem_w, taps, place):
    count, span = codes.shape
    chans = stem_w.shape[0]
    return pl.pallas_call(
        functools.partial(acts_kernel, taps, place),
        out_shape=jax.ShapeDtypeStruct((taps * chans, count * span), jnp.bfloat16),
        in_specs=[SMEM, VMEM, VMEM],
        out_specs=VMEM,
        scratch_shapes=[pltpu.VMEM((1, count * span + 2 * LANES), jnp.int32)],
        compiler_params=pltpu.CompilerParams(vmem_limit_bytes=48 * 2**20),
        cost_estimate=pl.CostEstimate(flops=128 * count * span * chans, bytes_accessed=2 * taps * chans * count * span, transcendentals=2 * count * span * chans),
        name="acts_part",
    )(seq, codes, stem_w)


def grad_kernel(taps, kept, blocks, seq_ref, acts_ref, *refs):
    g_refs, out_ref = refs[:-1], refs[-1]
    span = g_refs[0].shape[0] // blocks[0][1]
    chans = acts_ref.shape[0] // taps
    seq = seq_ref[0]
    total = jnp.zeros((acts_ref.shape[0], g_refs[0].shape[1]), jnp.float32)
    for ref, (masks, _) in zip(g_refs, blocks):
        for i, mask in enumerate(masks):
            at = pl.multiple_of((seq ^ mask) * span, LANES)
            total += dot(acts_ref[:, pl.ds(at, span)], ref[i * span : (i + 1) * span, :])
    for k in range(taps):
        out_ref[k] = 0.5 * total[k * chans : k * chans + kept]


def grad_part(seq, acts, arrays, masks, taps, kept):
    half = arrays[0].shape[1]
    blocks = [(m, len(m)) for m in masks]
    return pl.pallas_call(
        functools.partial(grad_kernel, taps, kept, blocks),
        out_shape=jax.ShapeDtypeStruct((taps, kept, half), jnp.float32),
        in_specs=[SMEM, VMEM] + [VMEM] * len(arrays),
        out_specs=VMEM,
        compiler_params=pltpu.CompilerParams(vmem_limit_bytes=48 * 2**20),
        cost_estimate=pl.CostEstimate(flops=2 * acts.shape[0] * acts.shape[1] * half, bytes_accessed=2 * acts.size, transcendentals=0),
        name="grad_part",
    )(seq, acts, *arrays)


def on_device(tokens, stem_weight, conv_weight, cotangent):
    count = lax.axis_size("seq")
    seq = lax.axis_index("seq")
    chan = lax.axis_index("chan")
    span = tokens.shape[0]
    taps, full, half = conv_weight.shape
    edge = taps - 1
    far = range(4, count, 4)
    seq_arg = seq.astype(jnp.int32).reshape(1)
    chan_arg = chan.astype(jnp.int32).reshape(1)

    codes = tokens + 1
    mate = swap(codes, 1)
    other = swap_next_chip(codes)
    even = seq % 2 == 0
    before = jnp.where(even, other, mate)[span - edge :]
    after = jnp.where(even, mate, other)[:edge]
    ext = jnp.concatenate([before, codes, after, jnp.zeros(round_up(span + 2 * edge, LANES) - span - 2 * edge, jnp.int32)])

    far_cot = [cotangent] + [swap(cotangent, m) for m in far]
    far_codes = [codes] + [swap(codes, m) for m in far]
    table = jnp.stack(far_codes)
    table = jnp.concatenate([table, swap(table, 2)])
    table = jnp.concatenate([table, swap(table, 1)])
    quarter = count // 4

    def place(m):
        return (m & 1) * (2 * quarter) + ((m >> 1) & 1) * quarter + (m >> 2)

    flat_w = stem_weight.reshape(4 * taps, full)
    flat_w = jnp.pad(flat_w, ((0, 32 - 4 * taps), (0, 0)))
    blended, keep, send = local_part(chan_arg, ext[None], flat_w, conv_weight, cotangent)

    own = full // count
    own_w = lax.dynamic_slice_in_dim(flat_w, seq * own, own, 1).T
    own_w = jnp.pad(own_w, ((0, round_up(own, 16) - own), (0, 0)))
    acts = acts_part(seq_arg, table, own_w, taps, place)

    stem_grad = keep + swap_chan(send)
    stem_grad = sum([swap(stem_grad, m) for m in far], stem_grad)
    stem_grad = stem_grad + swap(stem_grad, 2)
    stem_grad = stem_grad + swap(stem_grad, 1)

    near = [swap(c, 2) for c in far_cot]
    chips = jnp.concatenate(far_cot + near)
    mates = swap(chips, 1)
    masks = [4 * z + 2 * x for x in range(2) for z in range(quarter)]
    grad_conv = grad_part(seq_arg, acts, [chips, mates], [masks, [m + 1 for m in masks]], taps, own)
    return blended, grad_conv, stem_grad[: 4 * taps].reshape(taps, 4, half)


def solution(mesh):
    return jax.shard_map(
        on_device,
        mesh=mesh,
        in_specs=(P("seq"), P(), P(None, None, "chan"), P("seq", "chan")),
        out_specs=(P("seq", "chan"), P(None, "seq", "chan"), P(None, None, "chan")),
        check_vma=False,
    )
```

time: 215 us -> 56.7 us (0.26)
  blocking collectives: 62.8 us -> 0 us
  waiting for transfers between devices: 65.8 us -> 16.4 us
  matrix products: 23.3 us -> 0 us
  between operations: 15.8 us -> 0.83 us
  other arithmetic: 12.4 us -> 0.79 us
  Pallas kernels: 0 us -> 6 us
  starting transfers between devices: 29.8 us -> 26.8 us
    psum x1 -> x0, blocking collectives: 62.8 us -> none  [on_device(): grad_stem = lax.psum(stem_grad[0] + stem_grad[1], 'seq')]
    reduce_scatter x1 -> x0, waiting for transfers between devices: 29.8 us -> none  [on_device(): lax.psum_scatter(kernel_grad, 'seq', scatter_dimension=2, tiled=True)]
    dot_general x25 -> x0, matrix products: 23.3 us -> none  [the longest x5 10.7 us: on_device(): jnp.einsum('spc,spd->scd', act[:, k:k + positions], out_grad, preferred_e...]
    ppermute x16 -> x21, waiting for transfers between devices: 35.9 us -> 16.4 us  [the longest x19 13.9 us: swap(): return lax.ppermute(value, 'seq', [(i, i ^ mask) for i in range(count)])]
    pallas_call x0 -> x3, Pallas kernels: none -> 6 us  [the longest x1 2.96 us: local_part(): pl.pallas_call(functools.partial(local_kernel, taps), out_shape=(jax.Shap...]
    squeeze x1 -> x0, other arithmetic: 3.93 us -> none  [on_device(): conv_pair[:, k]]
    mul x1 -> x0, other arithmetic: 2.98 us -> none  [on_device(): stem_in = data_full * slope_rows]
    ppermute x16 -> x21, starting transfers between devices: 29.7 us -> 26.8 us  [the longest x19 24.7 us: swap(): return lax.ppermute(value, 'seq', [(i, i ^ mask) for i in range(count)])]
  transfers between devices with their start and end apart: 18 -> 21, of which waited for: 12 -> 8; matrix products, arithmetic and copies ran while one was open for 15% -> 5% of each run, Pallas kernels for 0% -> 7%
where the time goes in v1:
time: 56.7 us; the launch traced here: 56.4 us
  starting transfers between devices  26.8 us (47%)
  waiting for transfers between devices  16.4 us (29%)
  Pallas kernels  6 us (11%)
  local copies, waits for them, and re-layouts  5.63 us (10%)
  between operations  0.83 us (1%)
  other arithmetic  0.79 us (1%)
    ppermute x19, starting transfers between devices, swap(): return lax.ppermute(value, 'seq', [(i, i ^ mask) for i in range(count)])  24.7 us
    ppermute x19, waiting for transfers between devices, swap(): return lax.ppermute(value, 'seq', [(i, i ^ mask) for i in range(count)])  13.9 us
    unnamed x12, local copies, waits for them, and re-layouts  3.9 us
    pallas_call x1, Pallas kernels, local_part(): pl.pallas_call(functools.partial(local_kernel, taps), out_shape=(jax.Shap...  2.96 us
    ppermute x1, waiting for transfers between devices, swap_chan(): return lax.ppermute(value, 'chan', [(i, i ^ 1) for i in range(count)])  2.44 us
    pallas_call x1, Pallas kernels, grad_part(): pl.pallas_call(functools.partial(grad_kernel, taps, kept, blocks), out_sh...  1.9 us
    ppermute x1, starting transfers between devices, swap_chan(): return lax.ppermute(value, 'chan', [(i, i ^ 1) for i in range(count)])  1.52 us
  transfers between devices with their start and end apart: 21, of which 8 were waited for; matrix products, arithmetic and copies ran while one was open for 5% of the time, Pallas kernels for 7%

profile of v1, /device:TPU:0, one launch (start us, length us, event | category | flops | bytes accessed | tf_op | source)
XLA Modules:
  0.0 56.4 jit_solution(532926785890528402)
XLA Ops:
  0.6 0.7 %fusion = (s32[1,128]{1,0:T(1,128)S(1)}, s32[128]{0:T(128)S(1)}) fusion(s32[128]{0:T(128)} %param.4), kind=kLoop, calls=%fused_computation.16 | loop fusion | flops 128 | bytes 1536 | tf_op jit(solution)/shard_map/stack | solution.py:221
  1.3 0.5 collective-permute-start.1
  1.7 0.6 %collective-permute-start = (s32[128]{0:T(128)S(1)}, s32[128]{0:T(128)S(1)}, u32[]{:S(2)}, u32[]{:S(2)}) collective-permute-start(s32[128]{0:T(128)S(1)} %get-tuple-element.12), channel_id=1, source_target_pairs={{2,4},{6,8},{10,12},{14,16},{18,20},{22,24},{26,28},{4,2},{8,6},{1... | collective-permute-start | bytes 1544 | tf_op jit(solution)/shard_map/ppermute | solution.py:29
  2.4 7.4 %collective-permute-start.9 = (bf16[128,384]{1,0:T(8,128)(2,1)}, bf16[128,384]{1,0:T(8,128)(2,1)S(1)}, u32[]{:S(2)}, u32[]{:S(2)}) collective-permute-start(bf16[128,384]{1,0:T(8,128)(2,1)} %cot_ref.1), channel_id=1, source_target_pairs={{0,24},{2,26},{4,28},{6,30},{8,16},{10,18},{12,20},{14,22},{16,8},... | collective-permute-start | bytes 294920 | tf_op jit(solution)/shard_map/ppermute | solution.py:18
  9.8 0.0 collective-permute-start.8
  9.8 0.6 %collective-permute-start.7 = (bf16[128,384]{1,0:T(8,128)(2,1)}, bf16[128,384]{1,0:T(8,128)(2,1)S(1)}, u32[]{:S(2)}, u32[]{:S(2)}) collective-permute-start(bf16[128,384]{1,0:T(8,128)(2,1)} %cot_ref.1), channel_id=1, source_target_pairs={{0,8},{2,10},{4,12},{6,14},{8,0},{10,2},{12,4},{14,6},{16,24},{18,... | collective-permute-start | bytes 294920 | tf_op jit(solution)/shard_map/ppermute | solution.py:18
  10.4 0.9 %constant_dynamic-update-slice_fusion.7 = bf16[1024,384]{1,0:T(8,128)(2,1)S(1)} fusion(bf16[128,384]{1,0:T(8,128)(2,1)} %cot_ref.1), kind=kLoop, calls=%fused_computation.9 | loop fusion | bytes 196608
  11.4 0.8 %reshape.19 = bf16[20,768]{1,0:T(8,128)(2,1)S(1)} reshape(bf16[5,4,768]{2,1,0:T(4,128)(2,1)} %param.5) | data formatting | bytes 61440 | tf_op jit(solution)/shard_map/reshape | solution.py:229
  12.2 0.2 copy.9
  12.3 0.1 copy.11
  12.5 0.0 collective-permute-done.1
  12.5 0.7 %collective-permute-start.10 = (bf16[128,384]{1,0:T(8,128)(2,1)}, bf16[128,384]{1,0:T(8,128)(2,1)S(1)}, u32[]{:S(2)}, u32[]{:S(2)}) collective-permute-start(bf16[128,384]{1,0:T(8,128)(2,1)} %cot_ref.1), channel_id=1, source_target_pairs={{0,4},{2,6},{4,0},{6,2},{8,12},{10,14},{12,8},{14,10},{16,20},{18,... | collective-permute-start | bytes 294920 | tf_op jit(solution)/shard_map/ppermute | solution.py:18
  13.2 0.0 collective-permute-done
  13.2 0.1 slice.9
  13.3 0.1 pad_add_fusion.1
  13.4 0.3 collective-permute-done.9
  13.7 1.1 %collective-permute-start.13 = (bf16[128,384]{1,0:T(8,128)(2,1)S(1)}, bf16[128,384]{1,0:T(8,128)(2,1)S(1)}, u32[]{:S(2)}, u32[]{:S(2)}) collective-permute-start(bf16[128,384]{1,0:T(8,128)(2,1)S(1)} %collective-permute-done.9), channel_id=1, source_target_pairs={{0,4},{2,6},{4,0},{6,2},{8,12},{10,14},{12,8},{14,10},{16,20},{18,... | collective-permute-start | bytes 294920 | tf_op jit(solution)/shard_map/ppermute | solution.py:18
  14.8 3.8 %collective-permute-done.8 = bf16[128,384]{1,0:T(8,128)(2,1)S(1)} collective-permute-done((bf16[128,384]{1,0:T(8,128)(2,1)}, bf16[128,384]{1,0:T(8,128)(2,1)S(1)}, u32[]{:S(2)}, u32[]{:S(2)}) %collective-permute-start.8) | collective-permute-done | bytes 98336 | tf_op jit(solution)/shard_map/ppermute | solution.py:18
  18.6 1.4 %collective-permute-start.12 = (bf16[128,384]{1,0:T(8,128)(2,1)S(1)}, bf16[128,384]{1,0:T(8,128)(2,1)S(1)}, u32[]{:S(2)}, u32[]{:S(2)}) collective-permute-start(bf16[128,384]{1,0:T(8,128)(2,1)S(1)} %collective-permute-done.8), channel_id=1, source_target_pairs={{0,4},{2,6},{4,0},{6,2},{8,12},{10,14},{12,8},{14,10},{16,20},{18,... | collective-permute-start | bytes 294920 | tf_op jit(solution)/shard_map/ppermute | solution.py:18
  20.0 0.0 collective-permute-done.7
  20.0 0.6 %collective-permute-start.11 = (bf16[128,384]{1,0:T(8,128)(2,1)S(1)}, bf16[128,384]{1,0:T(8,128)(2,1)S(1)}, u32[]{:S(2)}, u32[]{:S(2)}) collective-permute-start(bf16[128,384]{1,0:T(8,128)(2,1)S(1)} %collective-permute-done.7), channel_id=1, source_target_pairs={{0,4},{2,6},{4,0},{6,2},{8,12},{10,14},{12,8},{14,10},{16,20},{18,... | collective-permute-start | bytes 294920 | tf_op jit(solution)/shard_map/ppermute | solution.py:18
  20.7 0.0 collective-permute-done.10
  20.7 4.6 %collective-permute-done.11 = bf16[128,384]{1,0:T(8,128)(2,1)S(1)} collective-permute-done((bf16[128,384]{1,0:T(8,128)(2,1)S(1)}, bf16[128,384]{1,0:T(8,128)(2,1)S(1)}, u32[]{:S(2)}, u32[]{:S(2)}) %collective-permute-start.11) | collective-permute-done | bytes 98336 | tf_op jit(solution)/shard_map/ppermute | solution.py:18
  25.3 0.0 collective-permute-done.12
  25.4 0.1 collective-permute-start.14
  25.5 0.0 copy-start
  25.5 0.9 %copy-done = bf16[128,384]{1,0:T(8,128)(2,1)S(1)} copy-done((bf16[128,384]{1,0:T(8,128)(2,1)S(1)}, bf16[128,384]{1,0:T(8,128)(2,1)}, u32[]{:S(2)}) %copy-start) | copy-done | bytes 98328
  26.4 1.8 %copy-done.1 = bf16[5,768,384]{2,1,0:T(8,128)(2,1)S(1)} copy-done((bf16[5,768,384]{2,1,0:T(8,128)(2,1)S(1)}, bf16[5,768,384]{2,1,0:T(8,128)(2,1)}, u32[]{:S(2)}) %copy-start.1) | copy-done | bytes 2949144
  28.2 3.0 %local_part.1 = (bf16[128,384]{1,0:T(8,128)(2,1)}, f32[24,384]{1,0:T(8,128)S(1)}, f32[24,384]{1,0:T(8,128)S(1)}) custom-call(s32[1]{0:T(128)} %bitcast.chan_ref, s32[1,256]{1,0:T(1,128)S(1)} %bitcast.11, bf16[32,768]{1,0:T(8,128)(2,1)S(1)} %pad.4.clone.stem_w_ref, bf16[5,768,384]{2,1,0:T(8,128)(2,1)S(1)} %copy-done.1, bf16[128,384]{1,0:T(8,128)(2,1)S(1)} %copy-done), custom_call_target="tpu_custom_call" | custom-call | flops 1132462080 | bytes 2949120 | tf_op jit(solution)/shard_map/local_part/pallas_call | solution.py:117
  31.2 1.5 %collective-permute-start.15 = (f32[24,384]{1,0:T(8,128)S(1)}, f32[24,384]{1,0:T(8,128)S(1)}, u32[]{:S(2)}, u32[]{:S(2)}) collective-permute-start(f32[24,384]{1,0:T(8,128)S(1)} %get-tuple-element.8), channel_id=1, source_target_pairs={{0,1},{1,0},{2,3},{3,2},{4,5},{5,4},{6,7},{7,6},{8,9},{9,8},{10,11... | collective-permute-start | bytes 110600 | tf_op jit(solution)/shard_map/ppermute | solution.py:23
  32.7 2.4 %collective-permute-done.15 = f32[24,384]{1,0:T(8,128)S(1)} collective-permute-done((f32[24,384]{1,0:T(8,128)S(1)}, f32[24,384]{1,0:T(8,128)S(1)}, u32[]{:S(2)}, u32[]{:S(2)}) %collective-permute-start.15) | collective-permute-done | bytes 36896 | tf_op jit(solution)/shard_map/ppermute | solution.py:23
  35.1 2.4 %collective-permute-start.18 = (f32[24,384]{1,0:T(8,128)S(1)}, f32[24,384]{1,0:T(8,128)S(1)}, u32[]{:S(2)}, u32[]{:S(2)}) collective-permute-start(f32[24,384]{1,0:T(8,128)S(1)} %add.37), channel_id=1, source_target_pairs={{0,24},{2,26},{4,28},{6,30},{8,16},{10,18},{12,20},{14,22},{16,8},... | collective-permute-start | bytes 110600 | tf_op jit(solution)/shard_map/ppermute | solution.py:18
  37.5 0.0 collective-permute-start.17
  37.6 2.0 %collective-permute-start.16 = (f32[24,384]{1,0:T(8,128)S(1)}, f32[24,384]{1,0:T(8,128)S(1)}, u32[]{:S(2)}, u32[]{:S(2)}) collective-permute-start(f32[24,384]{1,0:T(8,128)S(1)} %add.37), channel_id=1, source_target_pairs={{0,8},{2,10},{4,12},{6,14},{8,0},{10,2},{12,4},{14,6},{16,24},{18,... | collective-permute-start | bytes 110600 | tf_op jit(solution)/shard_map/ppermute | solution.py:18
  39.5 0.9 %collective-permute-start.3 = (s32[128]{0:T(128)S(1)}, s32[128]{0:T(128)S(1)}, u32[]{:S(2)}, u32[]{:S(2)}) collective-permute-start(s32[128]{0:T(128)S(1)} %get-tuple-element.12), channel_id=1, source_target_pairs={{0,16},{2,18},{4,20},{6,22},{8,24},{10,26},{12,28},{14,30},{16,0},... | collective-permute-start | bytes 1544 | tf_op jit(solution)/shard_map/ppermute | solution.py:18
  40.4 0.4 collective-permute-done.18
  40.9 1.6 %collective-permute-start.2 = (s32[128]{0:T(128)S(1)}, s32[128]{0:T(128)S(1)}, u32[]{:S(2)}, u32[]{:S(2)}) collective-permute-start(s32[128]{0:T(128)S(1)} %get-tuple-element.12), channel_id=1, source_target_pairs={{0,8},{2,10},{4,12},{6,14},{8,0},{10,2},{12,4},{14,6},{16,24},{18,... | collective-permute-start | bytes 1544 | tf_op jit(solution)/shard_map/ppermute | solution.py:18
  42.5 1.8 %collective-permute-start.4 = (s32[128]{0:T(128)S(1)}, s32[128]{0:T(128)S(1)}, u32[]{:S(2)}, u32[]{:S(2)}) collective-permute-start(s32[128]{0:T(128)S(1)} %get-tuple-element.12), channel_id=1, source_target_pairs={{0,24},{2,26},{4,28},{6,30},{8,16},{10,18},{12,20},{14,22},{16,8},... | collective-permute-start | bytes 1544 | tf_op jit(solution)/shard_map/ppermute | solution.py:18
  44.3 1.5 %collective-permute-start.19 = (f32[24,384]{1,0:T(8,128)S(1)}, f32[24,384]{1,0:T(8,128)S(1)}, u32[]{:S(2)}, u32[]{:S(2)}) collective-permute-start(f32[24,384]{1,0:T(8,128)S(1)} %add_add_fusion), channel_id=1, source_target_pairs={{0,4},{2,6},{4,0},{6,2},{8,12},{10,14},{12,8},{14,10},{16,20},{18,... | collective-permute-start | bytes 110600 | tf_op jit(solution)/shard_map/ppermute | solution.py:18
  45.9 2.0 %collective-permute-done.4 = s32[128]{0:T(128)S(1)} collective-permute-done((s32[128]{0:T(128)S(1)}, s32[128]{0:T(128)S(1)}, u32[]{:S(2)}, u32[]{:S(2)}) %collective-permute-start.4) | collective-permute-done | bytes 544 | tf_op jit(solution)/shard_map/ppermute | solution.py:18
  47.8 1.4 %collective-permute-start.5 = (s32[4,128]{1,0:T(4,128)S(1)}, s32[4,128]{1,0:T(4,128)S(1)}, u32[]{:S(2)}, u32[]{:S(2)}) collective-permute-start(s32[4,128]{1,0:T(4,128)S(1)} %pad_add_fusion), channel_id=1, source_target_pairs={{0,4},{2,6},{4,0},{6,2},{8,12},{10,14},{12,8},{14,10},{16,20},{18,... | collective-permute-start | bytes 6152 | tf_op jit(solution)/shard_map/ppermute | solution.py:18
  49.2 2.3 %collective-permute-done.5 = s32[4,128]{1,0:T(4,128)S(1)} collective-permute-done((s32[4,128]{1,0:T(4,128)S(1)}, s32[4,128]{1,0:T(4,128)S(1)}, u32[]{:S(2)}, u32[]{:S(2)}) %collective-permute-start.5) | collective-permute-done | bytes 2080 | tf_op jit(solution)/shard_map/ppermute | solution.py:18
  51.5 0.1 collective-permute-start.6
  51.6 0.5 collective-permute-start.20
  52.1 0.6 %collective-permute-done.6 = s32[8,128]{1,0:T(8,128)S(1)} collective-permute-done((s32[8,128]{1,0:T(8,128)S(1)}, s32[8,128]{1,0:T(8,128)S(1)}, u32[]{:S(2)}, u32[]{:S(2)}) %collective-permute-start.6) | collective-permute-done | bytes 4128 | tf_op jit(solution)/shard_map/ppermute | solution.py:18
  52.7 1.1 %acts_part.1.acts_ref = bf16[240,2048]{1,0:T(8,128)(2,1)S(1)} custom-call(s32[1]{0:T(128)} %bitcast.2.seq_ref, s32[16,128]{1,0:T(8,128)S(1)} %concatenate.16.codes_ref, bf16[48,32]{1,0:T(8,128)(2,1)S(1)} %dynamic-slice_bitcast_fusion.stem_w_ref), custom_call_target="tpu_custom_call" | custom-call | flops 12582912 | bytes 983040 | tf_op jit(solution)/shard_map/acts_part/pallas_call | solution.py:160
  53.9 0.6 %reshape.21 = f32[5,4,384]{2,1,0:T(4,128)} reshape(f32[20,384]{1,0:T(8,128)S(1)} %slice_add_fusion) | data formatting | bytes 61440 | tf_op jit(solution)/shard_map/reshape | solution.py:248
  54.5 1.9 %grad_part.1 = f32[5,48,384]{2,1,0:T(8,128)} custom-call(s32[1]{0:T(128)} %bitcast.2.seq_ref, bf16[240,2048]{1,0:T(8,128)(2,1)S(1)} %acts_part.1.acts_ref, bf16[1024,384]{1,0:T(8,128)(2,1)S(1)} %constant_dynamic-update-slice_fusion.refs_0_, bf16[1024,384]{1,0:T(8,128)(2,1)S(1)} %collective-permute-done.14.refs_1_), custom_call_target="tpu_custom_call" | custom-call | flops 377487360 | bytes 983040 | tf_op jit(solution)/shard_map/grad_part/pallas_call | solution.py:189
  (27 shorter events, 0.3 us)
Async XLA Ops:
  1.3 11.2 %collective-permute-start.1 = (s32[128]{0:T(128)S(1)}, s32[128]{0:T(128)S(1)}, u32[]{:S(2)}, u32[]{:S(2)}) collective-permute-start(s32[128]{0:T(128)S(1)} %get-tuple-element.12), channel_id=1, source_target_pairs={{0,2},{2,0},{4,6},{6,4},{8,10},{10,8},{12,14},{14,12},{16,18},{18,... | collective-permute-start | bytes 1544 | tf_op jit(solution)/shard_map/ppermute | solution.py:18
  1.7 11.5 %collective-permute-start = (s32[128]{0:T(128)S(1)}, s32[128]{0:T(128)S(1)}, u32[]{:S(2)}, u32[]{:S(2)}) collective-permute-start(s32[128]{0:T(128)S(1)} %get-tuple-element.12), channel_id=1, source_target_pairs={{2,4},{6,8},{10,12},{14,16},{18,20},{22,24},{26,28},{4,2},{8,6},{1... | collective-permute-start | bytes 1544 | tf_op jit(solution)/shard_map/ppermute | solution.py:29
  2.4 11.3 %collective-permute-start.9 = (bf16[128,384]{1,0:T(8,128)(2,1)}, bf16[128,384]{1,0:T(8,128)(2,1)S(1)}, u32[]{:S(2)}, u32[]{:S(2)}) collective-permute-start(bf16[128,384]{1,0:T(8,128)(2,1)} %cot_ref.1), channel_id=1, source_target_pairs={{0,24},{2,26},{4,28},{6,30},{8,16},{10,18},{12,20},{14,22},{16,8},... | collective-permute-start | bytes 294920 | tf_op jit(solution)/shard_map/ppermute | solution.py:18
  9.8 8.8 %collective-permute-start.8 = (bf16[128,384]{1,0:T(8,128)(2,1)}, bf16[128,384]{1,0:T(8,128)(2,1)S(1)}, u32[]{:S(2)}, u32[]{:S(2)}) collective-permute-start(bf16[128,384]{1,0:T(8,128)(2,1)} %cot_ref.1), channel_id=1, source_target_pairs={{0,16},{2,18},{4,20},{6,22},{8,24},{10,26},{12,28},{14,30},{16,0},... | collective-permute-start | bytes 294920 | tf_op jit(solution)/shard_map/ppermute | solution.py:18
  9.8 10.2 %collective-permute-start.7 = (bf16[128,384]{1,0:T(8,128)(2,1)}, bf16[128,384]{1,0:T(8,128)(2,1)S(1)}, u32[]{:S(2)}, u32[]{:S(2)}) collective-permute-start(bf16[128,384]{1,0:T(8,128)(2,1)} %cot_ref.1), channel_id=1, source_target_pairs={{0,8},{2,10},{4,12},{6,14},{8,0},{10,2},{12,4},{14,6},{16,24},{18,... | collective-permute-start | bytes 294920 | tf_op jit(solution)/shard_map/ppermute | solution.py:18
  12.5 8.2 %collective-permute-start.10 = (bf16[128,384]{1,0:T(8,128)(2,1)}, bf16[128,384]{1,0:T(8,128)(2,1)S(1)}, u32[]{:S(2)}, u32[]{:S(2)}) collective-permute-start(bf16[128,384]{1,0:T(8,128)(2,1)} %cot_ref.1), channel_id=1, source_target_pairs={{0,4},{2,6},{4,0},{6,2},{8,12},{10,14},{12,8},{14,10},{16,20},{18,... | collective-permute-start | bytes 294920 | tf_op jit(solution)/shard_map/ppermute | solution.py:18
  13.7 11.6 %collective-permute-start.13 = (bf16[128,384]{1,0:T(8,128)(2,1)S(1)}, bf16[128,384]{1,0:T(8,128)(2,1)S(1)}, u32[]{:S(2)}, u32[]{:S(2)}) collective-permute-start(bf16[128,384]{1,0:T(8,128)(2,1)S(1)} %collective-permute-done.9), channel_id=1, source_target_pairs={{0,4},{2,6},{4,0},{6,2},{8,12},{10,14},{12,8},{14,10},{16,20},{18,... | collective-permute-start | bytes 294920 | tf_op jit(solution)/shard_map/ppermute | solution.py:18
  18.6 6.7 %collective-permute-start.12 = (bf16[128,384]{1,0:T(8,128)(2,1)S(1)}, bf16[128,384]{1,0:T(8,128)(2,1)S(1)}, u32[]{:S(2)}, u32[]{:S(2)}) collective-permute-start(bf16[128,384]{1,0:T(8,128)(2,1)S(1)} %collective-permute-done.8), channel_id=1, source_target_pairs={{0,4},{2,6},{4,0},{6,2},{8,12},{10,14},{12,8},{14,10},{16,20},{18,... | collective-permute-start | bytes 294920 | tf_op jit(solution)/shard_map/ppermute | solution.py:18
  20.0 5.3 %collective-permute-start.11 = (bf16[128,384]{1,0:T(8,128)(2,1)S(1)}, bf16[128,384]{1,0:T(8,128)(2,1)S(1)}, u32[]{:S(2)}, u32[]{:S(2)}) collective-permute-start(bf16[128,384]{1,0:T(8,128)(2,1)S(1)} %collective-permute-done.7), channel_id=1, source_target_pairs={{0,4},{2,6},{4,0},{6,2},{8,12},{10,14},{12,8},{14,10},{16,20},{18,... | collective-permute-start | bytes 294920 | tf_op jit(solution)/shard_map/ppermute | solution.py:18
  25.4 29.1 %collective-permute-start.14 = (bf16[1024,384]{1,0:T(8,128)(2,1)S(1)}, bf16[1024,384]{1,0:T(8,128)(2,1)S(1)}, u32[]{:S(2)}, u32[]{:S(2)}) collective-permute-start(bf16[1024,384]{1,0:T(8,128)(2,1)S(1)} %constant_dynamic-update-slice_fusion.refs_0_), channel_id=1, source_target_pairs={{0,2},{2,0},{4,6},{6,4},{8,10},{10,8},{12,14},{14,12},{16,18},{18,... | collective-permute-start | bytes 2359304 | tf_op jit(solution)/shard_map/ppermute | solution.py:18
  25.5 0.9 %copy-start = (bf16[128,384]{1,0:T(8,128)(2,1)S(1)}, bf16[128,384]{1,0:T(8,128)(2,1)}, u32[]{:S(2)}) copy-start(bf16[128,384]{1,0:T(8,128)(2,1)} %cot_ref.1) | copy-start | bytes 294916
  26.4 1.8 %copy-start.1 = (bf16[5,768,384]{2,1,0:T(8,128)(2,1)S(1)}, bf16[5,768,384]{2,1,0:T(8,128)(2,1)}, u32[]{:S(2)}) copy-start(bf16[5,768,384]{2,1,0:T(8,128)(2,1)} %conv_w_ref.1) | copy-start | bytes 8847364
  31.2 4.0 %collective-permute-start.15 = (f32[24,384]{1,0:T(8,128)S(1)}, f32[24,384]{1,0:T(8,128)S(1)}, u32[]{:S(2)}, u32[]{:S(2)}) collective-permute-start(f32[24,384]{1,0:T(8,128)S(1)} %get-tuple-element.8), channel_id=1, source_target_pairs={{0,1},{1,0},{2,3},{3,2},{4,5},{5,4},{6,7},{7,6},{8,9},{9,8},{10,11... | collective-permute-start | bytes 110600 | tf_op jit(solution)/shard_map/ppermute | solution.py:23
  35.1 5.8 %collective-permute-start.18 = (f32[24,384]{1,0:T(8,128)S(1)}, f32[24,384]{1,0:T(8,128)S(1)}, u32[]{:S(2)}, u32[]{:S(2)}) collective-permute-start(f32[24,384]{1,0:T(8,128)S(1)} %add.37), channel_id=1, source_target_pairs={{0,24},{2,26},{4,28},{6,30},{8,16},{10,18},{12,20},{14,22},{16,8},... | collective-permute-start | bytes 110600 | tf_op jit(solution)/shard_map/ppermute | solution.py:18
  37.5 5.0 %collective-permute-start.17 = (f32[24,384]{1,0:T(8,128)S(1)}, f32[24,384]{1,0:T(8,128)S(1)}, u32[]{:S(2)}, u32[]{:S(2)}) collective-permute-start(f32[24,384]{1,0:T(8,128)S(1)} %add.37), channel_id=1, source_target_pairs={{0,16},{2,18},{4,20},{6,22},{8,24},{10,26},{12,28},{14,30},{16,0},... | collective-permute-start | bytes 110600 | tf_op jit(solution)/shard_map/ppermute | solution.py:18
  37.6 6.7 %collective-permute-start.16 = (f32[24,384]{1,0:T(8,128)S(1)}, f32[24,384]{1,0:T(8,128)S(1)}, u32[]{:S(2)}, u32[]{:S(2)}) collective-permute-start(f32[24,384]{1,0:T(8,128)S(1)} %add.37), channel_id=1, source_target_pairs={{0,8},{2,10},{4,12},{6,14},{8,0},{10,2},{12,4},{14,6},{16,24},{18,... | collective-permute-start | bytes 110600 | tf_op jit(solution)/shard_map/ppermute | solution.py:18
  39.5 6.3 %collective-permute-start.3 = (s32[128]{0:T(128)S(1)}, s32[128]{0:T(128)S(1)}, u32[]{:S(2)}, u32[]{:S(2)}) collective-permute-start(s32[128]{0:T(128)S(1)} %get-tuple-element.12), channel_id=1, source_target_pairs={{0,16},{2,18},{4,20},{6,22},{8,24},{10,26},{12,28},{14,30},{16,0},... | collective-permute-start | bytes 1544 | tf_op jit(solution)/shard_map/ppermute | solution.py:18
  40.9 5.0 %collective-permute-start.2 = (s32[128]{0:T(128)S(1)}, s32[128]{0:T(128)S(1)}, u32[]{:S(2)}, u32[]{:S(2)}) collective-permute-start(s32[128]{0:T(128)S(1)} %get-tuple-element.12), channel_id=1, source_target_pairs={{0,8},{2,10},{4,12},{6,14},{8,0},{10,2},{12,4},{14,6},{16,24},{18,... | collective-permute-start | bytes 1544 | tf_op jit(solution)/shard_map/ppermute | solution.py:18
  42.5 5.3 %collective-permute-start.4 = (s32[128]{0:T(128)S(1)}, s32[128]{0:T(128)S(1)}, u32[]{:S(2)}, u32[]{:S(2)}) collective-permute-start(s32[128]{0:T(128)S(1)} %get-tuple-element.12), channel_id=1, source_target_pairs={{0,24},{2,26},{4,28},{6,30},{8,16},{10,18},{12,20},{14,22},{16,8},... | collective-permute-start | bytes 1544 | tf_op jit(solution)/shard_map/ppermute | solution.py:18
  44.3 7.3 %collective-permute-start.19 = (f32[24,384]{1,0:T(8,128)S(1)}, f32[24,384]{1,0:T(8,128)S(1)}, u32[]{:S(2)}, u32[]{:S(2)}) collective-permute-start(f32[24,384]{1,0:T(8,128)S(1)} %add_add_fusion), channel_id=1, source_target_pairs={{0,4},{2,6},{4,0},{6,2},{8,12},{10,14},{12,8},{14,10},{16,20},{18,... | collective-permute-start | bytes 110600 | tf_op jit(solution)/shard_map/ppermute | solution.py:18
  47.8 3.7 %collective-permute-start.5 = (s32[4,128]{1,0:T(4,128)S(1)}, s32[4,128]{1,0:T(4,128)S(1)}, u32[]{:S(2)}, u32[]{:S(2)}) collective-permute-start(s32[4,128]{1,0:T(4,128)S(1)} %pad_add_fusion), channel_id=1, source_target_pairs={{0,4},{2,6},{4,0},{6,2},{8,12},{10,14},{12,8},{14,10},{16,20},{18,... | collective-permute-start | bytes 6152 | tf_op jit(solution)/shard_map/ppermute | solution.py:18
  51.5 1.2 %collective-permute-start.6 = (s32[8,128]{1,0:T(8,128)S(1)}, s32[8,128]{1,0:T(8,128)S(1)}, u32[]{:S(2)}, u32[]{:S(2)}) collective-permute-start(s32[8,128]{1,0:T(8,128)S(1)} %concatenate.15), channel_id=1, source_target_pairs={{0,2},{2,0},{4,6},{6,4},{8,10},{10,8},{12,14},{14,12},{16,18},{18,... | collective-permute-start | bytes 12296 | tf_op jit(solution)/shard_map/ppermute | solution.py:18
  51.6 2.3 %collective-permute-start.20 = (f32[24,384]{1,0:T(8,128)S(1)}, f32[24,384]{1,0:T(8,128)S(1)}, u32[]{:S(2)}, u32[]{:S(2)}) collective-permute-start(f32[24,384]{1,0:T(8,128)S(1)} %add.41), channel_id=1, source_target_pairs={{0,2},{2,0},{4,6},{6,4},{8,10},{10,8},{12,14},{14,12},{16,18},{18,... | collective-permute-start | bytes 110600 | tf_op jit(solution)/shard_map/ppermute | solution.py:18

commit v2 on v1

v2 whole, which is shorter than its diff:
```python
import functools
import math

import jax
import jax.numpy as jnp
from jax import lax
from jax.experimental import pallas as pl
from jax.experimental.pallas import tpu as pltpu
from jax.sharding import PartitionSpec as P

VMEM = pl.BlockSpec(memory_space=pltpu.VMEM)
LANES = 128
LIMIT = 24 * 2**20
CHEAP = pl.CostEstimate(flops=0, bytes_accessed=0, transcendentals=0)


def swap(value, mask):
    count = lax.axis_size("seq")
    return lax.ppermute(value, "seq", [(i, i ^ mask) for i in range(count)])


def swap_chan(value):
    count = lax.axis_size("chan")
    return lax.ppermute(value, "chan", [(i, i ^ 1) for i in range(count)])


def swap_next_chip(value):
    count = lax.axis_size("seq")
    pairs = [(i, i + 1) for i in range(1, count - 1, 2)]
    return lax.ppermute(value, "seq", pairs + [(b, a) for a, b in pairs])


def round_up(value, step):
    return (value + step - 1) // step * step


def gelu_value(stem):
    tanh_val = jnp.tanh(math.sqrt(2.0 / math.pi) * (stem + 0.044715 * stem * stem * stem))
    return 0.5 * stem * (1.0 + tanh_val), tanh_val


def gelu_slope(stem, tanh_val):
    coeff = math.sqrt(2.0 / math.pi)
    return 0.5 * (1.0 + tanh_val) + 0.5 * stem * (1.0 - tanh_val * tanh_val) * coeff * (
        1.0 + 3.0 * 0.044715 * stem * stem
    )


def indicators(bases, taps, shift, width, reverse):
    rows = 32
    size = bases.shape[1]
    wide = jnp.broadcast_to(bases, (rows, size))
    row = lax.broadcasted_iota(jnp.int32, (rows, width), 0)
    if reverse:
        row = 4 * taps - 1 - row
    seen = jnp.full((rows, width), -1, jnp.int32)
    for k in range(taps):
        move = (-shift - k) % size
        moved = (pltpu.roll(wide, move, 1) if move else wide)[:, :width]
        seen = jnp.where((row >= 4 * k) & (row < 4 * k + 4), moved, seen)
    return (seen == (row & 3)).astype(jnp.float32).astype(jnp.bfloat16)


def dot(left, right, dims=((1,), (0,))):
    return lax.dot_general(left, right, (dims, ((), ())), preferred_element_type=jnp.float32)


def flat_kernel(stem_w_hbm, out_ref, stem_w_ref, sem):
    copy = pltpu.make_async_copy(stem_w_hbm, stem_w_ref, sem)
    copy.start()
    out_ref[...] = jnp.zeros_like(out_ref)
    copy.wait()
    for k in range(stem_w_ref.shape[0]):
        out_ref[4 * k : 4 * k + 4, :] = stem_w_ref[k].astype(jnp.float32)


def flat_part(stem_w):
    return pl.pallas_call(
        flat_kernel,
        out_shape=jax.ShapeDtypeStruct((32, stem_w.shape[2]), jnp.float32),
        in_specs=[pl.BlockSpec(memory_space=pl.ANY)],
        out_specs=VMEM,
        scratch_shapes=[pltpu.VMEM(stem_w.shape, stem_w.dtype), pltpu.SemaphoreType.DMA(())],
        cost_estimate=pl.CostEstimate(flops=6 * 10**9, bytes_accessed=0, transcendentals=0),
        name="flat_part",
    )(stem_w)


def line_of(own_ref, mate_ref, other_ref, line):
    span = own_ref.shape[1]
    seq = lax.axis_index("seq")
    even = lax.rem(seq, 2) == 0
    mate, other = mate_ref[...], other_ref[...]
    line[:, :span] = jnp.where(even, other, mate)
    line[:, span : 2 * span] = own_ref[...]
    line[:, 2 * span :] = jnp.where(even, mate, other)
    at = lax.broadcasted_iota(jnp.int32, line.shape, 1) + (seq - 1) * span
    return jnp.where((at >= 0) & (at < span * lax.axis_size("seq")), line[...], -1)


def centre_rows(taps):
    row = lax.broadcasted_iota(jnp.int32, (32, LANES), 0)
    reach = taps // 2
    return ((row >= 4 * reach) & (row < 4 * reach + 4)).astype(jnp.float32).astype(jnp.bfloat16)


def own_half(ref, rows, half, chan):
    return ref[rows, pl.ds(pl.multiple_of(chan * half, LANES), half)]


def back_kernel(cot_ref, conv_w, dact_f, dact_r):
    taps = conv_w.shape[0]
    span = cot_ref.shape[0]
    dact_f[...] = jnp.zeros_like(dact_f)
    dact_r[...] = jnp.zeros_like(dact_r)
    cot = cot_ref[...]
    for k in range(taps):
        part = dot(cot, conv_w[k], ((1,), (1,)))
        dact_f[k : k + span] += part
        dact_r[taps - 1 - k : taps - 1 - k + span] += part


def back_part(cot, conv_w):
    taps, full, _ = conv_w.shape
    rows = round_up(cot.shape[0] + taps - 1, 16)
    return pl.pallas_call(
        back_kernel,
        out_shape=tuple(jax.ShapeDtypeStruct((rows, full), jnp.float32) for _ in range(2)),
        in_specs=[VMEM] * 2,
        out_specs=(VMEM, VMEM),
        compiler_params=pltpu.CompilerParams(vmem_limit_bytes=LIMIT),
        cost_estimate=pl.CostEstimate(flops=14 * 10**8, bytes_accessed=0, transcendentals=0),
        name="back_part",
    )(cot, conv_w)


def stem_kernel(taps, dact_f, dact_r, own_ref, mate_ref, other_ref, flat, keep_ref, send_ref, line, grad):
    rows, full = dact_f.shape
    half = keep_ref.shape[1]
    span = own_ref.shape[1]
    seq, chan = lax.axis_index("seq"), lax.axis_index("chan")
    bases = line_of(own_ref, mate_ref, other_ref, line)
    stem_w = flat[...].astype(jnp.bfloat16)
    result = jnp.zeros(grad.shape, jnp.float32)
    for strand, dact in enumerate((dact_f, dact_r)):
        hot = indicators(bases, taps, span - 2 * (taps // 2), rows, strand == 1)
        if strand == 0:
            inside = dot(hot, centre_rows(taps), ((0,), (0,)))[:, :1]
        stem = dot(hot, stem_w, ((0,), (0,))).astype(jnp.bfloat16).astype(jnp.float32)
        _, tanh_val = gelu_value(stem)
        dstem = 0.5 * dact[...] * gelu_slope(stem, tanh_val) * inside
        high = dstem.astype(jnp.bfloat16)
        low = (dstem - high.astype(jnp.float32)).astype(jnp.bfloat16)
        result += dot(hot, high) + dot(hot, low)
    grad[...] = result
    top = send_ref.shape[0]
    keep_ref[:top, :] = own_half(grad, slice(0, top), half, chan)
    send_ref[...] = own_half(grad, slice(0, top), half, 1 - chan)
    per_row = half // span
    shape = (keep_ref.shape[0] - top, half)
    place = lax.broadcasted_iota(jnp.int32, shape, 0) * per_row + lax.broadcasted_iota(jnp.int32, shape, 1) // span
    table = jnp.zeros(shape, jnp.float32)
    for ref, block in ((own_ref, seq), (mate_ref, seq ^ 1)):
        row = jnp.broadcast_to(jnp.concatenate([ref[...].astype(jnp.float32)] * per_row, axis=1), shape)
        table = jnp.where(place == block, row, table)
    keep_ref[top:, :] = table


def stem_part(dacts, own, mate, other, flat, taps, half):
    full = flat.shape[1]
    span = own.shape[1]
    blocks = lax.axis_size("seq")
    per_row = half // span
    top = round_up(4 * taps, 8)
    rows = top + round_up((blocks + per_row - 1) // per_row, 8)
    return pl.pallas_call(
        functools.partial(stem_kernel, taps),
        out_shape=tuple(jax.ShapeDtypeStruct((r, half), jnp.float32) for r in (rows, top)),
        in_specs=[VMEM] * 6,
        out_specs=(VMEM, VMEM),
        scratch_shapes=[pltpu.VMEM((1, 3 * span), jnp.int32), pltpu.VMEM((32, full), jnp.float32)],
        compiler_params=pltpu.CompilerParams(vmem_limit_bytes=LIMIT),
        cost_estimate=CHEAP,
        name="stem_part",
    )(*dacts, own, mate, other, flat)


def blend_kernel(own_ref, mate_ref, other_ref, flat, conv_w, blended_ref, line, act_f, act_r, stem_own):
    taps = conv_w.shape[0]
    span, half = blended_ref.shape
    rows = act_f.shape[0]
    reach = taps // 2
    chan = lax.axis_index("chan")
    bases = line_of(own_ref, mate_ref, other_ref, line)
    stem_w = flat[...].astype(jnp.bfloat16)
    for strand, act in enumerate((act_f, act_r)):
        hot = indicators(bases, taps, span - 2 * reach, rows, strand == 1)
        if strand == 0:
            inside = dot(hot, centre_rows(taps), ((0,), (0,)))[:, :1]
        stem = dot(hot, stem_w, ((0,), (0,))).astype(jnp.bfloat16).astype(jnp.float32)
        value, _ = gelu_value(stem)
        act[...] = (value * inside).astype(jnp.bfloat16).astype(jnp.float32)
        if strand == 0:
            stem_own[...] = stem
        else:
            stem_own[...] += stem
    total = own_half(stem_own, pl.ds(reach, span), half, chan)
    for k in range(taps):
        back = taps - 1 - k
        both = (act_f[k : k + span] + act_r[back : back + span]).astype(jnp.bfloat16)
        total += dot(both, conv_w[k])
    blended_ref[...] = (0.5 * total).astype(jnp.bfloat16)


def blend_part(own, mate, other, flat, conv_w):
    taps, full, half = conv_w.shape
    span = own.shape[1]
    rows = round_up(span + taps - 1, 16)
    return pl.pallas_call(
        blend_kernel,
        out_shape=jax.ShapeDtypeStruct((span, half), jnp.bfloat16),
        in_specs=[VMEM] * 5,
        out_specs=VMEM,
        scratch_shapes=[pltpu.VMEM((1, 3 * span), jnp.int32)] + [pltpu.VMEM((rows, full), jnp.float32) for _ in range(3)],
        compiler_params=pltpu.CompilerParams(vmem_limit_bytes=LIMIT),
        cost_estimate=pl.CostEstimate(flops=2 * 10**9, bytes_accessed=0, transcendentals=0),
        name="blend_part",
    )(own, mate, other, flat, conv_w)


def grad_kernel(taps, kept, chans, masks, flat, table_ref, *refs):
    cots, out_ref, line, acts = refs[: len(masks)], *refs[len(masks) :]
    count = sum(map(len, masks))
    half = table_ref.shape[1]
    span = cots[0].shape[0] // len(masks[0])
    seq = lax.axis_index("seq")
    per_row = half // span
    top = round_up(4 * taps, 8)
    line[...] = jnp.full(line.shape, -1, jnp.int32)
    for b in range(count):
        row, lane = top + b // per_row, b % per_row * span
        line[:, LANES + b * span : LANES + (b + 1) * span] = table_ref[row : row + 1, lane : lane + span].astype(jnp.int32)
    bases = line[...]
    width = bases.shape[1]
    full = flat.shape[1]
    own_w = pltpu.roll(flat[...], lax.rem(full - seq * (full // count), full), 1)[:, :chans].astype(jnp.bfloat16)
    values = []
    reach = taps // 2
    for reverse in (False, True):
        hot = indicators(bases, taps, -reach, width, reverse)
        stem = dot(own_w, hot, ((0,), (0,))).astype(jnp.bfloat16).astype(jnp.float32)
        value, _ = gelu_value(stem)
        values.append(jnp.where(bases >= 0, value, 0.0).astype(jnp.bfloat16).astype(jnp.float32))
    order = [m for own in masks for m in own]
    for k in range(taps):
        move = (reach - k) % width
        back = (k - reach) % width
        ahead = pltpu.roll(values[0], move, 1) if move else values[0]
        behind = pltpu.roll(values[1], back, 1) if back else values[1]
        both = (ahead + behind).astype(jnp.bfloat16)
        for b in range(count):
            mask = seq ^ b
            slot = (mask & 3) * (count // 4) + lax.rem(count // 4 - (mask >> 2), count // 4)
            acts[k * chans : (k + 1) * chans, pl.ds(pl.multiple_of(slot * span, LANES), span)] = both[:, LANES + b * span : LANES + (b + 1) * span]
    total = jnp.zeros((taps * chans, half), jnp.float32)
    at = 0
    for ref in cots:
        total += dot(acts[:, at : at + ref.shape[0]], ref[...])
        at += ref.shape[0]
    for k in range(taps):
        out_ref[k] = 0.5 * total[k * chans : k * chans + kept]


def grad_part(flat, table, arrays, masks, span, taps):
    full = flat.shape[1]
    half = arrays[0].shape[1]
    count = sum(map(len, masks))
    kept = full // count
    chans = round_up(kept, 16)
    return pl.pallas_call(
        functools.partial(grad_kernel, taps, kept, chans, masks),
        out_shape=jax.ShapeDtypeStruct((taps, kept, half), jnp.float32),
        in_specs=[VMEM] * (2 + len(arrays)),
        out_specs=VMEM,
        scratch_shapes=[
            pltpu.VMEM((1, count * span + 2 * LANES), jnp.int32),
            pltpu.VMEM((taps * chans, count * span), jnp.bfloat16),
        ],
        compiler_params=pltpu.CompilerParams(vmem_limit_bytes=LIMIT),
        cost_estimate=pl.CostEstimate(flops=2 * 10**9, bytes_accessed=0, transcendentals=0),
        name="grad_part",
    )(flat, table, *arrays)


def after(value, *others):
    return lax.optimization_barrier((value, *others))[0]


def on_device(tokens, stem_weight, conv_weight, cotangent):
    count = lax.axis_size("seq")
    span = tokens.shape[0]
    taps, full, half = conv_weight.shape
    far = range(count - 4, 0, -4)

    bases = tokens.reshape(1, span)
    flat = flat_part(stem_weight)
    mate = swap(after(bases, flat), 1)
    cot = after(cotangent, flat)
    far_cot = [swap(cot, m) for m in far]
    other = swap_next_chip(bases)
    dacts = back_part(cot, conv_weight)
    keep, send = stem_part(dacts, bases, mate, other, flat, taps, half)
    got = swap_chan(send)
    total = jnp.concatenate([keep[: got.shape[0]] + got, keep[got.shape[0] :]])
    total, *far_cot = lax.optimization_barrier((total, *far_cot))
    here = jnp.concatenate([cotangent, *far_cot])
    there = swap(here, 2)
    here_mate = swap(here, 1)
    blended = blend_part(bases, mate, other, flat, conv_weight)
    for bit in range(2, (count - 1).bit_length()):
        total = total + swap(total, 1 << bit)
    total, here_mate, there, blended = lax.optimization_barrier((total, here_mate, there, blended))
    there_mate = swap(there, 1)
    total = total + swap(total, 2)
    total, there_mate = lax.optimization_barrier((total, there_mate))
    masks = [0, *far]
    masks = [[m + i for m in masks] for i in range(4)]
    grad_conv = grad_part(flat, total, [here, here_mate, there, there_mate], masks, span, taps)
    total = total[: 4 * taps] + swap(total[: 4 * taps], 1)
    return blended, grad_conv, total.reshape(taps, 4, half)


def solution(mesh):
    return jax.shard_map(
        on_device,
        mesh=mesh,
        in_specs=(P("seq"), P(), P(None, None, "chan"), P("seq", "chan")),
        out_specs=(P("seq", "chan"), P(None, "seq", "chan"), P(None, None, "chan")),
        check_vma=False,
    )
```

time: 56.7 us -> 38.6 us (0.68)
  waiting for transfers between devices: 16.4 us -> 6.84 us
  starting transfers between devices: 26.8 us -> 21.4 us
  local copies, waits for them, and re-layouts: 5.63 us -> 0.72 us
  Pallas kernels: 6 us -> 8.62 us
  other arithmetic: 0.79 us -> 0.04 us
    ppermute x19 -> x11, waiting for transfers between devices: 13.9 us -> 4.42 us  [swap(): return lax.ppermute(value, 'seq', [(i, i ^ mask) for i in range(count)])]
    ppermute x19 -> x11, starting transfers between devices: 24.7 us -> 19.1 us  [swap(): return lax.ppermute(value, 'seq', [(i, i ^ mask) for i in range(count)])]
    unnamed x12 -> x11, local copies, waits for them, and re-layouts: 3.9 us -> 0.07 us
    pallas_call x3 -> x5, Pallas kernels: 6 us -> 8.62 us  [the longest x1 2.7 us: grad_part(): pl.pallas_call(functools.partial(grad_kernel, taps, kept, chans, masks),...]
    reshape x3 -> x1, local copies, waits for them, and re-layouts: 1.57 us -> 0.62 us  [on_device(): return (blended, grad_conv, total.reshape(taps, 4, half))]
    another operation x2 -> x0, other arithmetic: 0.67 us -> none  [on_device(): table = jnp.stack(far_codes)]
  transfers between devices with their start and end apart: 21 -> 13, of which waited for: 8 -> 3; matrix products, arithmetic and copies ran while one was open for 5% -> 0% of each run, Pallas kernels for 7% -> 18%
where the time goes in v2:
time: 38.6 us; the launch traced here: 38.4 us
  starting transfers between devices  21.4 us (55%)
  Pallas kernels  8.62 us (22%)
  waiting for transfers between devices  6.84 us (18%)
  between operations  0.85 us (2%)
  local copies, waits for them, and re-layouts  0.72 us (2%)
    ppermute x11, starting transfers between devices, swap(): return lax.ppermute(value, 'seq', [(i, i ^ mask) for i in range(count)])  19.1 us
    ppermute x11, waiting for transfers between devices, swap(): return lax.ppermute(value, 'seq', [(i, i ^ mask) for i in range(count)])  4.42 us
    pallas_call x1, Pallas kernels, grad_part(): pl.pallas_call(functools.partial(grad_kernel, taps, kept, chans, masks),...  2.7 us
    ppermute x1, waiting for transfers between devices, swap_chan(): return lax.ppermute(value, 'chan', [(i, i ^ 1) for i in range(count)])  2.41 us
    pallas_call x1, Pallas kernels, blend_part(): pl.pallas_call(blend_kernel, out_shape=jax.ShapeDtypeStruct((span, half),...  2.08 us
    ppermute x1, starting transfers between devices, swap_chan(): return lax.ppermute(value, 'chan', [(i, i ^ 1) for i in range(count)])  1.61 us
    pallas_call x1, Pallas kernels, flat_part(): pl.pallas_call(flat_kernel, out_shape=jax.ShapeDtypeStruct((32, stem_w.sh...  1.56 us
    pallas_call x1, Pallas kernels, stem_part(): pl.pallas_call(functools.partial(stem_kernel, taps), out_shape=tuple((jax...  1.27 us
  transfers between devices with their start and end apart: 13, of which 3 were waited for; matrix products, arithmetic and copies ran while one was open for 0% of the time, Pallas kernels for 18%

profile of v2, /device:TPU:0, one launch (start us, length us, event | category | flops | bytes accessed | tf_op | source)
XLA Modules:
  0.0 38.4 jit_solution(14348148584058667438)
XLA Ops:
  0.6 0.0 copy-start.1
  0.6 0.0 copy-start.2
  0.7 0.0 copy-start.3
  0.7 1.6 %flat_part.1.flat = f32[32,768]{1,0:T(8,128)} custom-call(bf16[5,4,768]{2,1,0:T(4,128)(2,1)} %stem_w_hbm.1), custom_call_target="tpu_custom_call" | custom-call | flops 6000000000 | tf_op jit(solution)/shard_map/flat_part/pallas_call | solution.py:78
  2.2 0.0 copy-done.1
  2.2 0.0 copy-start
  2.3 3.1 %collective-permute-start.5 = (bf16[128,384]{1,0:T(8,128)(2,1)S(1)}, bf16[128,384]{1,0:T(8,128)(2,1)S(1)}, u32[]{:S(2)}, u32[]{:S(2)}) collective-permute-start(bf16[128,384]{1,0:T(8,128)(2,1)S(1)} %copy-done.1), channel_id=1, source_target_pairs={{0,8},{2,10},{4,12},{6,14},{8,0},{10,2},{12,4},{14,6},{16,24},{18,... | collective-permute-start | bytes 294920 | tf_op jit(solution)/shard_map/ppermute | solution.py:19
  5.3 2.6 %collective-permute-start.4 = (bf16[128,384]{1,0:T(8,128)(2,1)S(1)}, bf16[128,384]{1,0:T(8,128)(2,1)S(1)}, u32[]{:S(2)}, u32[]{:S(2)}) collective-permute-start(bf16[128,384]{1,0:T(8,128)(2,1)S(1)} %copy-done.1), channel_id=1, source_target_pairs={{0,16},{2,18},{4,20},{6,22},{8,24},{10,26},{12,28},{14,30},{16,0},... | collective-permute-start | bytes 294920 | tf_op jit(solution)/shard_map/ppermute | solution.py:19
  7.9 0.0 collective-permute-start.3
  7.9 0.0 copy-done.2
  7.9 0.7 %collective-permute-start.1 = (s32[1,128]{1,0:T(1,128)S(1)}, s32[1,128]{1,0:T(1,128)S(1)}, u32[]{:S(2)}, u32[]{:S(2)}) collective-permute-start(s32[1,128]{1,0:T(1,128)S(1)} %bitcast.1), channel_id=1, source_target_pairs={{2,4},{6,8},{10,12},{14,16},{18,20},{22,24},{26,28},{4,2},{8,6},{1... | collective-permute-start | bytes 1544 | tf_op jit(solution)/shard_map/ppermute | solution.py:30
  8.6 3.1 %collective-permute-start = (s32[1,128]{1,0:T(1,128)S(1)}, s32[1,128]{1,0:T(1,128)S(1)}, u32[]{:S(2)}, u32[]{:S(2)}) collective-permute-start(s32[1,128]{1,0:T(1,128)S(1)} %bitcast.2), channel_id=1, source_target_pairs={{0,2},{2,0},{4,6},{6,4},{8,10},{10,8},{12,14},{14,12},{16,18},{18,... | collective-permute-start | bytes 1544 | tf_op jit(solution)/shard_map/ppermute | solution.py:19
  11.7 0.0 copy-done.3
  11.7 1.0 %back_part.1 = (f32[144,768]{1,0:T(8,128)S(1)}, f32[144,768]{1,0:T(8,128)S(1)}) custom-call(bf16[128,384]{1,0:T(8,128)(2,1)S(1)} %copy-done.1, bf16[5,768,384]{2,1,0:T(8,128)(2,1)S(1)} %copy-done.3), custom_call_target="tpu_custom_call" | custom-call | flops 1400000000 | tf_op jit(solution)/shard_map/back_part/pallas_call | solution.py:126
  12.8 0.0 collective-permute-done.1.other_ref
  12.8 0.0 collective-permute-done.mate_ref
  12.8 0.0 copy-done
  12.8 1.3 %stem_part.1 = (f32[32,384]{1,0:T(8,128)S(1)}, f32[24,384]{1,0:T(8,128)S(1)}) custom-call(f32[144,768]{1,0:T(8,128)S(1)} %get-tuple-element.20.dact_f, f32[144,768]{1,0:T(8,128)S(1)} %get-tuple-element.21.dact_r, s32[1,128]{1,0:T(1,128)S(1)} %bitcast.3, s32[1,128]{1,0:T(1,128)S(1)} %collective-permute-done.mate_ref, ...), custom_call_target="tpu_custom_call" | custom-call | tf_op jit(solution)/shard_map/stem_part/pallas_call | solution.py:176
  14.1 1.6 %collective-permute-start.2 = (f32[24,384]{1,0:T(8,128)S(1)}, f32[24,384]{1,0:T(8,128)S(1)}, u32[]{:S(2)}, u32[]{:S(2)}) collective-permute-start(f32[24,384]{1,0:T(8,128)S(1)} %get-tuple-element.24), channel_id=1, source_target_pairs={{0,1},{1,0},{2,3},{3,2},{4,5},{5,4},{6,7},{7,6},{8,9},{9,8},{10,11... | collective-permute-start | bytes 110600 | tf_op jit(solution)/shard_map/ppermute | solution.py:24
  15.7 2.4 %collective-permute-done.2 = f32[24,384]{1,0:T(8,128)S(1)} collective-permute-done((f32[24,384]{1,0:T(8,128)S(1)}, f32[24,384]{1,0:T(8,128)S(1)}, u32[]{:S(2)}, u32[]{:S(2)}) %collective-permute-start.2) | collective-permute-done | bytes 36896 | tf_op jit(solution)/shard_map/ppermute | solution.py:24
  18.1 0.0 collective-permute-done.5
  18.1 0.0 collective-permute-done.4
  18.1 0.0 collective-permute-done.3
  18.2 1.8 %collective-permute-start.9 = (bf16[512,384]{1,0:T(8,128)(2,1)S(1)}, bf16[512,384]{1,0:T(8,128)(2,1)S(1)}, u32[]{:S(2)}, u32[]{:S(2)}) collective-permute-start(bf16[512,384]{1,0:T(8,128)(2,1)S(1)} %constant_dynamic-update-slice_fusion.refs_0_), channel_id=1, source_target_pairs={{0,4},{2,6},{4,0},{6,2},{8,12},{10,14},{12,8},{14,10},{16,20},{18,... | collective-permute-start | bytes 1179656 | tf_op jit(solution)/shard_map/ppermute | solution.py:19
  20.0 0.0 collective-permute-start.8
  20.0 2.7 %collective-permute-start.6 = (f32[32,384]{1,0:T(8,128)S(1)}, f32[32,384]{1,0:T(8,128)S(1)}, u32[]{:S(2)}, u32[]{:S(2)}) collective-permute-start(f32[32,384]{1,0:T(8,128)S(1)} %pad_maximum_fusion), channel_id=1, source_target_pairs={{0,8},{2,10},{4,12},{6,14},{8,0},{10,2},{12,4},{14,6},{16,24},{18,... | collective-permute-start | bytes 147464 | tf_op jit(solution)/shard_map/ppermute | solution.py:19
  22.7 2.1 %collective-permute-done.6 = f32[32,384]{1,0:T(8,128)S(1)} collective-permute-done((f32[32,384]{1,0:T(8,128)S(1)}, f32[32,384]{1,0:T(8,128)S(1)}, u32[]{:S(2)}, u32[]{:S(2)}) %collective-permute-start.6) | collective-permute-done | bytes 49184 | tf_op jit(solution)/shard_map/ppermute | solution.py:19
  24.8 3.2 %collective-permute-start.7 = (f32[32,384]{1,0:T(8,128)S(1)}, f32[32,384]{1,0:T(8,128)S(1)}, u32[]{:S(2)}, u32[]{:S(2)}) collective-permute-start(f32[32,384]{1,0:T(8,128)S(1)} %add.16), channel_id=1, source_target_pairs={{0,16},{2,18},{4,20},{6,22},{8,24},{10,26},{12,28},{14,30},{16,0},... | collective-permute-start | bytes 147464 | tf_op jit(solution)/shard_map/ppermute | solution.py:19
  28.0 2.1 %blend_part.1 = bf16[128,384]{1,0:T(8,128)(2,1)} custom-call(s32[1,128]{1,0:T(1,128)S(1)} %bitcast.4, s32[1,128]{1,0:T(1,128)S(1)} %collective-permute-done.mate_ref, s32[1,128]{1,0:T(1,128)S(1)} %collective-permute-done.1.other_ref, f32[32,768]{1,0:T(8,128)S(1)} %copy-done, bf16[5,768,384]{2,1,0:T(8,128)(2,1)S(1)} %copy-done.3), custom_call_target="tpu_custom_call" | custom-call | flops 2000000000 | tf_op jit(solution)/shard_map/blend_part/pallas_call | solution.py:219
  30.0 0.0 collective-permute-done.7
  30.0 0.0 collective-permute-done.9.refs_2_
  30.1 0.0 collective-permute-done.8.refs_1_
  30.1 0.1 collective-permute-start.11
  30.1 2.5 %collective-permute-start.10 = (f32[32,384]{1,0:T(8,128)S(1)}, f32[32,384]{1,0:T(8,128)S(1)}, u32[]{:S(2)}, u32[]{:S(2)}) collective-permute-start(f32[32,384]{1,0:T(8,128)S(1)} %add.17), channel_id=1, source_target_pairs={{0,4},{2,6},{4,0},{6,2},{8,12},{10,14},{12,8},{14,10},{16,20},{18,... | collective-permute-start | bytes 147464 | tf_op jit(solution)/shard_map/ppermute | solution.py:19
  32.7 2.3 %collective-permute-done.10 = f32[32,384]{1,0:T(8,128)S(1)} collective-permute-done((f32[32,384]{1,0:T(8,128)S(1)}, f32[32,384]{1,0:T(8,128)S(1)}, u32[]{:S(2)}, u32[]{:S(2)}) %collective-permute-start.10) | collective-permute-done | bytes 49184 | tf_op jit(solution)/shard_map/ppermute | solution.py:19
  35.0 0.0 collective-permute-done.11.refs_3_
  35.0 0.1 collective-permute-start.12
  35.1 2.7 %grad_part.1 = f32[5,48,384]{2,1,0:T(8,128)} custom-call(f32[32,768]{1,0:T(8,128)S(1)} %copy-done, f32[32,384]{1,0:T(8,128)S(1)} %add.18.table_ref, bf16[512,384]{1,0:T(8,128)(2,1)S(1)} %constant_dynamic-update-slice_fusion.refs_0_, bf16[512,384]{1,0:T(8,128)(2,1)S(1)} %collective-permute-done.8.refs_1_, ...), custom_call_target="tpu_custom_call" | custom-call | flops 2000000000 | tf_op jit(solution)/shard_map/grad_part/pallas_call | solution.py:280
  37.8 0.0 collective-permute-done.12
  37.8 0.6 %reshape.13 = f32[5,4,384]{2,1,0:T(4,128)} reshape(f32[20,384]{1,0:T(8,128)S(1)} %slice_add_fusion.1) | data formatting | bytes 61440 | tf_op jit(solution)/shard_map/reshape | solution.py:330
  (12 shorter events, 0.1 us)
Async XLA Ops:
  0.6 1.6 %copy-start.1 = (bf16[128,384]{1,0:T(8,128)(2,1)S(1)}, bf16[128,384]{1,0:T(8,128)(2,1)}, u32[]{:S(2)}) copy-start(bf16[128,384]{1,0:T(8,128)(2,1)} %cot_ref) | copy-start | bytes 294916
  0.6 7.3 %copy-start.2 = (s32[128]{0:T(128)S(1)}, s32[128]{0:T(128)}, u32[]{:S(2)}) copy-start(s32[128]{0:T(128)} %param.4) | copy-start | bytes 1540
  0.7 11.1 %copy-start.3 = (bf16[5,768,384]{2,1,0:T(8,128)(2,1)S(1)}, bf16[5,768,384]{2,1,0:T(8,128)(2,1)}, u32[]{:S(2)}) copy-start(bf16[5,768,384]{2,1,0:T(8,128)(2,1)} %conv_w.3) | copy-start | bytes 8847364
  2.2 10.5 %copy-start = (f32[32,768]{1,0:T(8,128)S(1)}, f32[32,768]{1,0:T(8,128)}, u32[]{:S(2)}) copy-start(f32[32,768]{1,0:T(8,128)} %flat_part.1.flat) | copy-start | bytes 294916
  2.3 15.9 %collective-permute-start.5 = (bf16[128,384]{1,0:T(8,128)(2,1)S(1)}, bf16[128,384]{1,0:T(8,128)(2,1)S(1)}, u32[]{:S(2)}, u32[]{:S(2)}) collective-permute-start(bf16[128,384]{1,0:T(8,128)(2,1)S(1)} %copy-done.1), channel_id=1, source_target_pairs={{0,8},{2,10},{4,12},{6,14},{8,0},{10,2},{12,4},{14,6},{16,24},{18,... | collective-permute-start | bytes 294920 | tf_op jit(solution)/shard_map/ppermute | solution.py:19
  5.3 12.8 %collective-permute-start.4 = (bf16[128,384]{1,0:T(8,128)(2,1)S(1)}, bf16[128,384]{1,0:T(8,128)(2,1)S(1)}, u32[]{:S(2)}, u32[]{:S(2)}) collective-permute-start(bf16[128,384]{1,0:T(8,128)(2,1)S(1)} %copy-done.1), channel_id=1, source_target_pairs={{0,16},{2,18},{4,20},{6,22},{8,24},{10,26},{12,28},{14,30},{16,0},... | collective-permute-start | bytes 294920 | tf_op jit(solution)/shard_map/ppermute | solution.py:19
  7.9 10.2 %collective-permute-start.3 = (bf16[128,384]{1,0:T(8,128)(2,1)S(1)}, bf16[128,384]{1,0:T(8,128)(2,1)S(1)}, u32[]{:S(2)}, u32[]{:S(2)}) collective-permute-start(bf16[128,384]{1,0:T(8,128)(2,1)S(1)} %copy-done.1), channel_id=1, source_target_pairs={{0,24},{2,26},{4,28},{6,30},{8,16},{10,18},{12,20},{14,22},{16,8},... | collective-permute-start | bytes 294920 | tf_op jit(solution)/shard_map/ppermute | solution.py:19
  7.9 4.8 %collective-permute-start.1 = (s32[1,128]{1,0:T(1,128)S(1)}, s32[1,128]{1,0:T(1,128)S(1)}, u32[]{:S(2)}, u32[]{:S(2)}) collective-permute-start(s32[1,128]{1,0:T(1,128)S(1)} %bitcast.1), channel_id=1, source_target_pairs={{2,4},{6,8},{10,12},{14,16},{18,20},{22,24},{26,28},{4,2},{8,6},{1... | collective-permute-start | bytes 1544 | tf_op jit(solution)/shard_map/ppermute | solution.py:30
  8.6 4.2 %collective-permute-start = (s32[1,128]{1,0:T(1,128)S(1)}, s32[1,128]{1,0:T(1,128)S(1)}, u32[]{:S(2)}, u32[]{:S(2)}) collective-permute-start(s32[1,128]{1,0:T(1,128)S(1)} %bitcast.2), channel_id=1, source_target_pairs={{0,2},{2,0},{4,6},{6,4},{8,10},{10,8},{12,14},{14,12},{16,18},{18,... | collective-permute-start | bytes 1544 | tf_op jit(solution)/shard_map/ppermute | solution.py:19
  14.1 4.0 %collective-permute-start.2 = (f32[24,384]{1,0:T(8,128)S(1)}, f32[24,384]{1,0:T(8,128)S(1)}, u32[]{:S(2)}, u32[]{:S(2)}) collective-permute-start(f32[24,384]{1,0:T(8,128)S(1)} %get-tuple-element.24), channel_id=1, source_target_pairs={{0,1},{1,0},{2,3},{3,2},{4,5},{5,4},{6,7},{7,6},{8,9},{9,8},{10,11... | collective-permute-start | bytes 110600 | tf_op jit(solution)/shard_map/ppermute | solution.py:24
  18.2 11.8 %collective-permute-start.9 = (bf16[512,384]{1,0:T(8,128)(2,1)S(1)}, bf16[512,384]{1,0:T(8,128)(2,1)S(1)}, u32[]{:S(2)}, u32[]{:S(2)}) collective-permute-start(bf16[512,384]{1,0:T(8,128)(2,1)S(1)} %constant_dynamic-update-slice_fusion.refs_0_), channel_id=1, source_target_pairs={{0,4},{2,6},{4,0},{6,2},{8,12},{10,14},{12,8},{14,10},{16,20},{18,... | collective-permute-start | bytes 1179656 | tf_op jit(solution)/shard_map/ppermute | solution.py:19
  20.0 10.1 %collective-permute-start.8 = (bf16[512,384]{1,0:T(8,128)(2,1)S(1)}, bf16[512,384]{1,0:T(8,128)(2,1)S(1)}, u32[]{:S(2)}, u32[]{:S(2)}) collective-permute-start(bf16[512,384]{1,0:T(8,128)(2,1)S(1)} %constant_dynamic-update-slice_fusion.refs_0_), channel_id=1, source_target_pairs={{0,2},{2,0},{4,6},{6,4},{8,10},{10,8},{12,14},{14,12},{16,18},{18,... | collective-permute-start | bytes 1179656 | tf_op jit(solution)/shard_map/ppermute | solution.py:19
  20.0 4.8 %collective-permute-start.6 = (f32[32,384]{1,0:T(8,128)S(1)}, f32[32,384]{1,0:T(8,128)S(1)}, u32[]{:S(2)}, u32[]{:S(2)}) collective-permute-start(f32[32,384]{1,0:T(8,128)S(1)} %pad_maximum_fusion), channel_id=1, source_target_pairs={{0,8},{2,10},{4,12},{6,14},{8,0},{10,2},{12,4},{14,6},{16,24},{18,... | collective-permute-start | bytes 147464 | tf_op jit(solution)/shard_map/ppermute | solution.py:19
  24.8 5.3 %collective-permute-start.7 = (f32[32,384]{1,0:T(8,128)S(1)}, f32[32,384]{1,0:T(8,128)S(1)}, u32[]{:S(2)}, u32[]{:S(2)}) collective-permute-start(f32[32,384]{1,0:T(8,128)S(1)} %add.16), channel_id=1, source_target_pairs={{0,16},{2,18},{4,20},{6,22},{8,24},{10,26},{12,28},{14,30},{16,0},... | collective-permute-start | bytes 147464 | tf_op jit(solution)/shard_map/ppermute | solution.py:19
  30.1 4.9 %collective-permute-start.11 = (bf16[512,384]{1,0:T(8,128)(2,1)S(1)}, bf16[512,384]{1,0:T(8,128)(2,1)S(1)}, u32[]{:S(2)}, u32[]{:S(2)}) collective-permute-start(bf16[512,384]{1,0:T(8,128)(2,1)S(1)} %collective-permute-done.9.refs_2_), channel_id=1, source_target_pairs={{0,2},{2,0},{4,6},{6,4},{8,10},{10,8},{12,14},{14,12},{16,18},{18,... | collective-permute-start | bytes 1179656 | tf_op jit(solution)/shard_map/ppermute | solution.py:19
  30.1 4.9 %collective-permute-start.10 = (f32[32,384]{1,0:T(8,128)S(1)}, f32[32,384]{1,0:T(8,128)S(1)}, u32[]{:S(2)}, u32[]{:S(2)}) collective-permute-start(f32[32,384]{1,0:T(8,128)S(1)} %add.17), channel_id=1, source_target_pairs={{0,4},{2,6},{4,0},{6,2},{8,12},{10,14},{12,8},{14,10},{16,20},{18,... | collective-permute-start | bytes 147464 | tf_op jit(solution)/shard_map/ppermute | solution.py:19
  35.0 2.8 %collective-permute-start.12 = (f32[20,384]{1,0:T(8,128)S(1)}, f32[20,384]{1,0:T(8,128)S(1)}, u32[]{:S(2)}, u32[]{:S(2)}) collective-permute-start(f32[20,384]{1,0:T(8,128)S(1)} %slice.12), channel_id=1, source_target_pairs={{0,2},{2,0},{4,6},{6,4},{8,10},{10,8},{12,14},{14,12},{16,18},{18,... | collective-permute-start | bytes 92168 | tf_op jit(solution)/shard_map/ppermute | solution.py:19

commit v3 on v2

--- a/solution.py
+++ b/solution.py
@@ -228,18 +228,19 @@
     )(own, mate, other, flat, conv_w)
 
 
-def grad_kernel(taps, kept, chans, masks, flat, table_ref, *refs):
-    cots, out_ref, line, acts = refs[: len(masks)], *refs[len(masks) :]
+def grad_kernel(taps, kept, chans, masks, flat, table, *refs):
+    blocks, out_ref, line, acts, cots = refs[: len(masks)], *refs[len(masks) :]
     count = sum(map(len, masks))
-    half = table_ref.shape[1]
-    span = cots[0].shape[0] // len(masks[0])
+    span = cots.shape[0] // count
+    per_row = table.shape[1] // span
     seq = lax.axis_index("seq")
-    per_row = half // span
-    top = round_up(4 * taps, 8)
     line[...] = jnp.full(line.shape, -1, jnp.int32)
     for b in range(count):
-        row, lane = top + b // per_row, b % per_row * span
-        line[:, LANES + b * span : LANES + (b + 1) * span] = table_ref[row : row + 1, lane : lane + span].astype(jnp.int32)
+        row, lane = b // per_row, b % per_row * span
+        line[:, LANES + b * span : LANES + (b + 1) * span] = table[row : row + 1, lane : lane + span].astype(jnp.int32)
+    for ref, own in zip(blocks, masks):
+        for i, mask in enumerate(own):
+            cots[pl.ds(pl.multiple_of((seq ^ mask) * span, LANES), span), :] = ref[i * span : (i + 1) * span, :]
     bases = line[...]
     width = bases.shape[1]
     full = flat.shape[1]
@@ -251,24 +252,15 @@
         stem = dot(own_w, hot, ((0,), (0,))).astype(jnp.bfloat16).astype(jnp.float32)
         value, _ = gelu_value(stem)
         values.append(jnp.where(bases >= 0, value, 0.0).astype(jnp.bfloat16).astype(jnp.float32))
-    order = [m for own in masks for m in own]
     for k in range(taps):
         move = (reach - k) % width
         back = (k - reach) % width
         ahead = pltpu.roll(values[0], move, 1) if move else values[0]
         behind = pltpu.roll(values[1], back, 1) if back else values[1]
-        both = (ahead + behind).astype(jnp.bfloat16)
-        for b in range(count):
-            mask = seq ^ b
-            slot = (mask & 3) * (count // 4) + lax.rem(count // 4 - (mask >> 2), count // 4)
-            acts[k * chans : (k + 1) * chans, pl.ds(pl.multiple_of(slot * span, LANES), span)] = both[:, LANES + b * span : LANES + (b + 1) * span]
-    total = jnp.zeros((taps * chans, half), jnp.float32)
-    at = 0
-    for ref in cots:
-        total += dot(acts[:, at : at + ref.shape[0]], ref[...])
-        at += ref.shape[0]
-    for k in range(taps):
-        out_ref[k] = 0.5 * total[k * chans : k * chans + kept]
+        acts[k * chans : (k + 1) * chans, :] = (ahead + behind)[:, LANES : LANES + count * span].astype(jnp.bfloat16)
+    total = 0.5 * dot(acts[...], cots[...])
+    for k in range(taps):
+        out_ref[k] = total[k * chans : k * chans + kept]
 
 
 def grad_part(flat, table, arrays, masks, span, taps):
@@ -285,9 +277,10 @@
         scratch_shapes=[
             pltpu.VMEM((1, count * span + 2 * LANES), jnp.int32),
             pltpu.VMEM((taps * chans, count * span), jnp.bfloat16),
+            pltpu.VMEM((count * span, half), jnp.bfloat16),
         ],
         compiler_params=pltpu.CompilerParams(vmem_limit_bytes=LIMIT),
-        cost_estimate=pl.CostEstimate(flops=2 * 10**9, bytes_accessed=0, transcendentals=0),
+        cost_estimate=pl.CostEstimate(flops=25 * 10**8, bytes_accessed=0, transcendentals=0),
         name="grad_part",
     )(flat, table, *arrays)
 
@@ -303,16 +296,16 @@
     far = range(count - 4, 0, -4)
 
     bases = tokens.reshape(1, span)
-    flat = flat_part(stem_weight)
-    mate = swap(after(bases, flat), 1)
-    cot = after(cotangent, flat)
-    far_cot = [swap(cot, m) for m in far]
+    far_cot = [swap(cotangent, m) for m in far]
     other = swap_next_chip(bases)
-    dacts = back_part(cot, conv_weight)
+    mate = swap(after(bases, other), 1)
+    flat = flat_part(after(stem_weight, other))
+    dacts = back_part(after(cotangent, flat), conv_weight)
     keep, send = stem_part(dacts, bases, mate, other, flat, taps, half)
     got = swap_chan(send)
-    total = jnp.concatenate([keep[: got.shape[0]] + got, keep[got.shape[0] :]])
-    total, *far_cot = lax.optimization_barrier((total, *far_cot))
+    top = got.shape[0]
+    total = jnp.concatenate([keep[:top] + got, keep[top:]])
+    total = total + swap(total, 2)
     here = jnp.concatenate([cotangent, *far_cot])
     there = swap(here, 2)
     here_mate = swap(here, 1)
@@ -321,13 +314,12 @@
         total = total + swap(total, 1 << bit)
     total, here_mate, there, blended = lax.optimization_barrier((total, here_mate, there, blended))
     there_mate = swap(there, 1)
-    total = total + swap(total, 2)
-    total, there_mate = lax.optimization_barrier((total, there_mate))
+    total, table = total[:top], total[top:]
     masks = [0, *far]
     masks = [[m + i for m in masks] for i in range(4)]
-    grad_conv = grad_part(flat, total, [here, here_mate, there, there_mate], masks, span, taps)
-    total = total[: 4 * taps] + swap(total[: 4 * taps], 1)
-    return blended, grad_conv, total.reshape(taps, 4, half)
+    grad_conv = grad_part(flat, table, [here, here_mate, there, there_mate], masks, span, taps)
+    total = after(total, grad_conv) + swap(total, 1)
+    return blended, grad_conv, total[: 4 * taps].reshape(taps, 4, half)
 
 
 def solution(mesh):

time: 38.6 us -> 35.8 us (0.927)
  starting transfers between devices: 21.4 us -> 17.4 us
  waiting for transfers between devices: 6.84 us -> 8.55 us
  Pallas kernels: 8.62 us -> 8.02 us
    ppermute x11, starting transfers between devices: 19.1 us -> 15.1 us  [swap(): return lax.ppermute(value, 'seq', [(i, i ^ mask) for i in range(count)])]
    ppermute x11, waiting for transfers between devices: 4.42 us -> 6.13 us  [swap(): return lax.ppermute(value, 'seq', [(i, i ^ mask) for i in range(count)])]
    pallas_call x1, Pallas kernels: 2.7 us -> 2.25 us  [grad_part(): pl.pallas_call(functools.partial(grad_kernel, taps, kept, chans, masks),...]
  transfers between devices with their start and end apart: 13 -> 13, of which waited for: 3 -> 5; matrix products, arithmetic and copies ran while one was open for 0% -> 0% of each run, Pallas kernels for 18% -> 23%
where the time goes in v3:
time: 35.8 us; the launch traced here: 35.6 us
  starting transfers between devices  17.4 us (49%)
  waiting for transfers between devices  8.55 us (24%)
  Pallas kernels  8.02 us (22%)
  between operations  0.83 us (2%)
  local copies, waits for them, and re-layouts  0.72 us (2%)
    ppermute x11, starting transfers between devices, swap(): return lax.ppermute(value, 'seq', [(i, i ^ mask) for i in range(count)])  15.1 us
    ppermute x11, waiting for transfers between devices, swap(): return lax.ppermute(value, 'seq', [(i, i ^ mask) for i in range(count)])  6.13 us
    ppermute x1, waiting for transfers between devices, swap_chan(): return lax.ppermute(value, 'chan', [(i, i ^ 1) for i in range(count)])  2.42 us
    pallas_call x1, Pallas kernels, grad_part(): pl.pallas_call(functools.partial(grad_kernel, taps, kept, chans, masks),...  2.25 us
    pallas_call x1, Pallas kernels, blend_part(): pl.pallas_call(blend_kernel, out_shape=jax.ShapeDtypeStruct((span, half),...  2.07 us
    ppermute x1, starting transfers between devices, swap_chan(): return lax.ppermute(value, 'chan', [(i, i ^ 1) for i in range(count)])  1.58 us
    pallas_call x1, Pallas kernels, flat_part(): pl.pallas_call(flat_kernel, out_shape=jax.ShapeDtypeStruct((32, stem_w.sh...  1.41 us
    pallas_call x1, Pallas kernels, stem_part(): pl.pallas_call(functools.partial(stem_kernel, taps), out_shape=tuple((jax...  1.27 us
  transfers between devices with their start and end apart: 13, of which 5 were waited for; matrix products, arithmetic and copies ran while one was open for 0% of the time, Pallas kernels for 23%

profile of v3, /device:TPU:0, one launch (start us, length us, event | category | flops | bytes accessed | tf_op | source)
XLA Modules:
  0.0 35.6 jit_solution(15669334033309971894)
XLA Ops:
  0.6 0.0 copy-start.2
  0.6 0.0 copy-start.1
  0.7 0.0 copy-start.3
  0.7 0.8 %collective-permute-start = (s32[1,128]{1,0:T(1,128)}, s32[1,128]{1,0:T(1,128)S(1)}, u32[]{:S(2)}, u32[]{:S(2)}) collective-permute-start(s32[1,128]{1,0:T(1,128)} %bitcast.1), channel_id=1, source_target_pairs={{2,4},{6,8},{10,12},{14,16},{18,20},{22,24},{26,28},{4,2},{8,6},{1... | collective-permute-start | bytes 1544 | tf_op jit(solution)/shard_map/ppermute | solution.py:30
  1.5 7.3 %collective-permute-start.6 = (bf16[128,384]{1,0:T(8,128)(2,1)}, bf16[128,384]{1,0:T(8,128)(2,1)S(1)}, u32[]{:S(2)}, u32[]{:S(2)}) collective-permute-start(bf16[128,384]{1,0:T(8,128)(2,1)} %cot_ref), channel_id=1, source_target_pairs={{0,24},{2,26},{4,28},{6,30},{8,16},{10,18},{12,20},{14,22},{16,8},... | collective-permute-start | bytes 294920 | tf_op jit(solution)/shard_map/ppermute | solution.py:19
  8.8 0.0 collective-permute-start.7
  8.8 0.6 %collective-permute-start.8 = (bf16[128,384]{1,0:T(8,128)(2,1)}, bf16[128,384]{1,0:T(8,128)(2,1)S(1)}, u32[]{:S(2)}, u32[]{:S(2)}) collective-permute-start(bf16[128,384]{1,0:T(8,128)(2,1)} %cot_ref), channel_id=1, source_target_pairs={{0,8},{2,10},{4,12},{6,14},{8,0},{10,2},{12,4},{14,6},{16,24},{18,... | collective-permute-start | bytes 294920 | tf_op jit(solution)/shard_map/ppermute | solution.py:19
  9.4 0.0 collective-permute-done.other_ref
  9.4 1.4 %flat_part.1.flat = f32[32,768]{1,0:T(8,128)} custom-call(bf16[5,4,768]{2,1,0:T(4,128)(2,1)} %stem_w_hbm), custom_call_target="tpu_custom_call" | custom-call | flops 6000000000 | tf_op jit(solution)/shard_map/flat_part/pallas_call | solution.py:78
  10.8 0.0 copy-done.2
  10.8 0.0 copy-start
  10.9 0.3 collective-permute-start.1
  11.2 0.0 copy-done.1
  11.2 0.0 copy-done.3
  11.2 1.0 %back_part.1 = (f32[144,768]{1,0:T(8,128)S(1)}, f32[144,768]{1,0:T(8,128)S(1)}) custom-call(bf16[128,384]{1,0:T(8,128)(2,1)S(1)} %copy-done.1, bf16[5,768,384]{2,1,0:T(8,128)(2,1)S(1)} %copy-done.3), custom_call_target="tpu_custom_call" | custom-call | flops 1400000000 | tf_op jit(solution)/shard_map/back_part/pallas_call | solution.py:126
  12.2 0.0 collective-permute-done.1.mate_ref
  12.2 0.0 copy-done
  12.2 1.3 %stem_part.1 = (f32[32,384]{1,0:T(8,128)S(1)}, f32[24,384]{1,0:T(8,128)S(1)}) custom-call(f32[144,768]{1,0:T(8,128)S(1)} %get-tuple-element.17.dact_f, f32[144,768]{1,0:T(8,128)S(1)} %get-tuple-element.18.dact_r, s32[1,128]{1,0:T(1,128)S(1)} %bitcast.3, s32[1,128]{1,0:T(1,128)S(1)} %collective-permute-done.1.mate_ref, ...), custom_call_target="tpu_custom_call" | custom-call | tf_op jit(solution)/shard_map/stem_part/pallas_call | solution.py:176
  13.5 1.6 %collective-permute-start.2 = (f32[24,384]{1,0:T(8,128)S(1)}, f32[24,384]{1,0:T(8,128)S(1)}, u32[]{:S(2)}, u32[]{:S(2)}) collective-permute-start(f32[24,384]{1,0:T(8,128)S(1)} %get-tuple-element.21), channel_id=1, source_target_pairs={{0,1},{1,0},{2,3},{3,2},{4,5},{5,4},{6,7},{7,6},{8,9},{9,8},{10,11... | collective-permute-start | bytes 110600 | tf_op jit(solution)/shard_map/ppermute | solution.py:24
  15.1 2.4 %collective-permute-done.2 = f32[24,384]{1,0:T(8,128)S(1)} collective-permute-done((f32[24,384]{1,0:T(8,128)S(1)}, f32[24,384]{1,0:T(8,128)S(1)}, u32[]{:S(2)}, u32[]{:S(2)}) %collective-permute-start.2) | collective-permute-done | bytes 36896 | tf_op jit(solution)/shard_map/ppermute | solution.py:24
  17.5 1.5 %collective-permute-start.3 = (f32[32,384]{1,0:T(8,128)S(1)}, f32[32,384]{1,0:T(8,128)S(1)}, u32[]{:S(2)}, u32[]{:S(2)}) collective-permute-start(f32[32,384]{1,0:T(8,128)S(1)} %pad_maximum_fusion), channel_id=1, source_target_pairs={{0,4},{2,6},{4,0},{6,2},{8,12},{10,14},{12,8},{14,10},{16,20},{18,... | collective-permute-start | bytes 147464 | tf_op jit(solution)/shard_map/ppermute | solution.py:19
  19.0 0.0 collective-permute-done.6
  19.0 0.0 collective-permute-done.7
  19.1 0.0 collective-permute-done.8
  19.1 0.1 collective-permute-start.9
  19.2 0.7 %collective-permute-start.10 = (bf16[512,384]{1,0:T(8,128)(2,1)S(1)}, bf16[512,384]{1,0:T(8,128)(2,1)S(1)}, u32[]{:S(2)}, u32[]{:S(2)}) collective-permute-start(bf16[512,384]{1,0:T(8,128)(2,1)S(1)} %constant_dynamic-update-slice_fusion.refs_0_), channel_id=1, source_target_pairs={{0,4},{2,6},{4,0},{6,2},{8,12},{10,14},{12,8},{14,10},{16,20},{18,... | collective-permute-start | bytes 1179656 | tf_op jit(solution)/shard_map/ppermute | solution.py:19
  19.9 1.8 %collective-permute-done.3 = f32[32,384]{1,0:T(8,128)S(1)} collective-permute-done((f32[32,384]{1,0:T(8,128)S(1)}, f32[32,384]{1,0:T(8,128)S(1)}, u32[]{:S(2)}, u32[]{:S(2)}) %collective-permute-start.3) | collective-permute-done | bytes 49184 | tf_op jit(solution)/shard_map/ppermute | solution.py:19
  21.7 1.6 %collective-permute-start.4 = (f32[32,384]{1,0:T(8,128)S(1)}, f32[32,384]{1,0:T(8,128)S(1)}, u32[]{:S(2)}, u32[]{:S(2)}) collective-permute-start(f32[32,384]{1,0:T(8,128)S(1)} %fusion), channel_id=1, source_target_pairs={{0,8},{2,10},{4,12},{6,14},{8,0},{10,2},{12,4},{14,6},{16,24},{18,... | collective-permute-start | bytes 147464 | tf_op jit(solution)/shard_map/ppermute | solution.py:19
  23.3 2.5 %collective-permute-done.4 = f32[32,384]{1,0:T(8,128)S(1)} collective-permute-done((f32[32,384]{1,0:T(8,128)S(1)}, f32[32,384]{1,0:T(8,128)S(1)}, u32[]{:S(2)}, u32[]{:S(2)}) %collective-permute-start.4) | collective-permute-done | bytes 49184 | tf_op jit(solution)/shard_map/ppermute | solution.py:19
  25.8 2.4 %collective-permute-start.5 = (f32[32,384]{1,0:T(8,128)S(1)}, f32[32,384]{1,0:T(8,128)S(1)}, u32[]{:S(2)}, u32[]{:S(2)}) collective-permute-start(f32[32,384]{1,0:T(8,128)S(1)} %add.17), channel_id=1, source_target_pairs={{0,16},{2,18},{4,20},{6,22},{8,24},{10,26},{12,28},{14,30},{16,0},... | collective-permute-start | bytes 147464 | tf_op jit(solution)/shard_map/ppermute | solution.py:19
  28.3 2.1 %blend_part.1 = bf16[128,384]{1,0:T(8,128)(2,1)} custom-call(s32[1,128]{1,0:T(1,128)S(1)} %bitcast.4, s32[1,128]{1,0:T(1,128)S(1)} %collective-permute-done.1.mate_ref, s32[1,128]{1,0:T(1,128)S(1)} %collective-permute-done.other_ref, f32[32,768]{1,0:T(8,128)S(1)} %copy-done, bf16[5,768,384]{2,1,0:T(8,128)(2,1)S(1)} %copy-done.3), custom_call_target="tpu_custom_call" | custom-call | flops 2000000000 | tf_op jit(solution)/shard_map/blend_part/pallas_call | solution.py:219
  30.3 0.6 %collective-permute-done.5 = f32[32,384]{1,0:T(8,128)S(1)} collective-permute-done((f32[32,384]{1,0:T(8,128)S(1)}, f32[32,384]{1,0:T(8,128)S(1)}, u32[]{:S(2)}, u32[]{:S(2)}) %collective-permute-start.5) | collective-permute-done | bytes 49184 | tf_op jit(solution)/shard_map/ppermute | solution.py:19
  30.9 0.0 collective-permute-done.9.refs_1_
  30.9 0.0 collective-permute-done.10.refs_2_
  30.9 0.1 collective-permute-start.11
  31.0 0.5 %collective-permute-start.12 = (f32[24,384]{1,0:T(8,128)S(1)}, f32[24,384]{1,0:T(8,128)S(1)}, u32[]{:S(2)}, u32[]{:S(2)}) collective-permute-start(f32[24,384]{1,0:T(8,128)S(1)} %slice.18), channel_id=1, source_target_pairs={{0,2},{2,0},{4,6},{6,4},{8,10},{10,8},{12,14},{14,12},{16,18},{18,... | collective-permute-start | bytes 110600 | tf_op jit(solution)/shard_map/ppermute | solution.py:19
  31.5 1.2 %collective-permute-done.11.refs_3_ = bf16[512,384]{1,0:T(8,128)(2,1)S(1)} collective-permute-done((bf16[512,384]{1,0:T(8,128)(2,1)S(1)}, bf16[512,384]{1,0:T(8,128)(2,1)S(1)}, u32[]{:S(2)}, u32[]{:S(2)}) %collective-permute-start.11) | collective-permute-done | bytes 393248 | tf_op jit(solution)/shard_map/ppermute | solution.py:19
  32.7 2.3 %grad_part.1 = f32[5,48,384]{2,1,0:T(8,128)} custom-call(f32[32,768]{1,0:T(8,128)S(1)} %copy-done, f32[8,384]{1,0:T(8,128)S(1)} %slice.17.table, bf16[512,384]{1,0:T(8,128)(2,1)S(1)} %constant_dynamic-update-slice_fusion.refs_0_, bf16[512,384]{1,0:T(8,128)(2,1)S(1)} %collective-permute-done.9.refs_1_, bf16[512,384]{1,0:T(8,128)(2,1)S(1)} %collective-permute-done.10.refs_2_, ...), custom_call_target="tpu_custom_call" | custom-call | flops 2500000000 | tf_op jit(solution)/shard_map/grad_part/pallas_call | solution.py:272
  35.0 0.0 collective-permute-done.12
  35.0 0.6 %reshape.13 = f32[5,4,384]{2,1,0:T(4,128)} reshape(f32[20,384]{1,0:T(8,128)S(1)} %slice_add_fusion) | data formatting | bytes 61440 | tf_op jit(solution)/shard_map/reshape | solution.py:322
  (13 shorter events, 0.1 us)
Async XLA Ops:
  0.6 10.2 %copy-start.2 = (s32[128]{0:T(128)S(1)}, s32[128]{0:T(128)}, u32[]{:S(2)}) copy-start(s32[128]{0:T(128)} %param.4) | copy-start | bytes 1540
  0.6 10.5 %copy-start.1 = (bf16[128,384]{1,0:T(8,128)(2,1)S(1)}, bf16[128,384]{1,0:T(8,128)(2,1)}, u32[]{:S(2)}) copy-start(bf16[128,384]{1,0:T(8,128)(2,1)} %cot_ref) | copy-start | bytes 294916
  0.7 10.5 %copy-start.3 = (bf16[5,768,384]{2,1,0:T(8,128)(2,1)S(1)}, bf16[5,768,384]{2,1,0:T(8,128)(2,1)}, u32[]{:S(2)}) copy-start(bf16[5,768,384]{2,1,0:T(8,128)(2,1)} %conv_w.3) | copy-start | bytes 8847364
  0.7 8.8 %collective-permute-start = (s32[1,128]{1,0:T(1,128)}, s32[1,128]{1,0:T(1,128)S(1)}, u32[]{:S(2)}, u32[]{:S(2)}) collective-permute-start(s32[1,128]{1,0:T(1,128)} %bitcast.1), channel_id=1, source_target_pairs={{2,4},{6,8},{10,12},{14,16},{18,20},{22,24},{26,28},{4,2},{8,6},{1... | collective-permute-start | bytes 1544 | tf_op jit(solution)/shard_map/ppermute | solution.py:30
  1.5 17.5 %collective-permute-start.6 = (bf16[128,384]{1,0:T(8,128)(2,1)}, bf16[128,384]{1,0:T(8,128)(2,1)S(1)}, u32[]{:S(2)}, u32[]{:S(2)}) collective-permute-start(bf16[128,384]{1,0:T(8,128)(2,1)} %cot_ref), channel_id=1, source_target_pairs={{0,24},{2,26},{4,28},{6,30},{8,16},{10,18},{12,20},{14,22},{16,8},... | collective-permute-start | bytes 294920 | tf_op jit(solution)/shard_map/ppermute | solution.py:19
  8.8 10.2 %collective-permute-start.7 = (bf16[128,384]{1,0:T(8,128)(2,1)}, bf16[128,384]{1,0:T(8,128)(2,1)S(1)}, u32[]{:S(2)}, u32[]{:S(2)}) collective-permute-start(bf16[128,384]{1,0:T(8,128)(2,1)} %cot_ref), channel_id=1, source_target_pairs={{0,16},{2,18},{4,20},{6,22},{8,24},{10,26},{12,28},{14,30},{16,0},... | collective-permute-start | bytes 294920 | tf_op jit(solution)/shard_map/ppermute | solution.py:19
  8.8 10.3 %collective-permute-start.8 = (bf16[128,384]{1,0:T(8,128)(2,1)}, bf16[128,384]{1,0:T(8,128)(2,1)S(1)}, u32[]{:S(2)}, u32[]{:S(2)}) collective-permute-start(bf16[128,384]{1,0:T(8,128)(2,1)} %cot_ref), channel_id=1, source_target_pairs={{0,8},{2,10},{4,12},{6,14},{8,0},{10,2},{12,4},{14,6},{16,24},{18,... | collective-permute-start | bytes 294920 | tf_op jit(solution)/shard_map/ppermute | solution.py:19
  10.8 1.4 %copy-start = (f32[32,768]{1,0:T(8,128)S(1)}, f32[32,768]{1,0:T(8,128)}, u32[]{:S(2)}) copy-start(f32[32,768]{1,0:T(8,128)} %flat_part.1.flat) | copy-start | bytes 294916
  10.9 1.3 %collective-permute-start.1 = (s32[1,128]{1,0:T(1,128)S(1)}, s32[1,128]{1,0:T(1,128)S(1)}, u32[]{:S(2)}, u32[]{:S(2)}) collective-permute-start(s32[1,128]{1,0:T(1,128)S(1)} %bitcast.2), channel_id=1, source_target_pairs={{0,2},{2,0},{4,6},{6,4},{8,10},{10,8},{12,14},{14,12},{16,18},{18,... | collective-permute-start | bytes 1544 | tf_op jit(solution)/shard_map/ppermute | solution.py:19
  13.5 4.0 %collective-permute-start.2 = (f32[24,384]{1,0:T(8,128)S(1)}, f32[24,384]{1,0:T(8,128)S(1)}, u32[]{:S(2)}, u32[]{:S(2)}) collective-permute-start(f32[24,384]{1,0:T(8,128)S(1)} %get-tuple-element.21), channel_id=1, source_target_pairs={{0,1},{1,0},{2,3},{3,2},{4,5},{5,4},{6,7},{7,6},{8,9},{9,8},{10,11... | collective-permute-start | bytes 110600 | tf_op jit(solution)/shard_map/ppermute | solution.py:24
  17.5 4.2 %collective-permute-start.3 = (f32[32,384]{1,0:T(8,128)S(1)}, f32[32,384]{1,0:T(8,128)S(1)}, u32[]{:S(2)}, u32[]{:S(2)}) collective-permute-start(f32[32,384]{1,0:T(8,128)S(1)} %pad_maximum_fusion), channel_id=1, source_target_pairs={{0,4},{2,6},{4,0},{6,2},{8,12},{10,14},{12,8},{14,10},{16,20},{18,... | collective-permute-start | bytes 147464 | tf_op jit(solution)/shard_map/ppermute | solution.py:19
  19.1 11.8 %collective-permute-start.9 = (bf16[512,384]{1,0:T(8,128)(2,1)S(1)}, bf16[512,384]{1,0:T(8,128)(2,1)S(1)}, u32[]{:S(2)}, u32[]{:S(2)}) collective-permute-start(bf16[512,384]{1,0:T(8,128)(2,1)S(1)} %constant_dynamic-update-slice_fusion.refs_0_), channel_id=1, source_target_pairs={{0,2},{2,0},{4,6},{6,4},{8,10},{10,8},{12,14},{14,12},{16,18},{18,... | collective-permute-start | bytes 1179656 | tf_op jit(solution)/shard_map/ppermute | solution.py:19
  19.2 11.8 %collective-permute-start.10 = (bf16[512,384]{1,0:T(8,128)(2,1)S(1)}, bf16[512,384]{1,0:T(8,128)(2,1)S(1)}, u32[]{:S(2)}, u32[]{:S(2)}) collective-permute-start(bf16[512,384]{1,0:T(8,128)(2,1)S(1)} %constant_dynamic-update-slice_fusion.refs_0_), channel_id=1, source_target_pairs={{0,4},{2,6},{4,0},{6,2},{8,12},{10,14},{12,8},{14,10},{16,20},{18,... | collective-permute-start | bytes 1179656 | tf_op jit(solution)/shard_map/ppermute | solution.py:19
  21.7 4.1 %collective-permute-start.4 = (f32[32,384]{1,0:T(8,128)S(1)}, f32[32,384]{1,0:T(8,128)S(1)}, u32[]{:S(2)}, u32[]{:S(2)}) collective-permute-start(f32[32,384]{1,0:T(8,128)S(1)} %fusion), channel_id=1, source_target_pairs={{0,8},{2,10},{4,12},{6,14},{8,0},{10,2},{12,4},{14,6},{16,24},{18,... | collective-permute-start | bytes 147464 | tf_op jit(solution)/shard_map/ppermute | solution.py:19
  25.8 5.1 %collective-permute-start.5 = (f32[32,384]{1,0:T(8,128)S(1)}, f32[32,384]{1,0:T(8,128)S(1)}, u32[]{:S(2)}, u32[]{:S(2)}) collective-permute-start(f32[32,384]{1,0:T(8,128)S(1)} %add.17), channel_id=1, source_target_pairs={{0,16},{2,18},{4,20},{6,22},{8,24},{10,26},{12,28},{14,30},{16,0},... | collective-permute-start | bytes 147464 | tf_op jit(solution)/shard_map/ppermute | solution.py:19
  30.9 1.8 %collective-permute-start.11 = (bf16[512,384]{1,0:T(8,128)(2,1)S(1)}, bf16[512,384]{1,0:T(8,128)(2,1)S(1)}, u32[]{:S(2)}, u32[]{:S(2)}) collective-permute-start(bf16[512,384]{1,0:T(8,128)(2,1)S(1)} %collective-permute-done.10.refs_2_), channel_id=1, source_target_pairs={{0,2},{2,0},{4,6},{6,4},{8,10},{10,8},{12,14},{14,12},{16,18},{18,... | collective-permute-start | bytes 1179656 | tf_op jit(solution)/shard_map/ppermute | solution.py:19
  31.0 3.9 %collective-permute-start.12 = (f32[24,384]{1,0:T(8,128)S(1)}, f32[24,384]{1,0:T(8,128)S(1)}, u32[]{:S(2)}, u32[]{:S(2)}) collective-permute-start(f32[24,384]{1,0:T(8,128)S(1)} %slice.18), channel_id=1, source_target_pairs={{0,2},{2,0},{4,6},{6,4},{8,10},{10,8},{12,14},{14,12},{16,18},{18,... | collective-permute-start | bytes 110600 | tf_op jit(solution)/shard_map/ppermute | solution.py:19

commit v4 on v3

--- a/solution.py
+++ b/solution.py
@@ -65,25 +65,18 @@
     return lax.dot_general(left, right, (dims, ((), ())), preferred_element_type=jnp.float32)
 
 
-def flat_kernel(stem_w_hbm, out_ref, stem_w_ref, sem):
-    copy = pltpu.make_async_copy(stem_w_hbm, stem_w_ref, sem)
-    copy.start()
+def mark_kernel(out_ref):
     out_ref[...] = jnp.zeros_like(out_ref)
-    copy.wait()
-    for k in range(stem_w_ref.shape[0]):
-        out_ref[4 * k : 4 * k + 4, :] = stem_w_ref[k].astype(jnp.float32)
-
-
-def flat_part(stem_w):
-    return pl.pallas_call(
-        flat_kernel,
-        out_shape=jax.ShapeDtypeStruct((32, stem_w.shape[2]), jnp.float32),
-        in_specs=[pl.BlockSpec(memory_space=pl.ANY)],
+
+
+def mark_part():
+    return pl.pallas_call(
+        mark_kernel,
+        out_shape=jax.ShapeDtypeStruct((8, LANES), jnp.float32),
         out_specs=VMEM,
-        scratch_shapes=[pltpu.VMEM(stem_w.shape, stem_w.dtype), pltpu.SemaphoreType.DMA(())],
         cost_estimate=pl.CostEstimate(flops=6 * 10**9, bytes_accessed=0, transcendentals=0),
-        name="flat_part",
-    )(stem_w)
+        name="mark_part",
+    )()
 
 
 def line_of(own_ref, mate_ref, other_ref, line):
@@ -108,8 +101,11 @@
     return ref[rows, pl.ds(pl.multiple_of(chan * half, LANES), half)]
 
 
-def back_kernel(cot_ref, conv_w, dact_f, dact_r):
+def back_kernel(cot_ref, conv_w, stem_w_ref, dact_f, dact_r, flat_ref):
     taps = conv_w.shape[0]
+    flat_ref[...] = jnp.zeros_like(flat_ref)
+    for k in range(taps):
+        flat_ref[4 * k : 4 * k + 4, :] = stem_w_ref[k].astype(jnp.float32)
     span = cot_ref.shape[0]
     dact_f[...] = jnp.zeros_like(dact_f)
     dact_r[...] = jnp.zeros_like(dact_r)
@@ -120,18 +116,18 @@
         dact_r[taps - 1 - k : taps - 1 - k + span] += part
 
 
-def back_part(cot, conv_w):
+def back_part(cot, conv_w, stem_w):
     taps, full, _ = conv_w.shape
     rows = round_up(cot.shape[0] + taps - 1, 16)
     return pl.pallas_call(
         back_kernel,
-        out_shape=tuple(jax.ShapeDtypeStruct((rows, full), jnp.float32) for _ in range(2)),
-        in_specs=[VMEM] * 2,
-        out_specs=(VMEM, VMEM),
+        out_shape=tuple(jax.ShapeDtypeStruct((r, full), jnp.float32) for r in (rows, rows, 32)),
+        in_specs=[VMEM] * 3,
+        out_specs=(VMEM, VMEM, VMEM),
         compiler_params=pltpu.CompilerParams(vmem_limit_bytes=LIMIT),
         cost_estimate=pl.CostEstimate(flops=14 * 10**8, bytes_accessed=0, transcendentals=0),
         name="back_part",
-    )(cot, conv_w)
+    )(cot, conv_w, stem_w)
 
 
 def stem_kernel(taps, dact_f, dact_r, own_ref, mate_ref, other_ref, flat, keep_ref, send_ref, line, grad):
@@ -185,7 +181,7 @@
     )(*dacts, own, mate, other, flat)
 
 
-def blend_kernel(own_ref, mate_ref, other_ref, flat, conv_w, blended_ref, line, act_f, act_r, stem_own):
+def blend_kernel(mark_ref, own_ref, mate_ref, other_ref, flat, conv_w, blended_ref, line, act_f, act_r, stem_own):
     taps = conv_w.shape[0]
     span, half = blended_ref.shape
     rows = act_f.shape[0]
@@ -212,35 +208,45 @@
     blended_ref[...] = (0.5 * total).astype(jnp.bfloat16)
 
 
-def blend_part(own, mate, other, flat, conv_w):
+def blend_part(mark, own, mate, other, flat, conv_w):
     taps, full, half = conv_w.shape
     span = own.shape[1]
     rows = round_up(span + taps - 1, 16)
     return pl.pallas_call(
         blend_kernel,
         out_shape=jax.ShapeDtypeStruct((span, half), jnp.bfloat16),
-        in_specs=[VMEM] * 5,
+        in_specs=[pl.BlockSpec(memory_space=pl.ANY)] + [VMEM] * 5,
         out_specs=VMEM,
         scratch_shapes=[pltpu.VMEM((1, 3 * span), jnp.int32)] + [pltpu.VMEM((rows, full), jnp.float32) for _ in range(3)],
         compiler_params=pltpu.CompilerParams(vmem_limit_bytes=LIMIT),
         cost_estimate=pl.CostEstimate(flops=2 * 10**9, bytes_accessed=0, transcendentals=0),
         name="blend_part",
-    )(own, mate, other, flat, conv_w)
-
-
-def grad_kernel(taps, kept, chans, masks, flat, table, *refs):
-    blocks, out_ref, line, acts, cots = refs[: len(masks)], *refs[len(masks) :]
-    count = sum(map(len, masks))
-    span = cots.shape[0] // count
+    )(mark, own, mate, other, flat, conv_w)
+
+
+def pair_dots(acts_ref, own_ref, mate_ref, masks, cots):
+    span = own_ref.shape[0] // len(masks)
+    seq = lax.axis_index("seq")
+    total = jnp.zeros((acts_ref.shape[0], own_ref.shape[1]), jnp.float32)
+    for i, mask in enumerate(masks):
+        block = seq ^ mask
+        rows = slice(i * span, (i + 1) * span)
+        for ref, side in ((own_ref, block & 1), (mate_ref, 1 - (block & 1))):
+            cots[pl.ds(pl.multiple_of((2 * i + side) * span, LANES), span), :] = ref[rows, :]
+        at = pl.multiple_of((block >> 1) * (2 * span), 2 * LANES)
+        total += dot(acts_ref[:, pl.ds(at, 2 * span)], cots[2 * i * span : 2 * (i + 1) * span, :])
+    return total
+
+
+def acts_kernel(taps, chans, masks, flat, table, here_ref, mate_ref, acts_ref, total_ref, line, cots):
+    span = here_ref.shape[0] // len(masks)
+    count = 4 * len(masks)
     per_row = table.shape[1] // span
     seq = lax.axis_index("seq")
     line[...] = jnp.full(line.shape, -1, jnp.int32)
     for b in range(count):
         row, lane = b // per_row, b % per_row * span
         line[:, LANES + b * span : LANES + (b + 1) * span] = table[row : row + 1, lane : lane + span].astype(jnp.int32)
-    for ref, own in zip(blocks, masks):
-        for i, mask in enumerate(own):
-            cots[pl.ds(pl.multiple_of((seq ^ mask) * span, LANES), span), :] = ref[i * span : (i + 1) * span, :]
     bases = line[...]
     width = bases.shape[1]
     full = flat.shape[1]
@@ -257,32 +263,58 @@
         back = (k - reach) % width
         ahead = pltpu.roll(values[0], move, 1) if move else values[0]
         behind = pltpu.roll(values[1], back, 1) if back else values[1]
-        acts[k * chans : (k + 1) * chans, :] = (ahead + behind)[:, LANES : LANES + count * span].astype(jnp.bfloat16)
-    total = 0.5 * dot(acts[...], cots[...])
-    for k in range(taps):
-        out_ref[k] = total[k * chans : k * chans + kept]
-
-
-def grad_part(flat, table, arrays, masks, span, taps):
-    full = flat.shape[1]
-    half = arrays[0].shape[1]
-    count = sum(map(len, masks))
-    kept = full // count
-    chans = round_up(kept, 16)
-    return pl.pallas_call(
-        functools.partial(grad_kernel, taps, kept, chans, masks),
-        out_shape=jax.ShapeDtypeStruct((taps, kept, half), jnp.float32),
-        in_specs=[VMEM] * (2 + len(arrays)),
-        out_specs=VMEM,
+        acts_ref[k * chans : (k + 1) * chans, :] = (ahead + behind)[:, LANES : LANES + count * span].astype(jnp.bfloat16)
+    total_ref[...] = pair_dots(acts_ref, here_ref, mate_ref, masks, cots)
+
+
+def acts_part(flat, table, here, mate, masks, span, taps):
+    full, half = flat.shape[1], here.shape[1]
+    count = 4 * len(masks)
+    chans = round_up(full // count, 16)
+    return pl.pallas_call(
+        functools.partial(acts_kernel, taps, chans, masks),
+        out_shape=(
+            jax.ShapeDtypeStruct((taps * chans, count * span), jnp.bfloat16),
+            jax.ShapeDtypeStruct((taps * chans, half), jnp.float32),
+        ),
+        in_specs=[VMEM] * 4,
+        out_specs=(VMEM, VMEM),
         scratch_shapes=[
             pltpu.VMEM((1, count * span + 2 * LANES), jnp.int32),
-            pltpu.VMEM((taps * chans, count * span), jnp.bfloat16),
-            pltpu.VMEM((count * span, half), jnp.bfloat16),
+            pltpu.VMEM((2 * here.shape[0], half), jnp.bfloat16),
         ],
         compiler_params=pltpu.CompilerParams(vmem_limit_bytes=LIMIT),
-        cost_estimate=pl.CostEstimate(flops=25 * 10**8, bytes_accessed=0, transcendentals=0),
+        cost_estimate=pl.CostEstimate(flops=2 * 10**9, bytes_accessed=0, transcendentals=0),
+        name="acts_part",
+    )(flat, table, here, mate)
+
+
+def grad_kernel(masks, acts_ref, there_ref, mate_ref, first_ref, stem_ref, got_ref, out_ref, stem_out, cots):
+    taps, kept, _ = out_ref.shape
+    stem = stem_ref[...] + got_ref[...]
+    for k in range(taps):
+        stem_out[k] = stem[4 * k : 4 * k + 4]
+    chans = acts_ref.shape[0] // taps
+    total = 0.5 * (first_ref[...] + pair_dots(acts_ref, there_ref, mate_ref, masks, cots))
+    for k in range(taps):
+        out_ref[k] = total[k * chans : k * chans + kept]
+
+
+def grad_part(acts, there, mate, first, stem, got, masks, taps, kept):
+    half = there.shape[1]
+    return pl.pallas_call(
+        functools.partial(grad_kernel, masks),
+        out_shape=(
+            jax.ShapeDtypeStruct((taps, kept, half), jnp.float32),
+            jax.ShapeDtypeStruct((taps, 4, half), jnp.float32),
+        ),
+        in_specs=[VMEM] * 6,
+        out_specs=(VMEM, VMEM),
+        scratch_shapes=[pltpu.VMEM((2 * there.shape[0], half), jnp.bfloat16)],
+        compiler_params=pltpu.CompilerParams(vmem_limit_bytes=LIMIT),
+        cost_estimate=pl.CostEstimate(flops=10**9, bytes_accessed=0, transcendentals=0),
         name="grad_part",
-    )(flat, table, *arrays)
+    )(acts, there, mate, first, stem, got)
 
 
 def after(value, *others):
@@ -295,12 +327,12 @@
     taps, full, half = conv_weight.shape
     far = range(count - 4, 0, -4)
 
-    bases = tokens.reshape(1, span)
+    mark = mark_part()
+    bases = after(tokens.reshape(1, span), mark)
+    other = swap_next_chip(bases)
     far_cot = [swap(cotangent, m) for m in far]
-    other = swap_next_chip(bases)
     mate = swap(after(bases, other), 1)
-    flat = flat_part(after(stem_weight, other))
-    dacts = back_part(after(cotangent, flat), conv_weight)
+    *dacts, flat = back_part(after(cotangent, other), conv_weight, stem_weight)
     keep, send = stem_part(dacts, bases, mate, other, flat, taps, half)
     got = swap_chan(send)
     top = got.shape[0]
@@ -309,17 +341,18 @@
     here = jnp.concatenate([cotangent, *far_cot])
     there = swap(here, 2)
     here_mate = swap(here, 1)
-    blended = blend_part(bases, mate, other, flat, conv_weight)
+    blended = blend_part(mark, bases, mate, other, flat, conv_weight)
     for bit in range(2, (count - 1).bit_length()):
         total = total + swap(total, 1 << bit)
     total, here_mate, there, blended = lax.optimization_barrier((total, here_mate, there, blended))
     there_mate = swap(there, 1)
     total, table = total[:top], total[top:]
     masks = [0, *far]
-    masks = [[m + i for m in masks] for i in range(4)]
-    grad_conv = grad_part(flat, table, [here, here_mate, there, there_mate], masks, span, taps)
-    total = after(total, grad_conv) + swap(total, 1)
-    return blended, grad_conv, total[: 4 * taps].reshape(taps, 4, half)
+    acts, first = acts_part(flat, table, here, here_mate, masks, span, taps)
+    grad_conv, grad_stem = grad_part(
+        acts, there, there_mate, first, total, swap(total, 1), [m + 2 for m in masks], taps, full // count
+    )
+    return blended, grad_conv, grad_stem
 
 
 def solution(mesh):

time: 35.8 us -> 33.6 us (0.939)
  waiting for transfers between devices: 8.55 us -> 6.89 us
  local copies, waits for them, and re-layouts: 0.72 us -> 0.11 us
  starting transfers between devices: 17.4 us -> 17.8 us
    ppermute x11, waiting for transfers between devices: 6.13 us -> 4.47 us  [swap(): return lax.ppermute(value, 'seq', [(i, i ^ mask) for i in range(count)])]
    reshape x1 -> x0, local copies, waits for them, and re-layouts: 0.62 us -> none  [on_device(): return (blended, grad_conv, total[:4 * taps].reshape(taps, 4, half))]
    pallas_call x3 -> x4, Pallas kernels: 4.68 us -> 4.51 us  [the longest x1 1.61 us: acts_part(): pl.pallas_call(functools.partial(acts_kernel, taps, chans, masks), out_sh...]
  transfers between devices with their start and end apart: 13 -> 13, of which waited for: 5 -> 4; matrix products, arithmetic and copies ran while one was open for 0% -> 0% of each run, Pallas kernels for 23% -> 18%
where the time goes in v4:
time: 33.6 us; the launch traced here: 33.5 us
  starting transfers between devices  17.8 us (53%)
  Pallas kernels  7.85 us (23%)
  waiting for transfers between devices  6.89 us (21%)
  between operations  0.82 us (2%)
    ppermute x11, starting transfers between devices, swap(): return lax.ppermute(value, 'seq', [(i, i ^ mask) for i in range(count)])  15.4 us
    ppermute x11, waiting for transfers between devices, swap(): return lax.ppermute(value, 'seq', [(i, i ^ mask) for i in range(count)])  4.47 us
    ppermute x1, waiting for transfers between devices, swap_chan(): return lax.ppermute(value, 'chan', [(i, i ^ 1) for i in range(count)])  2.41 us
    pallas_call x1, Pallas kernels, blend_part(): pl.pallas_call(blend_kernel, out_shape=jax.ShapeDtypeStruct((span, half),...  2.08 us
    pallas_call x1, Pallas kernels, acts_part(): pl.pallas_call(functools.partial(acts_kernel, taps, chans, masks), out_sh...  1.61 us
    ppermute x1, starting transfers between devices, swap_chan(): return lax.ppermute(value, 'chan', [(i, i ^ 1) for i in range(count)])  1.58 us
    pallas_call x1, Pallas kernels, grad_part(): pl.pallas_call(functools.partial(grad_kernel, masks), out_shape=(jax.Shap...  1.29 us
    pallas_call x1, Pallas kernels, stem_part(): pl.pallas_call(functools.partial(stem_kernel, taps), out_shape=tuple((jax...  1.27 us
  transfers between devices with their start and end apart: 13, of which 4 were waited for; matrix products, arithmetic and copies ran while one was open for 0% of the time, Pallas kernels for 18%

profile of v4, /device:TPU:0, one launch (start us, length us, event | category | flops | bytes accessed | tf_op | source)
XLA Modules:
  0.0 33.5 jit_solution(15118887778660899136)
XLA Ops:
  0.6 0.0 copy-start.1
  0.6 0.0 copy-start
  0.7 0.0 copy-start.3
  0.7 0.0 copy-start.2
  0.7 0.6 %mark_part.1.mark_ref = f32[8,128]{1,0:T(8,128)} custom-call(), custom_call_target="tpu_custom_call" | custom-call | flops 6000000000 | tf_op jit(solution)/shard_map/mark_part/pallas_call | solution.py:73
  1.3 0.0 copy-done.1
  1.3 0.0 copy-start.4
  1.3 0.8 %collective-permute-start = (s32[1,128]{1,0:T(1,128)S(1)}, s32[1,128]{1,0:T(1,128)S(1)}, u32[]{:S(2)}, u32[]{:S(2)}) collective-permute-start(s32[1,128]{1,0:T(1,128)S(1)} %bitcast.1), channel_id=1, source_target_pairs={{2,4},{6,8},{10,12},{14,16},{18,20},{22,24},{26,28},{4,2},{8,6},{1... | collective-permute-start | bytes 1544 | tf_op jit(solution)/shard_map/ppermute | solution.py:30
  2.1 0.0 copy-done
  2.1 7.2 %collective-permute-start.6 = (bf16[128,384]{1,0:T(8,128)(2,1)S(1)}, bf16[128,384]{1,0:T(8,128)(2,1)S(1)}, u32[]{:S(2)}, u32[]{:S(2)}) collective-permute-start(bf16[128,384]{1,0:T(8,128)(2,1)S(1)} %copy-done), channel_id=1, source_target_pairs={{0,24},{2,26},{4,28},{6,30},{8,16},{10,18},{12,20},{14,22},{16,8},... | collective-permute-start | bytes 294920 | tf_op jit(solution)/shard_map/ppermute | solution.py:19
  9.3 0.0 collective-permute-start.7
  9.3 0.6 %collective-permute-start.8 = (bf16[128,384]{1,0:T(8,128)(2,1)S(1)}, bf16[128,384]{1,0:T(8,128)(2,1)S(1)}, u32[]{:S(2)}, u32[]{:S(2)}) collective-permute-start(bf16[128,384]{1,0:T(8,128)(2,1)S(1)} %copy-done), channel_id=1, source_target_pairs={{0,8},{2,10},{4,12},{6,14},{8,0},{10,2},{12,4},{14,6},{16,24},{18,... | collective-permute-start | bytes 294920 | tf_op jit(solution)/shard_map/ppermute | solution.py:19
  9.9 0.0 collective-permute-done.other_ref
  9.9 0.2 collective-permute-start.1
  10.1 0.0 copy-done.3
  10.1 0.0 copy-done.2
  10.1 1.0 %back_part.1 = (f32[144,768]{1,0:T(8,128)S(1)}, f32[144,768]{1,0:T(8,128)S(1)}, f32[32,768]{1,0:T(8,128)S(1)}) custom-call(bf16[128,384]{1,0:T(8,128)(2,1)S(1)} %copy-done, bf16[5,768,384]{2,1,0:T(8,128)(2,1)S(1)} %copy-done.2, bf16[5,4,768]{2,1,0:T(4,128)(2,1)S(1)} %copy-done.3), custom_call_target="tpu_custom_call" | custom-call | flops 1400000000 | tf_op jit(solution)/shard_map/back_part/pallas_call | solution.py:122
  11.2 0.0 collective-permute-done.1.mate_ref
  11.2 1.3 %stem_part.1 = (f32[32,384]{1,0:T(8,128)S(1)}, f32[24,384]{1,0:T(8,128)S(1)}) custom-call(f32[144,768]{1,0:T(8,128)S(1)} %get-tuple-element.21.dact_f, f32[144,768]{1,0:T(8,128)S(1)} %get-tuple-element.22.dact_r, s32[1,128]{1,0:T(1,128)S(1)} %bitcast.3, s32[1,128]{1,0:T(1,128)S(1)} %collective-permute-done.1.mate_ref, ...), custom_call_target="tpu_custom_call" | custom-call | tf_op jit(solution)/shard_map/stem_part/pallas_call | solution.py:172
  12.5 1.6 %collective-permute-start.2 = (f32[24,384]{1,0:T(8,128)S(1)}, f32[24,384]{1,0:T(8,128)S(1)}, u32[]{:S(2)}, u32[]{:S(2)}) collective-permute-start(f32[24,384]{1,0:T(8,128)S(1)} %get-tuple-element.26), channel_id=1, source_target_pairs={{0,1},{1,0},{2,3},{3,2},{4,5},{5,4},{6,7},{7,6},{8,9},{9,8},{10,11... | collective-permute-start | bytes 110600 | tf_op jit(solution)/shard_map/ppermute | solution.py:24
  14.1 2.4 %collective-permute-done.2 = f32[24,384]{1,0:T(8,128)S(1)} collective-permute-done((f32[24,384]{1,0:T(8,128)S(1)}, f32[24,384]{1,0:T(8,128)S(1)}, u32[]{:S(2)}, u32[]{:S(2)}) %collective-permute-start.2) | collective-permute-done | bytes 36896 | tf_op jit(solution)/shard_map/ppermute | solution.py:24
  16.5 1.5 %collective-permute-start.3 = (f32[32,384]{1,0:T(8,128)S(1)}, f32[32,384]{1,0:T(8,128)S(1)}, u32[]{:S(2)}, u32[]{:S(2)}) collective-permute-start(f32[32,384]{1,0:T(8,128)S(1)} %pad_maximum_fusion), channel_id=1, source_target_pairs={{0,4},{2,6},{4,0},{6,2},{8,12},{10,14},{12,8},{14,10},{16,20},{18,... | collective-permute-start | bytes 147464 | tf_op jit(solution)/shard_map/ppermute | solution.py:19
  18.0 0.0 collective-permute-done.6
  18.0 0.5 %collective-permute-done.7 = bf16[128,384]{1,0:T(8,128)(2,1)S(1)} collective-permute-done((bf16[128,384]{1,0:T(8,128)(2,1)S(1)}, bf16[128,384]{1,0:T(8,128)(2,1)S(1)}, u32[]{:S(2)}, u32[]{:S(2)}) %collective-permute-start.7) | collective-permute-done | bytes 98336 | tf_op jit(solution)/shard_map/ppermute | solution.py:19
  18.5 0.0 collective-permute-done.8
  18.5 0.3 collective-permute-start.10
  18.8 0.2 collective-permute-start.9
  19.0 1.6 %collective-permute-done.3 = f32[32,384]{1,0:T(8,128)S(1)} collective-permute-done((f32[32,384]{1,0:T(8,128)S(1)}, f32[32,384]{1,0:T(8,128)S(1)}, u32[]{:S(2)}, u32[]{:S(2)}) %collective-permute-start.3) | collective-permute-done | bytes 49184 | tf_op jit(solution)/shard_map/ppermute | solution.py:19
  20.7 1.8 %collective-permute-start.4 = (f32[32,384]{1,0:T(8,128)S(1)}, f32[32,384]{1,0:T(8,128)S(1)}, u32[]{:S(2)}, u32[]{:S(2)}) collective-permute-start(f32[32,384]{1,0:T(8,128)S(1)} %fusion), channel_id=1, source_target_pairs={{0,8},{2,10},{4,12},{6,14},{8,0},{10,2},{12,4},{14,6},{16,24},{18,... | collective-permute-start | bytes 147464 | tf_op jit(solution)/shard_map/ppermute | solution.py:19
  22.5 2.3 %collective-permute-done.4 = f32[32,384]{1,0:T(8,128)S(1)} collective-permute-done((f32[32,384]{1,0:T(8,128)S(1)}, f32[32,384]{1,0:T(8,128)S(1)}, u32[]{:S(2)}, u32[]{:S(2)}) %collective-permute-start.4) | collective-permute-done | bytes 49184 | tf_op jit(solution)/shard_map/ppermute | solution.py:19
  24.8 3.0 %collective-permute-start.5 = (f32[32,384]{1,0:T(8,128)S(1)}, f32[32,384]{1,0:T(8,128)S(1)}, u32[]{:S(2)}, u32[]{:S(2)}) collective-permute-start(f32[32,384]{1,0:T(8,128)S(1)} %add.14), channel_id=1, source_target_pairs={{0,16},{2,18},{4,20},{6,22},{8,24},{10,26},{12,28},{14,30},{16,0},... | collective-permute-start | bytes 147464 | tf_op jit(solution)/shard_map/ppermute | solution.py:19
  27.9 0.0 copy-done.4
  27.9 2.1 %blend_part.1 = bf16[128,384]{1,0:T(8,128)(2,1)} custom-call(f32[8,128]{1,0:T(8,128)S(1)} %copy-done.4, s32[1,128]{1,0:T(1,128)S(1)} %bitcast.4, s32[1,128]{1,0:T(1,128)S(1)} %collective-permute-done.1.mate_ref, s32[1,128]{1,0:T(1,128)S(1)} %collective-permute-done.other_ref, f32[32,768]{1,0:T(8,128)S(1)} %get-tuple-element.24.flat, ...), custom_call_target="tpu_custom_call" | custom-call | flops 2000000000 | tf_op jit(solution)/shard_map/blend_part/pallas_call | solution.py:215
  29.9 0.0 collective-permute-done.5
  30.0 0.0 collective-permute-done.10.there_ref
  30.0 0.0 collective-permute-done.9.mate_ref
  30.0 0.1 collective-permute-start.11
  30.1 0.5 %collective-permute-start.12 = (f32[24,384]{1,0:T(8,128)S(1)}, f32[24,384]{1,0:T(8,128)S(1)}, u32[]{:S(2)}, u32[]{:S(2)}) collective-permute-start(f32[24,384]{1,0:T(8,128)S(1)} %slice.15.stem_ref), channel_id=1, source_target_pairs={{0,2},{2,0},{4,6},{6,4},{8,10},{10,8},{12,14},{14,12},{16,18},{18,... | collective-permute-start | bytes 110600 | tf_op jit(solution)/shard_map/ppermute | solution.py:19
  30.6 1.6 %acts_part.1 = (bf16[240,2048]{1,0:T(8,128)(2,1)S(1)}, f32[240,384]{1,0:T(8,128)S(1)}) custom-call(f32[32,768]{1,0:T(8,128)S(1)} %get-tuple-element.24.flat, f32[8,384]{1,0:T(8,128)S(1)} %slice.14.table, bf16[512,384]{1,0:T(8,128)(2,1)S(1)} %constant_dynamic-update-slice_fusion.here_ref, bf16[512,384]{1,0:T(8,128)(2,1)S(1)} %collective-permute-done.9.mate_ref), custom_call_target="tpu_custom_call" | custom-call | flops 2000000000 | tf_op jit(solution)/shard_map/acts_part/pallas_call | solution.py:274
  32.2 0.0 collective-permute-done.12.got_ref
  32.2 0.0 collective-permute-done.11.mate_ref
  32.2 1.3 %grad_part.1 = (f32[5,48,384]{2,1,0:T(8,128)}, f32[5,4,384]{2,1,0:T(4,128)}) custom-call(bf16[240,2048]{1,0:T(8,128)(2,1)S(1)} %get-tuple-element.30.acts_ref, bf16[512,384]{1,0:T(8,128)(2,1)S(1)} %collective-permute-done.10.there_ref, bf16[512,384]{1,0:T(8,128)(2,1)S(1)} %collective-permute-done.11.mate_ref, f32[240,384]{1,0:T(8,128)S(1)} %get-tuple-element.32.first_ref, ...), custom_call_target="tpu_custom_call" | custom-call | flops 1000000000 | tf_op jit(solution)/shard_map/grad_part/pallas_call | solution.py:305
  (12 shorter events, 0.1 us)
Async XLA Ops:
  0.6 0.7 %copy-start.1 = (s32[128]{0:T(128)S(1)}, s32[128]{0:T(128)}, u32[]{:S(2)}) copy-start(s32[128]{0:T(128)} %param.4) | copy-start | bytes 1540
  0.6 1.4 %copy-start = (bf16[128,384]{1,0:T(8,128)(2,1)S(1)}, bf16[128,384]{1,0:T(8,128)(2,1)}, u32[]{:S(2)}) copy-start(bf16[128,384]{1,0:T(8,128)(2,1)} %cot_ref) | copy-start | bytes 294916
  0.7 9.5 %copy-start.3 = (bf16[5,4,768]{2,1,0:T(4,128)(2,1)S(1)}, bf16[5,4,768]{2,1,0:T(4,128)(2,1)}, u32[]{:S(2)}) copy-start(bf16[5,4,768]{2,1,0:T(4,128)(2,1)} %stem_w_ref.1) | copy-start | bytes 92164
  0.7 9.5 %copy-start.2 = (bf16[5,768,384]{2,1,0:T(8,128)(2,1)S(1)}, bf16[5,768,384]{2,1,0:T(8,128)(2,1)}, u32[]{:S(2)}) copy-start(bf16[5,768,384]{2,1,0:T(8,128)(2,1)} %conv_w.3) | copy-start | bytes 8847364
  1.3 26.6 %copy-start.4 = (f32[8,128]{1,0:T(8,128)S(1)}, f32[8,128]{1,0:T(8,128)}, u32[]{:S(2)}) copy-start(f32[8,128]{1,0:T(8,128)} %mark_part.1.mark_ref) | copy-start | bytes 12292
  1.3 8.6 %collective-permute-start = (s32[1,128]{1,0:T(1,128)S(1)}, s32[1,128]{1,0:T(1,128)S(1)}, u32[]{:S(2)}, u32[]{:S(2)}) collective-permute-start(s32[1,128]{1,0:T(1,128)S(1)} %bitcast.1), channel_id=1, source_target_pairs={{2,4},{6,8},{10,12},{14,16},{18,20},{22,24},{26,28},{4,2},{8,6},{1... | collective-permute-start | bytes 1544 | tf_op jit(solution)/shard_map/ppermute | solution.py:30
  2.1 15.9 %collective-permute-start.6 = (bf16[128,384]{1,0:T(8,128)(2,1)S(1)}, bf16[128,384]{1,0:T(8,128)(2,1)S(1)}, u32[]{:S(2)}, u32[]{:S(2)}) collective-permute-start(bf16[128,384]{1,0:T(8,128)(2,1)S(1)} %copy-done), channel_id=1, source_target_pairs={{0,24},{2,26},{4,28},{6,30},{8,16},{10,18},{12,20},{14,22},{16,8},... | collective-permute-start | bytes 294920 | tf_op jit(solution)/shard_map/ppermute | solution.py:19
  9.3 9.2 %collective-permute-start.7 = (bf16[128,384]{1,0:T(8,128)(2,1)S(1)}, bf16[128,384]{1,0:T(8,128)(2,1)S(1)}, u32[]{:S(2)}, u32[]{:S(2)}) collective-permute-start(bf16[128,384]{1,0:T(8,128)(2,1)S(1)} %copy-done), channel_id=1, source_target_pairs={{0,16},{2,18},{4,20},{6,22},{8,24},{10,26},{12,28},{14,30},{16,0},... | collective-permute-start | bytes 294920 | tf_op jit(solution)/shard_map/ppermute | solution.py:19
  9.3 9.2 %collective-permute-start.8 = (bf16[128,384]{1,0:T(8,128)(2,1)S(1)}, bf16[128,384]{1,0:T(8,128)(2,1)S(1)}, u32[]{:S(2)}, u32[]{:S(2)}) collective-permute-start(bf16[128,384]{1,0:T(8,128)(2,1)S(1)} %copy-done), channel_id=1, source_target_pairs={{0,8},{2,10},{4,12},{6,14},{8,0},{10,2},{12,4},{14,6},{16,24},{18,... | collective-permute-start | bytes 294920 | tf_op jit(solution)/shard_map/ppermute | solution.py:19
  9.9 1.3 %collective-permute-start.1 = (s32[1,128]{1,0:T(1,128)S(1)}, s32[1,128]{1,0:T(1,128)S(1)}, u32[]{:S(2)}, u32[]{:S(2)}) collective-permute-start(s32[1,128]{1,0:T(1,128)S(1)} %bitcast.2), channel_id=1, source_target_pairs={{0,2},{2,0},{4,6},{6,4},{8,10},{10,8},{12,14},{14,12},{16,18},{18,... | collective-permute-start | bytes 1544 | tf_op jit(solution)/shard_map/ppermute | solution.py:19
  12.5 4.0 %collective-permute-start.2 = (f32[24,384]{1,0:T(8,128)S(1)}, f32[24,384]{1,0:T(8,128)S(1)}, u32[]{:S(2)}, u32[]{:S(2)}) collective-permute-start(f32[24,384]{1,0:T(8,128)S(1)} %get-tuple-element.26), channel_id=1, source_target_pairs={{0,1},{1,0},{2,3},{3,2},{4,5},{5,4},{6,7},{7,6},{8,9},{9,8},{10,11... | collective-permute-start | bytes 110600 | tf_op jit(solution)/shard_map/ppermute | solution.py:24
  16.5 4.2 %collective-permute-start.3 = (f32[32,384]{1,0:T(8,128)S(1)}, f32[32,384]{1,0:T(8,128)S(1)}, u32[]{:S(2)}, u32[]{:S(2)}) collective-permute-start(f32[32,384]{1,0:T(8,128)S(1)} %pad_maximum_fusion), channel_id=1, source_target_pairs={{0,4},{2,6},{4,0},{6,2},{8,12},{10,14},{12,8},{14,10},{16,20},{18,... | collective-permute-start | bytes 147464 | tf_op jit(solution)/shard_map/ppermute | solution.py:19
  18.5 11.4 %collective-permute-start.10 = (bf16[512,384]{1,0:T(8,128)(2,1)S(1)}, bf16[512,384]{1,0:T(8,128)(2,1)S(1)}, u32[]{:S(2)}, u32[]{:S(2)}) collective-permute-start(bf16[512,384]{1,0:T(8,128)(2,1)S(1)} %constant_dynamic-update-slice_fusion.here_ref), channel_id=1, source_target_pairs={{0,4},{2,6},{4,0},{6,2},{8,12},{10,14},{12,8},{14,10},{16,20},{18,... | collective-permute-start | bytes 1179656 | tf_op jit(solution)/shard_map/ppermute | solution.py:19
  18.8 11.1 %collective-permute-start.9 = (bf16[512,384]{1,0:T(8,128)(2,1)S(1)}, bf16[512,384]{1,0:T(8,128)(2,1)S(1)}, u32[]{:S(2)}, u32[]{:S(2)}) collective-permute-start(bf16[512,384]{1,0:T(8,128)(2,1)S(1)} %constant_dynamic-update-slice_fusion.here_ref), channel_id=1, source_target_pairs={{0,2},{2,0},{4,6},{6,4},{8,10},{10,8},{12,14},{14,12},{16,18},{18,... | collective-permute-start | bytes 1179656 | tf_op jit(solution)/shard_map/ppermute | solution.py:19
  20.7 4.2 %collective-permute-start.4 = (f32[32,384]{1,0:T(8,128)S(1)}, f32[32,384]{1,0:T(8,128)S(1)}, u32[]{:S(2)}, u32[]{:S(2)}) collective-permute-start(f32[32,384]{1,0:T(8,128)S(1)} %fusion), channel_id=1, source_target_pairs={{0,8},{2,10},{4,12},{6,14},{8,0},{10,2},{12,4},{14,6},{16,24},{18,... | collective-permute-start | bytes 147464 | tf_op jit(solution)/shard_map/ppermute | solution.py:19
  24.8 5.1 %collective-permute-start.5 = (f32[32,384]{1,0:T(8,128)S(1)}, f32[32,384]{1,0:T(8,128)S(1)}, u32[]{:S(2)}, u32[]{:S(2)}) collective-permute-start(f32[32,384]{1,0:T(8,128)S(1)} %add.14), channel_id=1, source_target_pairs={{0,16},{2,18},{4,20},{6,22},{8,24},{10,26},{12,28},{14,30},{16,0},... | collective-permute-start | bytes 147464 | tf_op jit(solution)/shard_map/ppermute | solution.py:19
  30.0 2.2 %collective-permute-start.11 = (bf16[512,384]{1,0:T(8,128)(2,1)S(1)}, bf16[512,384]{1,0:T(8,128)(2,1)S(1)}, u32[]{:S(2)}, u32[]{:S(2)}) collective-permute-start(bf16[512,384]{1,0:T(8,128)(2,1)S(1)} %collective-permute-done.10.there_ref), channel_id=1, source_target_pairs={{0,2},{2,0},{4,6},{6,4},{8,10},{10,8},{12,14},{14,12},{16,18},{18,... | collective-permute-start | bytes 1179656 | tf_op jit(solution)/shard_map/ppermute | solution.py:19
  30.1 2.1 %collective-permute-start.12 = (f32[24,384]{1,0:T(8,128)S(1)}, f32[24,384]{1,0:T(8,128)S(1)}, u32[]{:S(2)}, u32[]{:S(2)}) collective-permute-start(f32[24,384]{1,0:T(8,128)S(1)} %slice.15.stem_ref), channel_id=1, source_target_pairs={{0,2},{2,0},{4,6},{6,4},{8,10},{10,8},{12,14},{14,12},{16,18},{18,... | collective-permute-start | bytes 110600 | tf_op jit(solution)/shard_map/ppermute | solution.py:19

commit v5 on v4

--- a/solution.py
+++ b/solution.py
@@ -34,31 +34,32 @@
     return (value + step - 1) // step * step
 
 
-def gelu_value(stem):
-    tanh_val = jnp.tanh(math.sqrt(2.0 / math.pi) * (stem + 0.044715 * stem * stem * stem))
-    return 0.5 * stem * (1.0 + tanh_val), tanh_val
-
-
-def gelu_slope(stem, tanh_val):
+def gelu_parts(stem):
+    square = stem * stem
     coeff = math.sqrt(2.0 / math.pi)
-    return 0.5 * (1.0 + tanh_val) + 0.5 * stem * (1.0 - tanh_val * tanh_val) * coeff * (
-        1.0 + 3.0 * 0.044715 * stem * stem
-    )
-
-
-def indicators(bases, taps, shift, width, reverse):
-    rows = 32
+    return 0.5 + 0.5 * jnp.tanh(stem * (coeff + coeff * 0.044715 * square)), square
+
+
+def gelu_slope(stem, step, square):
+    coeff = math.sqrt(2.0 / math.pi)
+    return step + step * (1.0 - step) * stem * (2.0 * coeff + 2.0 * coeff * 3.0 * 0.044715 * square)
+
+
+def indicators(bases, taps, shift, width):
     size = bases.shape[1]
-    wide = jnp.broadcast_to(bases, (rows, size))
-    row = lax.broadcasted_iota(jnp.int32, (rows, width), 0)
-    if reverse:
-        row = 4 * taps - 1 - row
-    seen = jnp.full((rows, width), -1, jnp.int32)
+    wide = jnp.broadcast_to(bases, (8, size))
+    moved = []
     for k in range(taps):
         move = (-shift - k) % size
-        moved = (pltpu.roll(wide, move, 1) if move else wide)[:, :width]
-        seen = jnp.where((row >= 4 * k) & (row < 4 * k + 4), moved, seen)
-    return (seen == (row & 3)).astype(jnp.float32).astype(jnp.bfloat16)
+        moved.append((pltpu.roll(wide, move, 1) if move else wide)[:, :width])
+    none = jnp.full((8, width), -1, jnp.int32)
+    row = lax.broadcasted_iota(jnp.int32, (8, width), 0)
+    results = []
+    for order, letter in ((moved, row & 3), (moved[::-1], 3 - (row & 3))):
+        order = order + [none] * (8 - taps)
+        groups = [jnp.where(row < 4, order[2 * g], order[2 * g + 1]) == letter for g in range(4)]
+        results.append(jnp.concatenate([g.astype(jnp.float32) for g in groups]).astype(jnp.bfloat16))
+    return results
 
 
 def dot(left, right, dims=((1,), (0,))):
@@ -132,33 +133,38 @@
 
 def stem_kernel(taps, dact_f, dact_r, own_ref, mate_ref, other_ref, flat, keep_ref, send_ref, line, grad):
     rows, full = dact_f.shape
-    half = keep_ref.shape[1]
+    half = full // lax.axis_size("chan")
     span = own_ref.shape[1]
     seq, chan = lax.axis_index("seq"), lax.axis_index("chan")
     bases = line_of(own_ref, mate_ref, other_ref, line)
     stem_w = flat[...].astype(jnp.bfloat16)
     result = jnp.zeros(grad.shape, jnp.float32)
-    for strand, dact in enumerate((dact_f, dact_r)):
-        hot = indicators(bases, taps, span - 2 * (taps // 2), rows, strand == 1)
+    hots = indicators(bases, taps, span - 2 * (taps // 2), rows)
+    for strand, (dact, hot) in enumerate(zip((dact_f, dact_r), hots)):
         if strand == 0:
             inside = dot(hot, centre_rows(taps), ((0,), (0,)))[:, :1]
         stem = dot(hot, stem_w, ((0,), (0,))).astype(jnp.bfloat16).astype(jnp.float32)
-        _, tanh_val = gelu_value(stem)
-        dstem = 0.5 * dact[...] * gelu_slope(stem, tanh_val) * inside
+        step, square = gelu_parts(stem)
+        dstem = dact[...] * gelu_slope(stem, step, square) * (0.5 * inside)
         high = dstem.astype(jnp.bfloat16)
         low = (dstem - high.astype(jnp.float32)).astype(jnp.bfloat16)
         result += dot(hot, high) + dot(hot, low)
     grad[...] = result
+    count = 4 * taps
     top = send_ref.shape[0]
-    keep_ref[:top, :] = own_half(grad, slice(0, top), half, chan)
-    send_ref[...] = own_half(grad, slice(0, top), half, 1 - chan)
-    per_row = half // span
-    shape = (keep_ref.shape[0] - top, half)
-    place = lax.broadcasted_iota(jnp.int32, shape, 0) * per_row + lax.broadcasted_iota(jnp.int32, shape, 1) // span
-    table = jnp.zeros(shape, jnp.float32)
+    send_ref[...] = jnp.zeros_like(send_ref)
+    keep_ref[:top, :] = jnp.zeros((top, LANES), jnp.float32)
+    for j in range(half // LANES):
+        rows = slice(j * count, (j + 1) * count)
+        for ref, side in ((keep_ref, chan), (send_ref, 1 - chan)):
+            ref[rows, :] = grad[:count, pl.ds(pl.multiple_of(side * half + j * LANES, LANES), LANES)]
+    lines = span // LANES
+    place = lax.broadcasted_iota(jnp.int32, (keep_ref.shape[0] - top, LANES), 0)
+    table = jnp.zeros(place.shape, jnp.float32)
     for ref, block in ((own_ref, seq), (mate_ref, seq ^ 1)):
-        row = jnp.broadcast_to(jnp.concatenate([ref[...].astype(jnp.float32)] * per_row, axis=1), shape)
-        table = jnp.where(place == block, row, table)
+        for i in range(lines):
+            row = jnp.broadcast_to(ref[:, i * LANES : (i + 1) * LANES].astype(jnp.float32), place.shape)
+            table = jnp.where(place == block * lines + i, row, table)
     keep_ref[top:, :] = table
 
 
@@ -166,12 +172,11 @@
     full = flat.shape[1]
     span = own.shape[1]
     blocks = lax.axis_size("seq")
-    per_row = half // span
-    top = round_up(4 * taps, 8)
-    rows = top + round_up((blocks + per_row - 1) // per_row, 8)
+    top = round_up(4 * taps * (half // LANES), 8)
+    rows = top + round_up(blocks * span // LANES, 8)
     return pl.pallas_call(
         functools.partial(stem_kernel, taps),
-        out_shape=tuple(jax.ShapeDtypeStruct((r, half), jnp.float32) for r in (rows, top)),
+        out_shape=tuple(jax.ShapeDtypeStruct((r, LANES), jnp.float32) for r in (rows, top)),
         in_specs=[VMEM] * 6,
         out_specs=(VMEM, VMEM),
         scratch_shapes=[pltpu.VMEM((1, 3 * span), jnp.int32), pltpu.VMEM((32, full), jnp.float32)],
@@ -189,13 +194,13 @@
     chan = lax.axis_index("chan")
     bases = line_of(own_ref, mate_ref, other_ref, line)
     stem_w = flat[...].astype(jnp.bfloat16)
-    for strand, act in enumerate((act_f, act_r)):
-        hot = indicators(bases, taps, span - 2 * reach, rows, strand == 1)
+    hots = indicators(bases, taps, span - 2 * reach, rows)
+    for strand, (act, hot) in enumerate(zip((act_f, act_r), hots)):
         if strand == 0:
             inside = dot(hot, centre_rows(taps), ((0,), (0,)))[:, :1]
         stem = dot(hot, stem_w, ((0,), (0,))).astype(jnp.bfloat16).astype(jnp.float32)
-        value, _ = gelu_value(stem)
-        act[...] = (value * inside).astype(jnp.bfloat16).astype(jnp.float32)
+        step, _ = gelu_parts(stem)
+        act[...] = (stem * step * inside).astype(jnp.bfloat16).astype(jnp.float32)
         if strand == 0:
             stem_own[...] = stem
         else:
@@ -241,29 +246,29 @@
 def acts_kernel(taps, chans, masks, flat, table, here_ref, mate_ref, acts_ref, total_ref, line, cots):
     span = here_ref.shape[0] // len(masks)
     count = 4 * len(masks)
-    per_row = table.shape[1] // span
+    lines = span // LANES
     seq = lax.axis_index("seq")
     line[...] = jnp.full(line.shape, -1, jnp.int32)
     for b in range(count):
-        row, lane = b // per_row, b % per_row * span
-        line[:, LANES + b * span : LANES + (b + 1) * span] = table[row : row + 1, lane : lane + span].astype(jnp.int32)
+        for i in range(lines):
+            at = LANES + b * span + i * LANES
+            line[:, at : at + LANES] = table[b * lines + i : b * lines + i + 1, :].astype(jnp.int32)
     bases = line[...]
     width = bases.shape[1]
     full = flat.shape[1]
     own_w = pltpu.roll(flat[...], lax.rem(full - seq * (full // count), full), 1)[:, :chans].astype(jnp.bfloat16)
     values = []
     reach = taps // 2
-    for reverse in (False, True):
-        hot = indicators(bases, taps, -reach, width, reverse)
+    for hot in indicators(bases, taps, -reach, width):
         stem = dot(own_w, hot, ((0,), (0,))).astype(jnp.bfloat16).astype(jnp.float32)
-        value, _ = gelu_value(stem)
-        values.append(jnp.where(bases >= 0, value, 0.0).astype(jnp.bfloat16).astype(jnp.float32))
+        step, _ = gelu_parts(stem)
+        values.append(jnp.where(bases >= 0, stem * step, 0.0).astype(jnp.bfloat16))
     for k in range(taps):
         move = (reach - k) % width
         back = (k - reach) % width
         ahead = pltpu.roll(values[0], move, 1) if move else values[0]
         behind = pltpu.roll(values[1], back, 1) if back else values[1]
-        acts_ref[k * chans : (k + 1) * chans, :] = (ahead + behind)[:, LANES : LANES + count * span].astype(jnp.bfloat16)
+        acts_ref[k * chans : (k + 1) * chans, :] = (ahead + behind)[:, LANES : LANES + count * span]
     total_ref[...] = pair_dots(acts_ref, here_ref, mate_ref, masks, cots)
 
 
@@ -293,7 +298,9 @@
     taps, kept, _ = out_ref.shape
     stem = stem_ref[...] + got_ref[...]
     for k in range(taps):
-        stem_out[k] = stem[4 * k : 4 * k + 4]
+        for j in range(stem_out.shape[2] // LANES):
+            at = 4 * (j * taps + k)
+            stem_out[k, :, j * LANES : (j + 1) * LANES] = stem[at : at + 4]
     chans = acts_ref.shape[0] // taps
     total = 0.5 * (first_ref[...] + pair_dots(acts_ref, there_ref, mate_ref, masks, cots))
     for k in range(taps):

time: 33.6 us -> 33 us (0.982)
  starting transfers between devices: 17.8 us -> 17.2 us
    ppermute x11, starting transfers between devices: 15.4 us -> 14.8 us  [swap(): return lax.ppermute(value, 'seq', [(i, i ^ mask) for i in range(count)])]
  transfers between devices with their start and end apart: 13 -> 13, of which waited for: 4 -> 6; matrix products, arithmetic and copies ran while one was open for 0% -> 0% of each run, Pallas kernels for 18% -> 18%
where the time goes in v5:
time: 33 us; the launch traced here: 32.9 us
  starting transfers between devices  17.2 us (52%)
  Pallas kernels  7.65 us (23%)
  waiting for transfers between devices  7.12 us (22%)
  between operations  0.79 us (2%)
    ppermute x11, starting transfers between devices, swap(): return lax.ppermute(value, 'seq', [(i, i ^ mask) for i in range(count)])  14.8 us
    ppermute x11, waiting for transfers between devices, swap(): return lax.ppermute(value, 'seq', [(i, i ^ mask) for i in range(count)])  4.75 us
    ppermute x1, waiting for transfers between devices, swap_chan(): return lax.ppermute(value, 'chan', [(i, i ^ 1) for i in range(count)])  2.37 us
    pallas_call x1, Pallas kernels, blend_part(): pl.pallas_call(blend_kernel, out_shape=jax.ShapeDtypeStruct((span, half),...  2.07 us
    ppermute x1, starting transfers between devices, swap_chan(): return lax.ppermute(value, 'chan', [(i, i ^ 1) for i in range(count)])  1.59 us
    pallas_call x1, Pallas kernels, acts_part(): pl.pallas_call(functools.partial(acts_kernel, taps, chans, masks), out_sh...  1.47 us
    pallas_call x1, Pallas kernels, grad_part(): pl.pallas_call(functools.partial(grad_kernel, masks), out_shape=(jax.Shap...  1.28 us
    pallas_call x1, Pallas kernels, stem_part(): pl.pallas_call(functools.partial(stem_kernel, taps), out_shape=tuple((jax...  1.21 us
  transfers between devices with their start and end apart: 13, of which 6 were waited for; matrix products, arithmetic and copies ran while one was open for 0% of the time, Pallas kernels for 18%

profile of v5, /device:TPU:0, one launch (start us, length us, event | category | flops | bytes accessed | tf_op | source)
XLA Modules:
  0.0 32.9 jit_solution(9666066724301723065)
XLA Ops:
  0.6 0.0 copy-start.1
  0.6 0.0 copy-start
  0.7 0.0 copy-start.3
  0.7 0.0 copy-start.2
  0.7 0.6 %mark_part.1.mark_ref = f32[8,128]{1,0:T(8,128)} custom-call(), custom_call_target="tpu_custom_call" | custom-call | flops 6000000000 | tf_op jit(solution)/shard_map/mark_part/pallas_call | solution.py:74
  1.3 0.0 copy-done.1
  1.3 0.0 copy-start.4
  1.3 0.8 %collective-permute-start = (s32[1,128]{1,0:T(1,128)S(1)}, s32[1,128]{1,0:T(1,128)S(1)}, u32[]{:S(2)}, u32[]{:S(2)}) collective-permute-start(s32[1,128]{1,0:T(1,128)S(1)} %bitcast.1), channel_id=1, source_target_pairs={{2,4},{6,8},{10,12},{14,16},{18,20},{22,24},{26,28},{4,2},{8,6},{1... | collective-permute-start | bytes 1544 | tf_op jit(solution)/shard_map/ppermute | solution.py:30
  2.1 0.0 copy-done
  2.1 7.2 %collective-permute-start.6 = (bf16[128,384]{1,0:T(8,128)(2,1)S(1)}, bf16[128,384]{1,0:T(8,128)(2,1)S(1)}, u32[]{:S(2)}, u32[]{:S(2)}) collective-permute-start(bf16[128,384]{1,0:T(8,128)(2,1)S(1)} %copy-done), channel_id=1, source_target_pairs={{0,24},{2,26},{4,28},{6,30},{8,16},{10,18},{12,20},{14,22},{16,8},... | collective-permute-start | bytes 294920 | tf_op jit(solution)/shard_map/ppermute | solution.py:19
  9.3 0.0 collective-permute-start.7
  9.3 0.6 %collective-permute-start.8 = (bf16[128,384]{1,0:T(8,128)(2,1)S(1)}, bf16[128,384]{1,0:T(8,128)(2,1)S(1)}, u32[]{:S(2)}, u32[]{:S(2)}) collective-permute-start(bf16[128,384]{1,0:T(8,128)(2,1)S(1)} %copy-done), channel_id=1, source_target_pairs={{0,8},{2,10},{4,12},{6,14},{8,0},{10,2},{12,4},{14,6},{16,24},{18,... | collective-permute-start | bytes 294920 | tf_op jit(solution)/shard_map/ppermute | solution.py:19
  9.9 0.0 collective-permute-done.other_ref
  9.9 0.2 collective-permute-start.1
  10.1 0.0 copy-done.3
  10.1 0.0 copy-done.2
  10.1 1.0 %back_part.1 = (f32[144,768]{1,0:T(8,128)S(1)}, f32[144,768]{1,0:T(8,128)S(1)}, f32[32,768]{1,0:T(8,128)S(1)}) custom-call(bf16[128,384]{1,0:T(8,128)(2,1)S(1)} %copy-done, bf16[5,768,384]{2,1,0:T(8,128)(2,1)S(1)} %copy-done.2, bf16[5,4,768]{2,1,0:T(4,128)(2,1)S(1)} %copy-done.3), custom_call_target="tpu_custom_call" | custom-call | flops 1400000000 | tf_op jit(solution)/shard_map/back_part/pallas_call | solution.py:123
  11.2 0.0 collective-permute-done.1.mate_ref
  11.2 1.2 %stem_part.1 = (f32[80,128]{1,0:T(8,128)S(1)}, f32[64,128]{1,0:T(8,128)S(1)}) custom-call(f32[144,768]{1,0:T(8,128)S(1)} %get-tuple-element.21.dact_f, f32[144,768]{1,0:T(8,128)S(1)} %get-tuple-element.22.dact_r, s32[1,128]{1,0:T(1,128)S(1)} %bitcast.3, s32[1,128]{1,0:T(1,128)S(1)} %collective-permute-done.1.mate_ref, ...), custom_call_target="tpu_custom_call" | custom-call | tf_op jit(solution)/shard_map/stem_part/pallas_call | solution.py:177
  12.4 1.6 %collective-permute-start.2 = (f32[64,128]{1,0:T(8,128)S(1)}, f32[64,128]{1,0:T(8,128)S(1)}, u32[]{:S(2)}, u32[]{:S(2)}) collective-permute-start(f32[64,128]{1,0:T(8,128)S(1)} %get-tuple-element.26), channel_id=1, source_target_pairs={{0,1},{1,0},{2,3},{3,2},{4,5},{5,4},{6,7},{7,6},{8,9},{9,8},{10,11... | collective-permute-start | bytes 98312 | tf_op jit(solution)/shard_map/ppermute | solution.py:24
  14.0 2.4 %collective-permute-done.2 = f32[64,128]{1,0:T(8,128)S(1)} collective-permute-done((f32[64,128]{1,0:T(8,128)S(1)}, f32[64,128]{1,0:T(8,128)S(1)}, u32[]{:S(2)}, u32[]{:S(2)}) %collective-permute-start.2) | collective-permute-done | bytes 32800 | tf_op jit(solution)/shard_map/ppermute | solution.py:24
  16.4 1.5 %collective-permute-start.3 = (f32[80,128]{1,0:T(8,128)S(1)}, f32[80,128]{1,0:T(8,128)S(1)}, u32[]{:S(2)}, u32[]{:S(2)}) collective-permute-start(f32[80,128]{1,0:T(8,128)S(1)} %pad_maximum_fusion), channel_id=1, source_target_pairs={{0,4},{2,6},{4,0},{6,2},{8,12},{10,14},{12,8},{14,10},{16,20},{18,... | collective-permute-start | bytes 122888 | tf_op jit(solution)/shard_map/ppermute | solution.py:19
  17.9 0.0 collective-permute-done.6
  17.9 0.6 %collective-permute-done.7 = bf16[128,384]{1,0:T(8,128)(2,1)S(1)} collective-permute-done((bf16[128,384]{1,0:T(8,128)(2,1)S(1)}, bf16[128,384]{1,0:T(8,128)(2,1)S(1)}, u32[]{:S(2)}, u32[]{:S(2)}) %collective-permute-start.7) | collective-permute-done | bytes 98336 | tf_op jit(solution)/shard_map/ppermute | solution.py:19
  18.5 0.0 collective-permute-done.8
  18.5 0.3 collective-permute-start.10
  18.8 0.2 collective-permute-start.9
  19.0 1.4 %collective-permute-done.3 = f32[80,128]{1,0:T(8,128)S(1)} collective-permute-done((f32[80,128]{1,0:T(8,128)S(1)}, f32[80,128]{1,0:T(8,128)S(1)}, u32[]{:S(2)}, u32[]{:S(2)}) %collective-permute-start.3) | collective-permute-done | bytes 40992 | tf_op jit(solution)/shard_map/ppermute | solution.py:19
  20.5 1.6 %collective-permute-start.4 = (f32[80,128]{1,0:T(8,128)S(1)}, f32[80,128]{1,0:T(8,128)S(1)}, u32[]{:S(2)}, u32[]{:S(2)}) collective-permute-start(f32[80,128]{1,0:T(8,128)S(1)} %fusion), channel_id=1, source_target_pairs={{0,8},{2,10},{4,12},{6,14},{8,0},{10,2},{12,4},{14,6},{16,24},{18,... | collective-permute-start | bytes 122888 | tf_op jit(solution)/shard_map/ppermute | solution.py:19
  22.1 2.4 %collective-permute-done.4 = f32[80,128]{1,0:T(8,128)S(1)} collective-permute-done((f32[80,128]{1,0:T(8,128)S(1)}, f32[80,128]{1,0:T(8,128)S(1)}, u32[]{:S(2)}, u32[]{:S(2)}) %collective-permute-start.4) | collective-permute-done | bytes 40992 | tf_op jit(solution)/shard_map/ppermute | solution.py:19
  24.5 2.7 %collective-permute-start.5 = (f32[80,128]{1,0:T(8,128)S(1)}, f32[80,128]{1,0:T(8,128)S(1)}, u32[]{:S(2)}, u32[]{:S(2)}) collective-permute-start(f32[80,128]{1,0:T(8,128)S(1)} %add.14), channel_id=1, source_target_pairs={{0,16},{2,18},{4,20},{6,22},{8,24},{10,26},{12,28},{14,30},{16,0},... | collective-permute-start | bytes 122888 | tf_op jit(solution)/shard_map/ppermute | solution.py:19
  27.2 0.0 copy-done.4
  27.2 2.1 %blend_part.1 = bf16[128,384]{1,0:T(8,128)(2,1)} custom-call(f32[8,128]{1,0:T(8,128)S(1)} %copy-done.4, s32[1,128]{1,0:T(1,128)S(1)} %bitcast.4, s32[1,128]{1,0:T(1,128)S(1)} %collective-permute-done.1.mate_ref, s32[1,128]{1,0:T(1,128)S(1)} %collective-permute-done.other_ref, f32[32,768]{1,0:T(8,128)S(1)} %get-tuple-element.24.flat, ...), custom_call_target="tpu_custom_call" | custom-call | flops 2000000000 | tf_op jit(solution)/shard_map/blend_part/pallas_call | solution.py:220
  29.3 0.1 collective-permute-done.5
  29.4 0.2 collective-permute-done.10.there_ref
  29.6 0.0 collective-permute-done.9.mate_ref
  29.6 0.0 collective-permute-start.11
  29.6 0.5 %collective-permute-start.12 = (f32[64,128]{1,0:T(8,128)S(1)}, f32[64,128]{1,0:T(8,128)S(1)}, u32[]{:S(2)}, u32[]{:S(2)}) collective-permute-start(f32[64,128]{1,0:T(8,128)S(1)} %slice.15.stem_ref), channel_id=1, source_target_pairs={{0,2},{2,0},{4,6},{6,4},{8,10},{10,8},{12,14},{14,12},{16,18},{18,... | collective-permute-start | bytes 98312 | tf_op jit(solution)/shard_map/ppermute | solution.py:19
  30.1 1.5 %acts_part.1 = (bf16[240,2048]{1,0:T(8,128)(2,1)S(1)}, f32[240,384]{1,0:T(8,128)S(1)}) custom-call(f32[32,768]{1,0:T(8,128)S(1)} %get-tuple-element.24.flat, f32[16,128]{1,0:T(8,128)S(1)} %slice.14.table, bf16[512,384]{1,0:T(8,128)(2,1)S(1)} %constant_dynamic-update-slice_fusion.here_ref, bf16[512,384]{1,0:T(8,128)(2,1)S(1)} %collective-permute-done.9.mate_ref), custom_call_target="tpu_custom_call" | custom-call | flops 2000000000 | tf_op jit(solution)/shard_map/acts_part/pallas_call | solution.py:279
  31.6 0.0 collective-permute-done.12.got_ref
  31.6 0.0 collective-permute-done.11.mate_ref
  31.6 1.3 %grad_part.1 = (f32[5,48,384]{2,1,0:T(8,128)}, f32[5,4,384]{2,1,0:T(4,128)}) custom-call(bf16[240,2048]{1,0:T(8,128)(2,1)S(1)} %get-tuple-element.30.acts_ref, bf16[512,384]{1,0:T(8,128)(2,1)S(1)} %collective-permute-done.10.there_ref, bf16[512,384]{1,0:T(8,128)(2,1)S(1)} %collective-permute-done.11.mate_ref, f32[240,384]{1,0:T(8,128)S(1)} %get-tuple-element.32.first_ref, ...), custom_call_target="tpu_custom_call" | custom-call | flops 1000000000 | tf_op jit(solution)/shard_map/grad_part/pallas_call | solution.py:312
  (12 shorter events, 0.1 us)
Async XLA Ops:
  0.6 0.7 %copy-start.1 = (s32[128]{0:T(128)S(1)}, s32[128]{0:T(128)}, u32[]{:S(2)}) copy-start(s32[128]{0:T(128)} %param.4) | copy-start | bytes 1540
  0.6 1.4 %copy-start = (bf16[128,384]{1,0:T(8,128)(2,1)S(1)}, bf16[128,384]{1,0:T(8,128)(2,1)}, u32[]{:S(2)}) copy-start(bf16[128,384]{1,0:T(8,128)(2,1)} %cot_ref) | copy-start | bytes 294916
  0.7 9.5 %copy-start.3 = (bf16[5,4,768]{2,1,0:T(4,128)(2,1)S(1)}, bf16[5,4,768]{2,1,0:T(4,128)(2,1)}, u32[]{:S(2)}) copy-start(bf16[5,4,768]{2,1,0:T(4,128)(2,1)} %stem_w_ref.1) | copy-start | bytes 92164
  0.7 9.5 %copy-start.2 = (bf16[5,768,384]{2,1,0:T(8,128)(2,1)S(1)}, bf16[5,768,384]{2,1,0:T(8,128)(2,1)}, u32[]{:S(2)}) copy-start(bf16[5,768,384]{2,1,0:T(8,128)(2,1)} %conv_w.3) | copy-start | bytes 8847364
  1.3 25.9 %copy-start.4 = (f32[8,128]{1,0:T(8,128)S(1)}, f32[8,128]{1,0:T(8,128)}, u32[]{:S(2)}) copy-start(f32[8,128]{1,0:T(8,128)} %mark_part.1.mark_ref) | copy-start | bytes 12292
  1.3 8.6 %collective-permute-start = (s32[1,128]{1,0:T(1,128)S(1)}, s32[1,128]{1,0:T(1,128)S(1)}, u32[]{:S(2)}, u32[]{:S(2)}) collective-permute-start(s32[1,128]{1,0:T(1,128)S(1)} %bitcast.1), channel_id=1, source_target_pairs={{2,4},{6,8},{10,12},{14,16},{18,20},{22,24},{26,28},{4,2},{8,6},{1... | collective-permute-start | bytes 1544 | tf_op jit(solution)/shard_map/ppermute | solution.py:30
  2.1 15.8 %collective-permute-start.6 = (bf16[128,384]{1,0:T(8,128)(2,1)S(1)}, bf16[128,384]{1,0:T(8,128)(2,1)S(1)}, u32[]{:S(2)}, u32[]{:S(2)}) collective-permute-start(bf16[128,384]{1,0:T(8,128)(2,1)S(1)} %copy-done), channel_id=1, source_target_pairs={{0,24},{2,26},{4,28},{6,30},{8,16},{10,18},{12,20},{14,22},{16,8},... | collective-permute-start | bytes 294920 | tf_op jit(solution)/shard_map/ppermute | solution.py:19
  9.3 9.2 %collective-permute-start.7 = (bf16[128,384]{1,0:T(8,128)(2,1)S(1)}, bf16[128,384]{1,0:T(8,128)(2,1)S(1)}, u32[]{:S(2)}, u32[]{:S(2)}) collective-permute-start(bf16[128,384]{1,0:T(8,128)(2,1)S(1)} %copy-done), channel_id=1, source_target_pairs={{0,16},{2,18},{4,20},{6,22},{8,24},{10,26},{12,28},{14,30},{16,0},... | collective-permute-start | bytes 294920 | tf_op jit(solution)/shard_map/ppermute | solution.py:19
  9.3 9.2 %collective-permute-start.8 = (bf16[128,384]{1,0:T(8,128)(2,1)S(1)}, bf16[128,384]{1,0:T(8,128)(2,1)S(1)}, u32[]{:S(2)}, u32[]{:S(2)}) collective-permute-start(bf16[128,384]{1,0:T(8,128)(2,1)S(1)} %copy-done), channel_id=1, source_target_pairs={{0,8},{2,10},{4,12},{6,14},{8,0},{10,2},{12,4},{14,6},{16,24},{18,... | collective-permute-start | bytes 294920 | tf_op jit(solution)/shard_map/ppermute | solution.py:19
  9.9 1.3 %collective-permute-start.1 = (s32[1,128]{1,0:T(1,128)S(1)}, s32[1,128]{1,0:T(1,128)S(1)}, u32[]{:S(2)}, u32[]{:S(2)}) collective-permute-start(s32[1,128]{1,0:T(1,128)S(1)} %bitcast.2), channel_id=1, source_target_pairs={{0,2},{2,0},{4,6},{6,4},{8,10},{10,8},{12,14},{14,12},{16,18},{18,... | collective-permute-start | bytes 1544 | tf_op jit(solution)/shard_map/ppermute | solution.py:19
  12.4 4.0 %collective-permute-start.2 = (f32[64,128]{1,0:T(8,128)S(1)}, f32[64,128]{1,0:T(8,128)S(1)}, u32[]{:S(2)}, u32[]{:S(2)}) collective-permute-start(f32[64,128]{1,0:T(8,128)S(1)} %get-tuple-element.26), channel_id=1, source_target_pairs={{0,1},{1,0},{2,3},{3,2},{4,5},{5,4},{6,7},{7,6},{8,9},{9,8},{10,11... | collective-permute-start | bytes 98312 | tf_op jit(solution)/shard_map/ppermute | solution.py:24
  16.4 4.1 %collective-permute-start.3 = (f32[80,128]{1,0:T(8,128)S(1)}, f32[80,128]{1,0:T(8,128)S(1)}, u32[]{:S(2)}, u32[]{:S(2)}) collective-permute-start(f32[80,128]{1,0:T(8,128)S(1)} %pad_maximum_fusion), channel_id=1, source_target_pairs={{0,4},{2,6},{4,0},{6,2},{8,12},{10,14},{12,8},{14,10},{16,20},{18,... | collective-permute-start | bytes 122888 | tf_op jit(solution)/shard_map/ppermute | solution.py:19
  18.5 11.0 %collective-permute-start.10 = (bf16[512,384]{1,0:T(8,128)(2,1)S(1)}, bf16[512,384]{1,0:T(8,128)(2,1)S(1)}, u32[]{:S(2)}, u32[]{:S(2)}) collective-permute-start(bf16[512,384]{1,0:T(8,128)(2,1)S(1)} %constant_dynamic-update-slice_fusion.here_ref), channel_id=1, source_target_pairs={{0,4},{2,6},{4,0},{6,2},{8,12},{10,14},{12,8},{14,10},{16,20},{18,... | collective-permute-start | bytes 1179656 | tf_op jit(solution)/shard_map/ppermute | solution.py:19
  18.8 10.7 %collective-permute-start.9 = (bf16[512,384]{1,0:T(8,128)(2,1)S(1)}, bf16[512,384]{1,0:T(8,128)(2,1)S(1)}, u32[]{:S(2)}, u32[]{:S(2)}) collective-permute-start(bf16[512,384]{1,0:T(8,128)(2,1)S(1)} %constant_dynamic-update-slice_fusion.here_ref), channel_id=1, source_target_pairs={{0,2},{2,0},{4,6},{6,4},{8,10},{10,8},{12,14},{14,12},{16,18},{18,... | collective-permute-start | bytes 1179656 | tf_op jit(solution)/shard_map/ppermute | solution.py:19
  20.5 4.0 %collective-permute-start.4 = (f32[80,128]{1,0:T(8,128)S(1)}, f32[80,128]{1,0:T(8,128)S(1)}, u32[]{:S(2)}, u32[]{:S(2)}) collective-permute-start(f32[80,128]{1,0:T(8,128)S(1)} %fusion), channel_id=1, source_target_pairs={{0,8},{2,10},{4,12},{6,14},{8,0},{10,2},{12,4},{14,6},{16,24},{18,... | collective-permute-start | bytes 122888 | tf_op jit(solution)/shard_map/ppermute | solution.py:19
  24.5 4.9 %collective-permute-start.5 = (f32[80,128]{1,0:T(8,128)S(1)}, f32[80,128]{1,0:T(8,128)S(1)}, u32[]{:S(2)}, u32[]{:S(2)}) collective-permute-start(f32[80,128]{1,0:T(8,128)S(1)} %add.14), channel_id=1, source_target_pairs={{0,16},{2,18},{4,20},{6,22},{8,24},{10,26},{12,28},{14,30},{16,0},... | collective-permute-start | bytes 122888 | tf_op jit(solution)/shard_map/ppermute | solution.py:19
  29.6 2.0 %collective-permute-start.11 = (bf16[512,384]{1,0:T(8,128)(2,1)S(1)}, bf16[512,384]{1,0:T(8,128)(2,1)S(1)}, u32[]{:S(2)}, u32[]{:S(2)}) collective-permute-start(bf16[512,384]{1,0:T(8,128)(2,1)S(1)} %collective-permute-done.10.there_ref), channel_id=1, source_target_pairs={{0,2},{2,0},{4,6},{6,4},{8,10},{10,8},{12,14},{14,12},{16,18},{18,... | collective-permute-start | bytes 1179656 | tf_op jit(solution)/shard_map/ppermute | solution.py:19
  29.6 2.0 %collective-permute-start.12 = (f32[64,128]{1,0:T(8,128)S(1)}, f32[64,128]{1,0:T(8,128)S(1)}, u32[]{:S(2)}, u32[]{:S(2)}) collective-permute-start(f32[64,128]{1,0:T(8,128)S(1)} %slice.15.stem_ref), channel_id=1, source_target_pairs={{0,2},{2,0},{4,6},{6,4},{8,10},{10,8},{12,14},{14,12},{16,18},{18,... | collective-permute-start | bytes 98312 | tf_op jit(solution)/shard_map/ppermute | solution.py:19

commit v6 on v5

--- a/solution.py
+++ b/solution.py
@@ -67,14 +67,14 @@
 
 
 def mark_kernel(out_ref):
-    out_ref[...] = jnp.zeros_like(out_ref)
+    del out_ref
 
 
 def mark_part():
     return pl.pallas_call(
         mark_kernel,
         out_shape=jax.ShapeDtypeStruct((8, LANES), jnp.float32),
-        out_specs=VMEM,
+        out_specs=pl.BlockSpec(memory_space=pl.ANY),
         cost_estimate=pl.CostEstimate(flops=6 * 10**9, bytes_accessed=0, transcendentals=0),
         name="mark_part",
     )()
@@ -335,9 +335,9 @@
     far = range(count - 4, 0, -4)
 
     mark = mark_part()
-    bases = after(tokens.reshape(1, span), mark)
+    bases = tokens.reshape(1, span)
     other = swap_next_chip(bases)
-    far_cot = [swap(cotangent, m) for m in far]
+    far_cot = [swap(after(cotangent, mark), m) for m in far]
     mate = swap(after(bases, other), 1)
     *dacts, flat = back_part(after(cotangent, other), conv_weight, stem_weight)
     keep, send = stem_part(dacts, bases, mate, other, flat, taps, half)

time: 33 us -> 32.6 us (0.988)
  Pallas kernels: 7.65 us -> 7.05 us
    pallas_call x1, Pallas kernels: 0.6 us -> 0.01 us  [mark_part(): pl.pallas_call(mark_kernel, out_shape=jax.ShapeDtypeStruct((8, LANES), jn...]
  transfers between devices with their start and end apart: 13 -> 13, of which waited for: 6 -> 5; matrix products, arithmetic and copies ran while one was open for 0% -> 0% of each run, Pallas kernels for 18% -> 18%
where the time goes in v6:
time: 32.6 us; the launch traced here: 32.4 us
  starting transfers between devices  17.4 us (53%)
  Pallas kernels  7.05 us (22%)
  waiting for transfers between devices  7.04 us (22%)
  between operations  0.79 us (2%)
    ppermute x11, starting transfers between devices, swap(): return lax.ppermute(value, 'seq', [(i, i ^ mask) for i in range(count)])  15 us
    ppermute x11, waiting for transfers between devices, swap(): return lax.ppermute(value, 'seq', [(i, i ^ mask) for i in range(count)])  4.66 us
    ppermute x1, waiting for transfers between devices, swap_chan(): return lax.ppermute(value, 'chan', [(i, i ^ 1) for i in range(count)])  2.37 us
    pallas_call x1, Pallas kernels, blend_part(): pl.pallas_call(blend_kernel, out_shape=jax.ShapeDtypeStruct((span, half),...  2.07 us
    ppermute x1, starting transfers between devices, swap_chan(): return lax.ppermute(value, 'chan', [(i, i ^ 1) for i in range(count)])  1.59 us
    pallas_call x1, Pallas kernels, acts_part(): pl.pallas_call(functools.partial(acts_kernel, taps, chans, masks), out_sh...  1.47 us
    pallas_call x1, Pallas kernels, grad_part(): pl.pallas_call(functools.partial(grad_kernel, masks), out_shape=(jax.Shap...  1.28 us
    pallas_call x1, Pallas kernels, stem_part(): pl.pallas_call(functools.partial(stem_kernel, taps), out_shape=tuple((jax...  1.21 us
  transfers between devices with their start and end apart: 13, of which 5 were waited for; matrix products, arithmetic and copies ran while one was open for 0% of the time, Pallas kernels for 18%

profile of v6, /device:TPU:0, one launch (start us, length us, event | category | flops | bytes accessed | tf_op | source)
XLA Modules:
  0.0 32.4 jit_solution(1558168511827809478)
XLA Ops:
  0.6 0.0 copy-start
  0.6 0.0 copy-start.1
  0.7 0.0 copy-start.2
  0.7 0.0 copy-start.3
  0.7 0.8 %collective-permute-start = (s32[1,128]{1,0:T(1,128)}, s32[1,128]{1,0:T(1,128)S(1)}, u32[]{:S(2)}, u32[]{:S(2)}) collective-permute-start(s32[1,128]{1,0:T(1,128)} %bitcast.1), channel_id=1, source_target_pairs={{2,4},{6,8},{10,12},{14,16},{18,20},{22,24},{26,28},{4,2},{8,6},{1... | collective-permute-start | bytes 1544 | tf_op jit(solution)/shard_map/ppermute | solution.py:30
  1.5 0.0 copy-done
  1.5 0.0 copy-start.4
  1.5 7.3 %collective-permute-start.6 = (bf16[128,384]{1,0:T(8,128)(2,1)S(1)}, bf16[128,384]{1,0:T(8,128)(2,1)S(1)}, u32[]{:S(2)}, u32[]{:S(2)}) collective-permute-start(bf16[128,384]{1,0:T(8,128)(2,1)S(1)} %copy-done), channel_id=1, source_target_pairs={{0,24},{2,26},{4,28},{6,30},{8,16},{10,18},{12,20},{14,22},{16,8},... | collective-permute-start | bytes 294920 | tf_op jit(solution)/shard_map/ppermute | solution.py:19
  8.8 0.0 collective-permute-start.7
  8.8 0.6 %collective-permute-start.8 = (bf16[128,384]{1,0:T(8,128)(2,1)S(1)}, bf16[128,384]{1,0:T(8,128)(2,1)S(1)}, u32[]{:S(2)}, u32[]{:S(2)}) collective-permute-start(bf16[128,384]{1,0:T(8,128)(2,1)S(1)} %copy-done), channel_id=1, source_target_pairs={{0,8},{2,10},{4,12},{6,14},{8,0},{10,2},{12,4},{14,6},{16,24},{18,... | collective-permute-start | bytes 294920 | tf_op jit(solution)/shard_map/ppermute | solution.py:19
  9.5 0.0 collective-permute-done.other_ref
  9.5 0.0 copy-done.1
  9.5 0.2 collective-permute-start.1
  9.7 0.0 copy-done.2
  9.7 0.0 copy-done.3
  9.7 1.0 %back_part.1 = (f32[144,768]{1,0:T(8,128)S(1)}, f32[144,768]{1,0:T(8,128)S(1)}, f32[32,768]{1,0:T(8,128)S(1)}) custom-call(bf16[128,384]{1,0:T(8,128)(2,1)S(1)} %copy-done, bf16[5,768,384]{2,1,0:T(8,128)(2,1)S(1)} %copy-done.2, bf16[5,4,768]{2,1,0:T(4,128)(2,1)S(1)} %copy-done.3), custom_call_target="tpu_custom_call" | custom-call | flops 1400000000 | tf_op jit(solution)/shard_map/back_part/pallas_call | solution.py:123
  10.7 0.0 collective-permute-done.1.mate_ref
  10.7 1.2 %stem_part.1 = (f32[80,128]{1,0:T(8,128)S(1)}, f32[64,128]{1,0:T(8,128)S(1)}) custom-call(f32[144,768]{1,0:T(8,128)S(1)} %get-tuple-element.20.dact_f, f32[144,768]{1,0:T(8,128)S(1)} %get-tuple-element.21.dact_r, s32[1,128]{1,0:T(1,128)S(1)} %bitcast.3, s32[1,128]{1,0:T(1,128)S(1)} %collective-permute-done.1.mate_ref, ...), custom_call_target="tpu_custom_call" | custom-call | tf_op jit(solution)/shard_map/stem_part/pallas_call | solution.py:177
  12.0 1.6 %collective-permute-start.2 = (f32[64,128]{1,0:T(8,128)S(1)}, f32[64,128]{1,0:T(8,128)S(1)}, u32[]{:S(2)}, u32[]{:S(2)}) collective-permute-start(f32[64,128]{1,0:T(8,128)S(1)} %get-tuple-element.25), channel_id=1, source_target_pairs={{0,1},{1,0},{2,3},{3,2},{4,5},{5,4},{6,7},{7,6},{8,9},{9,8},{10,11... | collective-permute-start | bytes 98312 | tf_op jit(solution)/shard_map/ppermute | solution.py:24
  13.6 2.4 %collective-permute-done.2 = f32[64,128]{1,0:T(8,128)S(1)} collective-permute-done((f32[64,128]{1,0:T(8,128)S(1)}, f32[64,128]{1,0:T(8,128)S(1)}, u32[]{:S(2)}, u32[]{:S(2)}) %collective-permute-start.2) | collective-permute-done | bytes 32800 | tf_op jit(solution)/shard_map/ppermute | solution.py:24
  15.9 1.5 %collective-permute-start.3 = (f32[80,128]{1,0:T(8,128)S(1)}, f32[80,128]{1,0:T(8,128)S(1)}, u32[]{:S(2)}, u32[]{:S(2)}) collective-permute-start(f32[80,128]{1,0:T(8,128)S(1)} %pad_maximum_fusion), channel_id=1, source_target_pairs={{0,4},{2,6},{4,0},{6,2},{8,12},{10,14},{12,8},{14,10},{16,20},{18,... | collective-permute-start | bytes 122888 | tf_op jit(solution)/shard_map/ppermute | solution.py:19
  17.4 0.0 collective-permute-done.6
  17.4 0.6 %collective-permute-done.7 = bf16[128,384]{1,0:T(8,128)(2,1)S(1)} collective-permute-done((bf16[128,384]{1,0:T(8,128)(2,1)S(1)}, bf16[128,384]{1,0:T(8,128)(2,1)S(1)}, u32[]{:S(2)}, u32[]{:S(2)}) %collective-permute-start.7) | collective-permute-done | bytes 98336 | tf_op jit(solution)/shard_map/ppermute | solution.py:19
  18.1 0.0 collective-permute-done.8
  18.1 0.3 collective-permute-start.10
  18.4 0.2 collective-permute-start.9
  18.6 1.5 %collective-permute-done.3 = f32[80,128]{1,0:T(8,128)S(1)} collective-permute-done((f32[80,128]{1,0:T(8,128)S(1)}, f32[80,128]{1,0:T(8,128)S(1)}, u32[]{:S(2)}, u32[]{:S(2)}) %collective-permute-start.3) | collective-permute-done | bytes 40992 | tf_op jit(solution)/shard_map/ppermute | solution.py:19
  20.0 1.6 %collective-permute-start.4 = (f32[80,128]{1,0:T(8,128)S(1)}, f32[80,128]{1,0:T(8,128)S(1)}, u32[]{:S(2)}, u32[]{:S(2)}) collective-permute-start(f32[80,128]{1,0:T(8,128)S(1)} %fusion), channel_id=1, source_target_pairs={{0,8},{2,10},{4,12},{6,14},{8,0},{10,2},{12,4},{14,6},{16,24},{18,... | collective-permute-start | bytes 122888 | tf_op jit(solution)/shard_map/ppermute | solution.py:19
  21.6 2.4 %collective-permute-done.4 = f32[80,128]{1,0:T(8,128)S(1)} collective-permute-done((f32[80,128]{1,0:T(8,128)S(1)}, f32[80,128]{1,0:T(8,128)S(1)}, u32[]{:S(2)}, u32[]{:S(2)}) %collective-permute-start.4) | collective-permute-done | bytes 40992 | tf_op jit(solution)/shard_map/ppermute | solution.py:19
  24.0 2.8 %collective-permute-start.5 = (f32[80,128]{1,0:T(8,128)S(1)}, f32[80,128]{1,0:T(8,128)S(1)}, u32[]{:S(2)}, u32[]{:S(2)}) collective-permute-start(f32[80,128]{1,0:T(8,128)S(1)} %add.14), channel_id=1, source_target_pairs={{0,16},{2,18},{4,20},{6,22},{8,24},{10,26},{12,28},{14,30},{16,0},... | collective-permute-start | bytes 122888 | tf_op jit(solution)/shard_map/ppermute | solution.py:19
  26.8 0.0 copy-done.4
  26.8 2.1 %blend_part.1 = bf16[128,384]{1,0:T(8,128)(2,1)} custom-call(f32[8,128]{1,0:T(8,128)S(1)} %copy-done.4, s32[1,128]{1,0:T(1,128)S(1)} %bitcast.4, s32[1,128]{1,0:T(1,128)S(1)} %collective-permute-done.1.mate_ref, s32[1,128]{1,0:T(1,128)S(1)} %collective-permute-done.other_ref, f32[32,768]{1,0:T(8,128)S(1)} %get-tuple-element.23.flat, ...), custom_call_target="tpu_custom_call" | custom-call | flops 2000000000 | tf_op jit(solution)/shard_map/blend_part/pallas_call | solution.py:220
  28.9 0.0 collective-permute-done.5
  28.9 0.2 collective-permute-done.10.there_ref
  29.1 0.0 collective-permute-done.9.mate_ref
  29.1 0.0 collective-permute-start.11
  29.1 0.5 %collective-permute-start.12 = (f32[64,128]{1,0:T(8,128)S(1)}, f32[64,128]{1,0:T(8,128)S(1)}, u32[]{:S(2)}, u32[]{:S(2)}) collective-permute-start(f32[64,128]{1,0:T(8,128)S(1)} %slice.15.stem_ref), channel_id=1, source_target_pairs={{0,2},{2,0},{4,6},{6,4},{8,10},{10,8},{12,14},{14,12},{16,18},{18,... | collective-permute-start | bytes 98312 | tf_op jit(solution)/shard_map/ppermute | solution.py:19
  29.6 1.5 %acts_part.1 = (bf16[240,2048]{1,0:T(8,128)(2,1)S(1)}, f32[240,384]{1,0:T(8,128)S(1)}) custom-call(f32[32,768]{1,0:T(8,128)S(1)} %get-tuple-element.23.flat, f32[16,128]{1,0:T(8,128)S(1)} %slice.14.table, bf16[512,384]{1,0:T(8,128)(2,1)S(1)} %constant_dynamic-update-slice_fusion.here_ref, bf16[512,384]{1,0:T(8,128)(2,1)S(1)} %collective-permute-done.9.mate_ref), custom_call_target="tpu_custom_call" | custom-call | flops 2000000000 | tf_op jit(solution)/shard_map/acts_part/pallas_call | solution.py:279
  31.1 0.0 collective-permute-done.12.got_ref
  31.1 0.0 collective-permute-done.11.mate_ref
  31.1 1.3 %grad_part.1 = (f32[5,48,384]{2,1,0:T(8,128)}, f32[5,4,384]{2,1,0:T(4,128)}) custom-call(bf16[240,2048]{1,0:T(8,128)(2,1)S(1)} %get-tuple-element.30.acts_ref, bf16[512,384]{1,0:T(8,128)(2,1)S(1)} %collective-permute-done.10.there_ref, bf16[512,384]{1,0:T(8,128)(2,1)S(1)} %collective-permute-done.11.mate_ref, f32[240,384]{1,0:T(8,128)S(1)} %get-tuple-element.32.first_ref, ...), custom_call_target="tpu_custom_call" | custom-call | flops 1000000000 | tf_op jit(solution)/shard_map/grad_part/pallas_call | solution.py:312
  (13 shorter events, 0.1 us)
Async XLA Ops:
  0.6 0.9 %copy-start = (bf16[128,384]{1,0:T(8,128)(2,1)S(1)}, bf16[128,384]{1,0:T(8,128)(2,1)}, u32[]{:S(2)}) copy-start(bf16[128,384]{1,0:T(8,128)(2,1)} %cot_ref) | copy-start | bytes 294916
  0.6 8.8 %copy-start.1 = (s32[128]{0:T(128)S(1)}, s32[128]{0:T(128)}, u32[]{:S(2)}) copy-start(s32[128]{0:T(128)} %param.4) | copy-start | bytes 1540
  0.7 9.0 %copy-start.2 = (bf16[5,768,384]{2,1,0:T(8,128)(2,1)S(1)}, bf16[5,768,384]{2,1,0:T(8,128)(2,1)}, u32[]{:S(2)}) copy-start(bf16[5,768,384]{2,1,0:T(8,128)(2,1)} %conv_w.3) | copy-start | bytes 8847364
  0.7 9.0 %copy-start.3 = (bf16[5,4,768]{2,1,0:T(4,128)(2,1)S(1)}, bf16[5,4,768]{2,1,0:T(4,128)(2,1)}, u32[]{:S(2)}) copy-start(bf16[5,4,768]{2,1,0:T(4,128)(2,1)} %stem_w_ref.1) | copy-start | bytes 92164
  0.7 8.8 %collective-permute-start = (s32[1,128]{1,0:T(1,128)}, s32[1,128]{1,0:T(1,128)S(1)}, u32[]{:S(2)}, u32[]{:S(2)}) collective-permute-start(s32[1,128]{1,0:T(1,128)} %bitcast.1), channel_id=1, source_target_pairs={{2,4},{6,8},{10,12},{14,16},{18,20},{22,24},{26,28},{4,2},{8,6},{1... | collective-permute-start | bytes 1544 | tf_op jit(solution)/shard_map/ppermute | solution.py:30
  1.5 25.3 %copy-start.4 = (f32[8,128]{1,0:T(8,128)S(1)}, f32[8,128]{1,0:T(8,128)}, u32[]{:S(2)}) copy-start(f32[8,128]{1,0:T(8,128)} %mark_part.1.mark_ref) | copy-start | bytes 12292
  1.5 15.9 %collective-permute-start.6 = (bf16[128,384]{1,0:T(8,128)(2,1)S(1)}, bf16[128,384]{1,0:T(8,128)(2,1)S(1)}, u32[]{:S(2)}, u32[]{:S(2)}) collective-permute-start(bf16[128,384]{1,0:T(8,128)(2,1)S(1)} %copy-done), channel_id=1, source_target_pairs={{0,24},{2,26},{4,28},{6,30},{8,16},{10,18},{12,20},{14,22},{16,8},... | collective-permute-start | bytes 294920 | tf_op jit(solution)/shard_map/ppermute | solution.py:19
  8.8 9.2 %collective-permute-start.7 = (bf16[128,384]{1,0:T(8,128)(2,1)S(1)}, bf16[128,384]{1,0:T(8,128)(2,1)S(1)}, u32[]{:S(2)}, u32[]{:S(2)}) collective-permute-start(bf16[128,384]{1,0:T(8,128)(2,1)S(1)} %copy-done), channel_id=1, source_target_pairs={{0,16},{2,18},{4,20},{6,22},{8,24},{10,26},{12,28},{14,30},{16,0},... | collective-permute-start | bytes 294920 | tf_op jit(solution)/shard_map/ppermute | solution.py:19
  8.8 9.2 %collective-permute-start.8 = (bf16[128,384]{1,0:T(8,128)(2,1)S(1)}, bf16[128,384]{1,0:T(8,128)(2,1)S(1)}, u32[]{:S(2)}, u32[]{:S(2)}) collective-permute-start(bf16[128,384]{1,0:T(8,128)(2,1)S(1)} %copy-done), channel_id=1, source_target_pairs={{0,8},{2,10},{4,12},{6,14},{8,0},{10,2},{12,4},{14,6},{16,24},{18,... | collective-permute-start | bytes 294920 | tf_op jit(solution)/shard_map/ppermute | solution.py:19
  9.5 1.3 %collective-permute-start.1 = (s32[1,128]{1,0:T(1,128)S(1)}, s32[1,128]{1,0:T(1,128)S(1)}, u32[]{:S(2)}, u32[]{:S(2)}) collective-permute-start(s32[1,128]{1,0:T(1,128)S(1)} %bitcast.2), channel_id=1, source_target_pairs={{0,2},{2,0},{4,6},{6,4},{8,10},{10,8},{12,14},{14,12},{16,18},{18,... | collective-permute-start | bytes 1544 | tf_op jit(solution)/shard_map/ppermute | solution.py:19
  12.0 4.0 %collective-permute-start.2 = (f32[64,128]{1,0:T(8,128)S(1)}, f32[64,128]{1,0:T(8,128)S(1)}, u32[]{:S(2)}, u32[]{:S(2)}) collective-permute-start(f32[64,128]{1,0:T(8,128)S(1)} %get-tuple-element.25), channel_id=1, source_target_pairs={{0,1},{1,0},{2,3},{3,2},{4,5},{5,4},{6,7},{7,6},{8,9},{9,8},{10,11... | collective-permute-start | bytes 98312 | tf_op jit(solution)/shard_map/ppermute | solution.py:24
  15.9 4.1 %collective-permute-start.3 = (f32[80,128]{1,0:T(8,128)S(1)}, f32[80,128]{1,0:T(8,128)S(1)}, u32[]{:S(2)}, u32[]{:S(2)}) collective-permute-start(f32[80,128]{1,0:T(8,128)S(1)} %pad_maximum_fusion), channel_id=1, source_target_pairs={{0,4},{2,6},{4,0},{6,2},{8,12},{10,14},{12,8},{14,10},{16,20},{18,... | collective-permute-start | bytes 122888 | tf_op jit(solution)/shard_map/ppermute | solution.py:19
  18.1 11.0 %collective-permute-start.10 = (bf16[512,384]{1,0:T(8,128)(2,1)S(1)}, bf16[512,384]{1,0:T(8,128)(2,1)S(1)}, u32[]{:S(2)}, u32[]{:S(2)}) collective-permute-start(bf16[512,384]{1,0:T(8,128)(2,1)S(1)} %constant_dynamic-update-slice_fusion.here_ref), channel_id=1, source_target_pairs={{0,4},{2,6},{4,0},{6,2},{8,12},{10,14},{12,8},{14,10},{16,20},{18,... | collective-permute-start | bytes 1179656 | tf_op jit(solution)/shard_map/ppermute | solution.py:19
  18.4 10.7 %collective-permute-start.9 = (bf16[512,384]{1,0:T(8,128)(2,1)S(1)}, bf16[512,384]{1,0:T(8,128)(2,1)S(1)}, u32[]{:S(2)}, u32[]{:S(2)}) collective-permute-start(bf16[512,384]{1,0:T(8,128)(2,1)S(1)} %constant_dynamic-update-slice_fusion.here_ref), channel_id=1, source_target_pairs={{0,2},{2,0},{4,6},{6,4},{8,10},{10,8},{12,14},{14,12},{16,18},{18,... | collective-permute-start | bytes 1179656 | tf_op jit(solution)/shard_map/ppermute | solution.py:19
  20.0 4.0 %collective-permute-start.4 = (f32[80,128]{1,0:T(8,128)S(1)}, f32[80,128]{1,0:T(8,128)S(1)}, u32[]{:S(2)}, u32[]{:S(2)}) collective-permute-start(f32[80,128]{1,0:T(8,128)S(1)} %fusion), channel_id=1, source_target_pairs={{0,8},{2,10},{4,12},{6,14},{8,0},{10,2},{12,4},{14,6},{16,24},{18,... | collective-permute-start | bytes 122888 | tf_op jit(solution)/shard_map/ppermute | solution.py:19
  24.0 4.9 %collective-permute-start.5 = (f32[80,128]{1,0:T(8,128)S(1)}, f32[80,128]{1,0:T(8,128)S(1)}, u32[]{:S(2)}, u32[]{:S(2)}) collective-permute-start(f32[80,128]{1,0:T(8,128)S(1)} %add.14), channel_id=1, source_target_pairs={{0,16},{2,18},{4,20},{6,22},{8,24},{10,26},{12,28},{14,30},{16,0},... | collective-permute-start | bytes 122888 | tf_op jit(solution)/shard_map/ppermute | solution.py:19
  29.1 2.0 %collective-permute-start.11 = (bf16[512,384]{1,0:T(8,128)(2,1)S(1)}, bf16[512,384]{1,0:T(8,128)(2,1)S(1)}, u32[]{:S(2)}, u32[]{:S(2)}) collective-permute-start(bf16[512,384]{1,0:T(8,128)(2,1)S(1)} %collective-permute-done.10.there_ref), channel_id=1, source_target_pairs={{0,2},{2,0},{4,6},{6,4},{8,10},{10,8},{12,14},{14,12},{16,18},{18,... | collective-permute-start | bytes 1179656 | tf_op jit(solution)/shard_map/ppermute | solution.py:19
  29.1 2.0 %collective-permute-start.12 = (f32[64,128]{1,0:T(8,128)S(1)}, f32[64,128]{1,0:T(8,128)S(1)}, u32[]{:S(2)}, u32[]{:S(2)}) collective-permute-start(f32[64,128]{1,0:T(8,128)S(1)} %slice.15.stem_ref), channel_id=1, source_target_pairs={{0,2},{2,0},{4,6},{6,4},{8,10},{10,8},{12,14},{14,12},{16,18},{18,... | collective-permute-start | bytes 98312 | tf_op jit(solution)/shard_map/ppermute | solution.py:19
